TPU v7x, 512 devices: a whole 4x4x16 slice. The times are simulated.
512 devices in a mesh: gen: 64 (over y, z), mp: 8 (over x, core).
Axes of the slice: x: 4, y: 4, z: 16, core: 2. Of those that a mesh axis runs over, the one named last changes fastest.
Arguments:
- pre_x: bfloat16 [64, 512, 4096], P('gen', None, 'mp'), may hold values from -6 to 6
- pre_z: bfloat16 [64, 512, 4096], P('gen', None, 'mp'), may hold values from -6 to 6
- pre_bc: bfloat16 [64, 2, 512, 512], P('gen', None, None, 'mp'), may hold values from -2 to 2
- pre_raw: bfloat16 [64, 512, 64], P('gen', None, 'mp'), may hold values from -6 to 6
- prompt_len: int32 [64], P('gen'), may hold values from 1 to 512, as said below
- live_state: bfloat16 [2048, 64, 64, 64], P('gen', 'mp'), may hold values from -6 to 6
- live_conv: bfloat16 [2048, 3, 4096], P('gen', None, 'mp'), may hold values from -6 to 6
- source: int32 [2048], P('gen'), may hold values from 0 to 2047, as said below
- reader: int32 [1024], P('gen'), may hold values from 0 to 63, as said below
- step_xz: bfloat16 [4, 2, 3072, 4096], P(None, None, 'gen', 'mp'), may hold values from -6 to 6
- step_bc: bfloat16 [4, 2, 3072, 512], P(None, None, 'gen', 'mp'), may hold values from -2 to 2
- step_raw: bfloat16 [4, 3072, 64], P(None, 'gen', 'mp'), may hold values from -6 to 6
- decay: float32 [64], P('mp'), may hold values from 0.02 to 2
- dt_bias: float32 [64], P('mp'), may hold values from -4 to 0
- conv_weight: bfloat16 [4, 4096], P(None, 'mp'), may hold values from -3 to 3
- conv_bias: float32 [4096], P('mp'), may hold values from -3 to 3
- skip: float32 [64], P('mp'), may hold values from 0.5 to 1.5
- norm_gain: float32 [4096], P('mp'), may hold values from 0.5 to 1.5
Outputs:
- prefill_out: bfloat16 [64, 512, 4096], P('gen', None, 'mp')
- decode_out: bfloat16 [4, 3072, 4096], P(None, 'gen', 'mp')
Inputs may be any that keep to these rules, and one draw needn't show every extreme that they name: source is a permutation; new row i*32 + k takes an old row of slot k, the 32 new rows of one gen index come from 32 different gen indices, so at most one old row of one gen index goes to any one gen index. `reader`: each prompt is continued by exactly 16 rows, on 16 different gen indices; the 16 rows of one gen index continue 16 different prompts. `prompt_len`: one prompt has exactly 512 tokens.
All inputs are finite; a program needn't handle non-finite values.
Results may differ from a plain program's by a relative error of at most 0.006.
Values may be sent and summed in bfloat16 or wider, within the bound.
No kernel may reach another device: no remote copies, remote signals or barrier semaphores. Data moves between devices by JAX's collectives and lax.ppermute only.
A program may use at most 128 MiB of HBM per device.

v0:
```python
import jax
import jax.numpy as jnp
from jax import lax
from jax.sharding import PartitionSpec as P

STATE = 64


EPS = 1e-05


def prefill_local(xin, zin, bcin, rawin, length, decay, dt_bias, conv_weight, conv_bias, skip):
    span, width = xin.shape
    heads = rawin.shape[1]
    hdim = width // heads
    groups = bcin.shape[2] // STATE
    per_group = heads // groups
    taps = conv_weight.shape[0]
    padded = jnp.concatenate([jnp.zeros((taps - 1, width), jnp.bfloat16), xin], 0)
    acc = conv_bias
    for offset in range(taps):
        acc = acc + lax.slice_in_dim(padded, offset, offset + span, axis=0).astype(
            jnp.float32
        ) * conv_weight[offset].astype(jnp.float32)
    xconv = jax.nn.silu(acc).astype(jnp.bfloat16)
    spots = jnp.arange(span, dtype=jnp.int32)
    dt = jnp.where(
        (spots < length)[:, None], jax.nn.softplus(rawin.astype(jnp.float32) + dt_bias), 0.0
    )
    cum = jnp.cumsum(dt * -decay, axis=0)
    causal = spots[:, None] >= spots[None, :]
    heads_x = xconv.reshape(span, heads, hdim)
    bmat = bcin[0, :, 0:STATE]
    cmat = bcin[1, :, 0:STATE]
    scores = jnp.einsum("tn,sn->ts", cmat, bmat, preferred_element_type=jnp.float32)
    bwide = bmat.astype(jnp.float32)

    def one_head(head, scores=scores, bwide=bwide):
        rate = lax.dynamic_index_in_dim(cum, head, 1, False)
        stride = lax.dynamic_index_in_dim(dt, head, 1, False)
        gap = jnp.where(causal, rate[:, None] - rate[None, :], -jnp.inf)
        weights = (scores * jnp.exp(gap) * stride[None, :]).astype(jnp.bfloat16)
        xhead = lax.dynamic_index_in_dim(heads_x, head, 1, False)
        yhead = jnp.dot(weights, xhead, preferred_element_type=jnp.float32) + skip[
            head
        ] * xhead.astype(jnp.float32)
        tail = jnp.exp(rate[-1] - rate) * stride
        state = jnp.dot(
            xhead.astype(jnp.float32).T, bwide * tail[:, None], precision=lax.Precision.HIGHEST
        )
        return (yhead, state.astype(jnp.bfloat16))

    yparts, sparts = lax.map(one_head, 0 + jnp.arange(per_group, dtype=jnp.int32))
    y = jnp.transpose(yparts, (1, 0, 2)).reshape(span, width)
    gate = y * jax.nn.silu(zin.astype(jnp.float32))
    tail_rows = lax.dynamic_slice_in_dim(padded, length, taps - 1, 0)
    return (gate, sparts, tail_rows)


def decode_local(
    state, conv, step_xz, step_bc, step_raw, decay, dt_bias, conv_weight, conv_bias, skip
):
    rows = state.shape[0]
    heads = step_raw.shape[2]
    hdim = step_xz.shape[3] // heads
    groups = step_bc.shape[3] // STATE
    per_group = heads // groups
    taps = conv_weight.shape[0]
    gates = []
    for step in range(step_xz.shape[0]):
        window = jnp.concatenate([conv, step_xz[step, 0][:, None]], 1)
        acc = conv_bias
        for offset in range(taps):
            acc = acc + window[:, offset].astype(jnp.float32) * conv_weight[offset].astype(
                jnp.float32
            )
        xconv = jax.nn.silu(acc).astype(jnp.bfloat16)
        conv = window[:, 1:]
        dt = jax.nn.softplus(step_raw[step].astype(jnp.float32) + dt_bias)
        bexp = jnp.repeat(
            step_bc[step, 0].reshape(rows, groups, STATE).astype(jnp.float32), per_group, axis=1
        )
        cexp = jnp.repeat(
            step_bc[step, 1].reshape(rows, groups, STATE).astype(jnp.float32), per_group, axis=1
        )
        xhead = xconv.reshape(rows, heads, hdim).astype(jnp.float32)
        state = (
            jnp.exp(-dt * decay)[:, :, None, None] * state
            + (dt[:, :, None] * xhead)[:, :, :, None] * bexp[:, :, None, :]
        )
        y = (
            jnp.einsum("rhpn,rhn->rhp", state, cexp, precision=lax.Precision.HIGHEST)
            + skip[None, :, None] * xhead
        )
        gates.append(
            y.reshape(rows, heads * hdim) * jax.nn.silu(step_xz[step, 1].astype(jnp.float32))
        )
    return gates


def finish(gate, total, width_all, norm_gain):
    return (gate * lax.rsqrt(total / width_all + EPS)[:, None] * norm_gain).astype(jnp.bfloat16)


def per_device(
    pre_x,
    pre_z,
    pre_bc,
    pre_raw,
    prompt_len,
    live_state,
    live_conv,
    source,
    reader,
    step_xz,
    step_bc,
    step_raw,
    decay,
    dt_bias,
    conv_weight,
    conv_bias,
    skip,
    norm_gain,
):
    width_all = pre_x.shape[2] * lax.axis_size("mp")
    gen_count = lax.axis_size("gen")
    live_dev = source.shape[0]
    readers = reader.shape[0]
    me = lax.axis_index("gen")
    gens = jnp.arange(gen_count, dtype=jnp.int32)
    pre_gate, prefix_state, prefix_tail = prefill_local(
        pre_x[0],
        pre_z[0],
        pre_bc[0],
        pre_raw[0],
        prompt_len[0],
        decay,
        dt_bias,
        conv_weight,
        conv_bias,
        skip,
    )
    piece = (
        lax.all_gather(prefix_state[None], "gen", axis=0, tiled=True),
        lax.all_gather(prefix_tail[None], "gen", axis=0, tiled=True),
    )
    count = piece[0].shape[0]
    pick = (reader[:, None] == jnp.arange(count, dtype=jnp.int32)[None, :]).astype(jnp.bfloat16)
    fan_state = jnp.dot(pick, piece[0].reshape(count, -1), preferred_element_type=jnp.float32)
    fan_tail = jnp.dot(pick, piece[1].reshape(count, -1), preferred_element_type=jnp.float32)
    fan_state = fan_state.astype(jnp.bfloat16).reshape((readers,) + prefix_state.shape)
    fan_tail = fan_tail.astype(jnp.bfloat16).reshape((readers,) + prefix_tail.shape)
    everyone = lax.all_gather(source, "gen", axis=0, tiled=True)
    mine = me * live_dev + jnp.arange(live_dev, dtype=jnp.int32)
    slots = jnp.arange(everyone.shape[0], dtype=jnp.int32)
    dest_row = jnp.sum(jnp.where(everyone[None, :] == mine[:, None], slots[None, :], 0), axis=1)
    to_pick = (gens[:, None] == (dest_row // live_dev)[None, :]).astype(jnp.bfloat16)
    from_pick = ((source // live_dev)[:, None] == gens[None, :]).astype(jnp.bfloat16)
    send_state = jnp.dot(
        to_pick, live_state.reshape(live_dev, -1), preferred_element_type=jnp.float32
    ).astype(jnp.bfloat16)
    send_conv = jnp.dot(
        to_pick, live_conv.reshape(live_dev, -1), preferred_element_type=jnp.float32
    ).astype(jnp.bfloat16)
    got_state, got_conv = (
        lax.all_to_all(send_state, "gen", split_axis=0, concat_axis=0, tiled=True),
        lax.all_to_all(send_conv, "gen", split_axis=0, concat_axis=0, tiled=True),
    )
    moved_state = (
        jnp.dot(from_pick, got_state, preferred_element_type=jnp.float32)
        .astype(jnp.bfloat16)
        .reshape(live_state.shape)
    )
    moved_conv = (
        jnp.dot(from_pick, got_conv, preferred_element_type=jnp.float32)
        .astype(jnp.bfloat16)
        .reshape(live_conv.shape)
    )
    rows_state = jnp.concatenate([moved_state, fan_state], 0).astype(jnp.float32)
    rows_conv = jnp.concatenate([moved_conv, fan_tail], 0)
    gates = decode_local(
        rows_state,
        rows_conv,
        step_xz,
        step_bc,
        step_raw,
        decay,
        dt_bias,
        conv_weight,
        conv_bias,
        skip,
    )
    pre_total = lax.psum(jnp.sum(pre_gate * pre_gate, axis=-1), "mp")
    step_totals = [lax.psum(jnp.sum(gate * gate, axis=-1), "mp") for gate in gates]
    prefill_out = finish(pre_gate, pre_total, width_all, norm_gain)[None]
    decoded = jnp.stack(
        [finish(gate, total, width_all, norm_gain) for gate, total in zip(gates, step_totals)]
    )
    return (prefill_out, decoded)


def solution(mesh):
    placed = (
        P("gen", None, "mp"),
        P("gen", None, "mp"),
        P("gen", None, None, "mp"),
        P("gen", None, "mp"),
        P("gen"),
        P("gen", "mp", None, None),
        P("gen", None, "mp"),
        P("gen"),
        P("gen"),
        P(None, None, "gen", "mp"),
        P(None, None, "gen", "mp"),
        P(None, "gen", "mp"),
        P("mp"),
        P("mp"),
        P(None, "mp"),
        P("mp"),
        P("mp"),
        P("mp"),
    )
    return jax.shard_map(
        per_device,
        mesh=mesh,
        in_specs=placed,
        out_specs=(P("gen", None, "mp"), P(None, "gen", "mp")),
        check_vma=False,
    )
```

profile of v0, /device:TPU:1, one launch (start us, length us, event | category | flops | bytes accessed | tf_op | source)
XLA Modules:
  0.0 575.2 jit_solution(12296808790478046895)
XLA Ops:
  7.2 1.3 dynamic-slice
  9.1 0.9 dynamic-update-slice
  10.0 30.4 %all-reduce.1 = s32[2048]{0:T(1024)S(1)} all-reduce(s32[2048]{0:T(1024)S(1)} %dynamic-update-slice), channel_id=1, replica_groups=mesh['gen'=64,'mp'=8] {'gen'}, use_global_device_ids=true, to_apply=%add.1 | all-reduce | flops 2048 | bytes 16384
  40.6 0.9 copy.102
  42.2 0.7 reduce.29
  43.6 7.3 %all-to-all-start.1 = ((bf16[64,2,768]{2,1,0:T(2,128)(2,1)}), bf16[64,2,768]{2,1,0:T(2,128)(2,1)S(1)}, u32[]{:S(2)}, u32[]{:S(2)}) async-start(bf16[64,2,768]{2,1,0:T(2,128)(2,1)} %reshape.1202), calls=%async_computation.1 | async-start | bytes 393216 | tf_op jit(solution)/shard_map/all_to_all | solution.py:167
  50.9 5.0 reshape.1111
  55.9 3.2 fusion.19
  59.1 6.7 %reduce.30 = bf16[64,32768]{1,0:T(8,128)(2,1)} reduce(bf16[64,1,32768]{2,0,1:T(8,128)(2,1)} %fusion.19, bf16[]{:T(256)} %broadcast.662), dimensions={1}, to_apply=%copy.80.reduce_sub_computation | reduce | bytes 8388610 | tf_op jit(solution)/shard_map/all_to_all | solution.py:166
  65.9 7.9 %reshape.1204 = bf16[64,2,16384]{2,1,0:T(2,128)(2,1)} reshape(bf16[64,32768]{1,0:T(8,128)(2,1)} %reduce.30) | data formatting | bytes 8388608
  73.8 14.8 %all-to-all-start = ((bf16[64,2,16384]{2,1,0:T(2,128)(2,1)}), bf16[64,2,16384]{2,1,0:T(2,128)(2,1)}, u32[]{:S(2)}, u32[]{:S(2)}) async-start(bf16[64,2,16384]{2,1,0:T(2,128)(2,1)} %reshape.1204), calls=%async_computation | async-start | bytes 8388608 | tf_op jit(solution)/shard_map/all_to_all | solution.py:166
  90.5 1.1 reduce-window.6
  92.1 2.2 fusion.102
  94.2 62.2 %while.13 = (s32[]{:T(128)}, f32[8,512,64]{1,2,0:T(8,128)S(1)}, bf16[8,64,64]{2,1,0:T(8,128)(2,1)}, s32[8]{0:T(128)S(1)}, f32[512,8]{0,1:T(8,128)S(1)}, /*index=...) while((s32[]{:T(128)}, f32[8,512,64]{1,2,0:T(8,128)S(1)}, ...), condition=%wide.region_3.4_spmd.clone, body=%wide.region_2.3_spmd.clone.sunk | while | flops 60429316 | bytes 1674987 | solution.py:53
  97.7 1.2 dynamic_slice.49
  98.9 2.2 fusion.173
  101.1 0.9 fusion.174
  105.4 1.2 dynamic_slice.49
  106.6 2.2 fusion.173
  108.8 0.9 fusion.174
  113.2 1.2 dynamic_slice.49
  114.4 2.2 fusion.173
  116.6 0.9 fusion.174
  121.0 1.2 dynamic_slice.49
  122.2 2.2 fusion.173
  124.4 0.9 fusion.174
  128.7 1.2 dynamic_slice.49
  130.0 2.2 fusion.173
  132.2 0.9 fusion.174
  136.5 1.2 dynamic_slice.49
  137.7 2.2 fusion.173
  139.9 0.9 fusion.174
  144.3 1.2 dynamic_slice.49
  145.5 2.2 fusion.173
  147.7 0.9 fusion.174
  152.1 1.2 dynamic_slice.49
  153.3 2.2 fusion.173
  155.5 0.9 fusion.174
  156.5 189.7 %all-gather.2 = bf16[64,3,512]{2,1,0:T(4,128)(2,1)S(1)} all-gather(bf16[1,3,512]{2,1,0:T(4,128)(2,1)S(1)} %fusion.143), channel_id=3, replica_groups=mesh['gen'=64,'mp'=8] {'gen'}, dimensions={0}, use_global_device_ids=true | all-gather | bytes 199680 | tf_op jit(solution)/shard_map/all_gather | solution.py:145
  346.9 0.8 reshape.1151
  351.3 0.8 reshape.1143
  352.1 0.8 reshape.1149
  352.8 0.8 reshape.1155
  353.6 1.3 copy.78
  354.9 1.3 and_select_fusion.1
  356.1 1.5 bitcast_convert_fusion.7
  358.2 0.9 convolution_convert_fusion.5
  359.2 1.2 fusion.73
  360.7 1.0 reshape.1132
  361.7 2.3 convert_multiply_fusion.7
  364.0 10.6 %reshape.1113 = bf16[64,32768]{1,0:T(8,128)(2,1)} reshape(bf16[512,64,64]{2,1,0:T(8,128)(2,1)} %all-gather.5.cloned.1.call-done) | data formatting | bytes 8388608 | tf_op jit(solution)/shard_map/reshape | solution.py:149
  374.6 3.9 convolution_convert_fusion.3
  378.5 4.1 reshape.1114
  382.5 19.8 %reshape.1205 = bf16[64,1,32768]{2,1,0:T(2,128)(2,1)} reshape(bf16[64,2,16384]{2,1,0:T(2,128)(2,1)} %all-to-all-done) | data formatting | bytes 8388608
  402.4 8.5 %convolution_convert_fusion.2 = bf16[32,32768]{1,0:T(8,128)(2,1)S(1)} fusion(bf16[64,1,32768]{2,1,0:T(2,128)(2,1)} %reshape.1205, s32[32]{0:T(128)S(1)} %copy-done.34), kind=kOutput, calls=%fused_computation.27 | convolution fusion | flops 135268352 | bytes 6291584 | tf_op jit(solution)/shard_map/dot_general | solution.py:170
  410.8 5.5 reshape.1112
  416.5 23.8 %fusion.24 = f32[48,8,1,64]{3,2,1,0:T(1,128)S(1)} fusion(f32[48,8,64,1]{2,3,1,0:T(1,128)S(1)} %bitcast.276, f32[48,64]{1,0:T(8,128)S(1)} %copy-done.23, f32[48,8,64]{2,1,0:T(8,128)S(1)} %copy-done.13, f32[48,8]{1,0:T(8,128)S(1)} %copy-done.25, bf16[16,8,64,64]{3,2,1,0:T(8,128)(2,1)} %reshape.1114, bf16[32,8,64,64]{3,2,1,0:T(8,128)(2,1)} %reshape.1112), kind=kOutput, calls=%fused_computation.36 | convolution fusion | flops 26738688 | bytes 3454464 | tf_op jit(solution)/shard_map/rhpn,rhn->rhp/dot_general | solution.py:92
  440.4 28.7 %fusion.25 = f32[48,8,1,64]{3,2,1,0:T(1,128)S(1)} fusion(f32[48,8,64,1]{2,3,1,0:T(1,128)S(1)} %bitcast.277, f32[48,64]{1,0:T(8,128)S(1)} %copy-done.22, f32[48,8,64]{2,1,0:T(8,128)S(1)} %copy-done.14, f32[48,8]{1,0:T(8,128)S(1)} %copy-done.26, f32[48,64]{1,0:T(8,128)S(1)} %copy-done.23, f32[48,8,64]{2,1,0:T(8,128)S(1)} %copy-done.13, ...), kind=kOutput, calls=%fused_computation.37 | convolution fusion | flops 31457280 | bytes 3566592 | tf_op jit(solution)/shard_map/rhpn,rhn->rhp/dot_general | solution.py:92
  469.2 32.0 %fusion.26 = f32[48,8,1,64]{3,2,1,0:T(1,128)S(1)} fusion(f32[48,8,64,1]{2,3,1,0:T(1,128)S(1)} %bitcast.278, f32[48,64]{1,0:T(8,128)S(1)} %copy-done.21, f32[48,8,64]{2,1,0:T(8,128)S(1)} %copy-done.15, f32[48,8]{1,0:T(8,128)S(1)} %copy-done.27, f32[48,64]{1,0:T(8,128)S(1)} %copy-done.22, f32[48,8,64]{2,1,0:T(8,128)S(1)} %copy-done.14, ...), kind=kOutput, calls=%fused_computation.38 | convolution fusion | flops 36175872 | bytes 3678720 | tf_op jit(solution)/shard_map/rhpn,rhn->rhp/dot_general | solution.py:92
  501.4 40.3 %fusion.20 = f32[48,8,1,64]{3,2,1,0:T(1,128)S(1)} fusion(f32[48,8,64,1]{2,3,1,0:T(1,128)S(1)} %bitcast.275, f32[48,64]{1,0:T(8,128)S(1)} %copy-done.24, f32[48,8,64]{2,1,0:T(8,128)S(1)} %copy-done.16, f32[48,8]{1,0:T(8,128)S(1)} %copy-done.28, f32[48,64]{1,0:T(8,128)S(1)} %copy-done.21, f32[48,8,64]{2,1,0:T(8,128)S(1)} %copy-done.15, ...), kind=kOutput, calls=%fused_computation.29 | convolution fusion | flops 40894464 | bytes 3790848 | tf_op jit(solution)/shard_map/rhpn,rhn->rhp/dot_general | solution.py:92
  541.8 1.2 multiply_reduce_fusion.3
  543.1 1.0 reshape.1120
  544.4 21.6 %all-reduce.2 = (f32[512]{0:T(512)S(1)}, f32[48]{0:T(128)S(1)}, f32[48]{0:T(128)S(1)}, f32[48]{0:T(128)S(1)}, f32[48]{0:T(128)S(1)}) all-reduce(f32[512]{0:T(512)S(1)} %fusion.64, f32[48]{0:T(128)S(1)} %get-tuple-element.187, f32[48]{0:T(128)S(1)} %get-tuple-element.185, ...), channel_id=1, replica_groups=mesh['gen'=64,'mp'=8] {'mp'}, use_global_device_ids=true, to_apply=%region_5.6 | all-reduce | flops 704 | bytes 5632 | tf_op jit(solution)/shard_map/psum | solution.py:193
  566.4 1.0 copy.90
  (175 shorter events, 23.7 us)
Async XLA Ops:
  43.6 30.2 %all-to-all-start.1 = ((bf16[64,2,768]{2,1,0:T(2,128)(2,1)}), bf16[64,2,768]{2,1,0:T(2,128)(2,1)S(1)}, u32[]{:S(2)}, u32[]{:S(2)}) async-start(bf16[64,2,768]{2,1,0:T(2,128)(2,1)} %reshape.1202), calls=%async_computation.1 | async-start | bytes 393216 | tf_op jit(solution)/shard_map/all_to_all | solution.py:167
  65.8 23.5 %copy-start.20 = (bf16[4,512]{1,0:T(4,128)(2,1)S(1)}, bf16[4,512]{1,0:T(4,128)(2,1)}, u32[]{:S(2)}) copy-start(bf16[4,512]{1,0:T(4,128)(2,1)} %param.34) | copy-start | bytes 12292
  65.8 23.5 %copy-start.4 = (bf16[1,512,512]{2,1,0:T(8,128)(2,1)S(1)}, bf16[1,512,512]{2,1,0:T(8,128)(2,1)}, u32[]{:S(2)}) copy-start(bf16[1,512,512]{2,1,0:T(8,128)(2,1)} %param.20) | copy-start | bytes 1572868
  65.8 23.6 %copy-start.29 = (f32[512]{0:T(512)S(1)}, f32[512]{0:T(512)}, u32[]{:S(2)}) copy-start(f32[512]{0:T(512)} %param.35) | copy-start | bytes 6148
  65.8 24.5 %copy-start.37 = (f32[8]{0:T(128)S(1)}, f32[8]{0:T(128)}, u32[]{:S(2)}) copy-start(f32[8]{0:T(128)} %param.32) | copy-start | bytes 100
  65.8 24.5 %copy-start.30 = (bf16[1,512,8]{1,2,0:T(8,128)(2,1)S(1)}, bf16[1,512,8]{1,2,0:T(8,128)(2,1)}, u32[]{:S(2)}) copy-start(bf16[1,512,8]{1,2,0:T(8,128)(2,1)} %param.23) | copy-start | bytes 24580
  65.8 24.6 %copy-start.33 = (f32[8]{0:T(128)S(1)}, f32[8]{0:T(128)}, u32[]{:S(2)}) copy-start(f32[8]{0:T(128)} %param.33) | copy-start | bytes 100
  65.8 26.0 %slice-start = ((bf16[1,2,512,64]{2,3,1,0:T(8,128)(2,1)}), bf16[1,1,512,64]{2,3,1,0:T(8,128)(2,1)S(1)}, s32[]{:S(2)}) async-start(bf16[1,2,512,64]{2,3,1,0:T(8,128)(2,1)} %param.22), calls=%async_computation.3 | async-start | bytes 131072 | tf_op jit(solution)/shard_map/slice | solution.py:33
  73.8 308.8 %all-to-all-start = ((bf16[64,2,16384]{2,1,0:T(2,128)(2,1)}), bf16[64,2,16384]{2,1,0:T(2,128)(2,1)}, u32[]{:S(2)}, u32[]{:S(2)}) async-start(bf16[64,2,16384]{2,1,0:T(2,128)(2,1)} %reshape.1204), calls=%async_computation | async-start | bytes 8388608 | tf_op jit(solution)/shard_map/all_to_all | solution.py:166
  88.6 275.4 %all-gather.5.cloned.1.call-start = ((), (), s32[]{:S(2)}) async-start(), calls=%async_computation.2 | async-start | bytes 8519680 | tf_op jit(solution)/shard_map/all_gather | solution.py:144
  90.3 256.0 %copy-start.35 = (s32[16]{0:T(128)S(1)}, s32[16]{0:T(128)}, u32[]{:S(2)}) copy-start(s32[16]{0:T(128)} %param.28) | copy-start | bytes 196
  90.3 256.2 %copy-start.5 = (bf16[4,2,48,512]{3,2,1,0:T(8,128)(2,1)S(1)}, bf16[4,2,48,512]{3,2,1,0:T(8,128)(2,1)}, u32[]{:S(2)}) copy-start(bf16[4,2,48,512]{3,2,1,0:T(8,128)(2,1)} %param.29) | copy-start | bytes 1179652
  94.2 253.5 %copy-start.31 = (bf16[4,48,8]{1,2,0:T(8,128)(2,1)S(1)}, bf16[4,48,8]{1,2,0:T(8,128)(2,1)}, u32[]{:S(2)}) copy-start(bf16[4,48,8]{1,2,0:T(8,128)(2,1)} %param.31) | copy-start | bytes 9220
  156.4 218.2 %copy-start.1 = (f32[8,512,64]{1,2,0:T(8,128)}, f32[8,512,64]{1,2,0:T(8,128)S(1)}, u32[]{:S(2)}) copy-start(f32[8,512,64]{1,2,0:T(8,128)S(1)} %get-tuple-element.60) | copy-start | bytes 3145732
  359.2 15.4 %copy-start.36 = (s32[16]{0:T(128)S(1)}, s32[16]{0:T(128)}, u32[]{:S(2)}) copy-start(s32[16]{0:T(128)} %param.28) | copy-start | bytes 196
  378.5 23.9 %copy-start.34 = (s32[32]{0:T(128)S(1)}, s32[32]{0:T(128)}, u32[]{:S(2)}) copy-start(s32[32]{0:T(128)} %and_select_fusion.1) | copy-start | bytes 388
  402.3 14.0 %copy-start.19 = (f32[48,64]{1,0:T(8,128)S(1)}, f32[48,64]{1,0:T(8,128)}, u32[]{:S(2)}) copy-start(f32[48,64]{1,0:T(8,128)} %get-tuple-element.161) | copy-start | bytes 36868
  402.3 14.0 %copy-start.13 = (f32[48,8,64]{2,1,0:T(8,128)S(1)}, f32[48,8,64]{2,1,0:T(8,128)}, u32[]{:S(2)}) copy-start(f32[48,8,64]{2,1,0:T(8,128)} %get-tuple-element.135) | copy-start | bytes 294916
  402.3 14.1 %copy-start.23 = (f32[48,64]{1,0:T(8,128)S(1)}, f32[48,64]{1,0:T(8,128)}, u32[]{:S(2)}) copy-start(f32[48,64]{1,0:T(8,128)} %get-tuple-element.166) | copy-start | bytes 36868
  402.4 14.1 %copy-start.25 = (f32[48,8]{1,0:T(8,128)S(1)}, f32[48,8]{1,0:T(8,128)}, u32[]{:S(2)}) copy-start(f32[48,8]{1,0:T(8,128)} %copy.79) | copy-start | bytes 4612
  416.4 23.9 %copy-start.18 = (f32[48,64]{1,0:T(8,128)S(1)}, f32[48,64]{1,0:T(8,128)}, u32[]{:S(2)}) copy-start(f32[48,64]{1,0:T(8,128)} %get-tuple-element.164) | copy-start | bytes 36868
  416.4 23.9 %copy-start = (bf16[32,8,64,64]{3,2,1,0:T(8,128)(2,1)S(1)}, bf16[32,8,64,64]{3,2,1,0:T(8,128)(2,1)}, u32[]{:S(2)}) copy-start(bf16[32,8,64,64]{3,2,1,0:T(8,128)(2,1)} %reshape.1112) | copy-start | bytes 6291460
  416.4 23.9 %copy-start.3 = (bf16[16,8,64,64]{3,2,1,0:T(8,128)(2,1)S(1)}, bf16[16,8,64,64]{3,2,1,0:T(8,128)(2,1)}, u32[]{:S(2)}) copy-start(bf16[16,8,64,64]{3,2,1,0:T(8,128)(2,1)} %reshape.1114) | copy-start | bytes 3145732
  416.4 23.9 %copy-start.14 = (f32[48,8,64]{2,1,0:T(8,128)S(1)}, f32[48,8,64]{2,1,0:T(8,128)}, u32[]{:S(2)}) copy-start(f32[48,8,64]{2,1,0:T(8,128)} %get-tuple-element.143) | copy-start | bytes 294916
  416.5 23.9 %copy-start.22 = (f32[48,64]{1,0:T(8,128)S(1)}, f32[48,64]{1,0:T(8,128)}, u32[]{:S(2)}) copy-start(f32[48,64]{1,0:T(8,128)} %get-tuple-element.165) | copy-start | bytes 36868
  416.5 23.9 %copy-start.26 = (f32[48,8]{1,0:T(8,128)S(1)}, f32[48,8]{1,0:T(8,128)}, u32[]{:S(2)}) copy-start(f32[48,8]{1,0:T(8,128)} %copy.84) | copy-start | bytes 4612
  440.4 28.7 %copy-start.17 = (f32[48,64]{1,0:T(8,128)S(1)}, f32[48,64]{1,0:T(8,128)}, u32[]{:S(2)}) copy-start(f32[48,64]{1,0:T(8,128)} %get-tuple-element.162) | copy-start | bytes 36868
  440.4 28.7 %copy-start.15 = (f32[48,8,64]{2,1,0:T(8,128)S(1)}, f32[48,8,64]{2,1,0:T(8,128)}, u32[]{:S(2)}) copy-start(f32[48,8,64]{2,1,0:T(8,128)} %get-tuple-element.145) | copy-start | bytes 294916
  440.4 28.7 %copy-start.21 = (f32[48,64]{1,0:T(8,128)S(1)}, f32[48,64]{1,0:T(8,128)}, u32[]{:S(2)}) copy-start(f32[48,64]{1,0:T(8,128)} %get-tuple-element.163) | copy-start | bytes 36868
  440.4 28.7 %copy-start.27 = (f32[48,8]{1,0:T(8,128)S(1)}, f32[48,8]{1,0:T(8,128)}, u32[]{:S(2)}) copy-start(f32[48,8]{1,0:T(8,128)} %copy.86) | copy-start | bytes 4612
  469.2 32.1 %copy-start.16 = (f32[48,8,64]{2,1,0:T(8,128)S(1)}, f32[48,8,64]{2,1,0:T(8,128)}, u32[]{:S(2)}) copy-start(f32[48,8,64]{2,1,0:T(8,128)} %get-tuple-element.147) | copy-start | bytes 294916
  469.2 32.1 %copy-start.24 = (f32[48,64]{1,0:T(8,128)S(1)}, f32[48,64]{1,0:T(8,128)}, u32[]{:S(2)}) copy-start(f32[48,64]{1,0:T(8,128)} %get-tuple-element.168) | copy-start | bytes 36868
  469.2 32.1 %copy-start.28 = (f32[48,8]{1,0:T(8,128)S(1)}, f32[48,8]{1,0:T(8,128)}, u32[]{:S(2)}) copy-start(f32[48,8]{1,0:T(8,128)} %copy.88) | copy-start | bytes 4612
  501.3 40.5 %copy-start.6 = (f32[48,8,64]{2,1,0:T(8,128)S(1)}, f32[48,8,64]{2,1,0:T(8,128)}, u32[]{:S(2)}) copy-start(f32[48,8,64]{2,1,0:T(8,128)} %reshape.1143) | copy-start | bytes 294916
  501.3 40.5 %copy-start.7 = (f32[48,8,64]{2,1,0:T(8,128)S(1)}, f32[48,8,64]{2,1,0:T(8,128)}, u32[]{:S(2)}) copy-start(f32[48,8,64]{2,1,0:T(8,128)} %reshape.1149) | copy-start | bytes 294916
  501.3 40.5 %copy-start.8 = (f32[48,8,64]{2,1,0:T(8,128)S(1)}, f32[48,8,64]{2,1,0:T(8,128)}, u32[]{:S(2)}) copy-start(f32[48,8,64]{2,1,0:T(8,128)} %reshape.1155) | copy-start | bytes 294916
  501.3 40.5 %copy-start.9 = (bf16[48,8,64]{2,1,0:T(8,128)(2,1)S(1)}, bf16[48,8,64]{2,1,0:T(8,128)(2,1)}, u32[]{:S(2)}) copy-start(bf16[48,8,64]{2,1,0:T(8,128)(2,1)} %get-tuple-element.136) | copy-start | bytes 147460
  501.3 40.5 %copy-start.10 = (bf16[48,8,64]{2,1,0:T(8,128)(2,1)S(1)}, bf16[48,8,64]{2,1,0:T(8,128)(2,1)}, u32[]{:S(2)}) copy-start(bf16[48,8,64]{2,1,0:T(8,128)(2,1)} %get-tuple-element.144) | copy-start | bytes 147460
  501.4 40.5 %copy-start.11 = (bf16[48,8,64]{2,1,0:T(8,128)(2,1)S(1)}, bf16[48,8,64]{2,1,0:T(8,128)(2,1)}, u32[]{:S(2)}) copy-start(bf16[48,8,64]{2,1,0:T(8,128)(2,1)} %get-tuple-element.146) | copy-start | bytes 147460
  501.4 40.5 %copy-start.12 = (bf16[48,8,64]{2,1,0:T(8,128)(2,1)S(1)}, bf16[48,8,64]{2,1,0:T(8,128)(2,1)}, u32[]{:S(2)}) copy-start(bf16[48,8,64]{2,1,0:T(8,128)(2,1)} %get-tuple-element.148) | copy-start | bytes 147460
  501.4 40.5 %copy-start.38 = (f32[8]{0:T(128)S(1)}, f32[8]{0:T(128)}, u32[]{:S(2)}) copy-start(f32[8]{0:T(128)} %get-tuple-element.309) | copy-start | bytes 100
  501.4 64.7 %copy-start.2 = (f32[8,512,64]{1,2,0:T(8,128)S(1)}, f32[8,512,64]{1,2,0:T(8,128)}, u32[]{:S(2)}) copy-start(f32[8,512,64]{1,2,0:T(8,128)} %copy-done.1) | copy-start | bytes 3145732
  501.4 64.7 %copy-start.32 = (f32[512]{0:T(512)S(1)}, f32[512]{0:T(512)}, u32[]{:S(2)}) copy-start(f32[512]{0:T(512)} %param.37) | copy-start | bytes 6148
Sparse Core Ops, SparseCore 0:
  156.6 187.7 all-gather.4
where the time goes:
time: 578 us; the launch traced here: 575 us
  blocking collectives  242 us (42%)
  matrix products  169 us (29%)
  local copies, waits for them, and re-layouts  88.6 us (15%)
  other arithmetic  23.8 us (4%)
  starting transfers between devices  22.2 us (4%)
  between operations  16.1 us (3%)
  loops' own time  13.8 us (2%)
    all_gather x1, blocking collectives, per_device(): lax.all_gather(prefix_tail[None], 'gen', axis=0, tiled=True)  190 us
    dot_general x4, matrix products, decode_local(): jnp.einsum('rhpn,rhn->rhp', state, cexp, precision=lax.Precision.HIGHEST)  125 us
    unnamed x91, local copies, waits for them, and re-layouts  33.4 us
    unnamed x1, blocking collectives  30.4 us
    psum x1, blocking collectives, per_device(): pre_total = lax.psum(jnp.sum(pre_gate * pre_gate, axis=-1), 'mp')  21.6 us
    dot_general x8, matrix products, one_head(): jnp.dot(weights, xhead, preferred_element_type=jnp.float32)  17.6 us
    all_to_all x1, starting transfers between devices, per_device(): lax.all_to_all(send_state, 'gen', split_axis=0, concat_axis=0, tiled=True)  14.8 us
    another operation x1, loops' own time, prefill_local(): lax.map(one_head, 0 + jnp.arange(per_group, dtype=jnp.int32))  13.8 us
  transfers between devices with their start and end apart: 3, of which 0 were waited for; matrix products, arithmetic and copies ran while one was open for 20% of the time, Pallas kernels for 0%

commit v1 on v0

v1 whole, which is shorter than its diff:
```python
import jax
import jax.numpy as jnp
from jax import lax
from jax.experimental import pallas as pl
from jax.experimental.pallas import tpu as pltpu
from jax.sharding import PartitionSpec as P

STATE = 64
EPS = 1e-05
SUB = 8
F32 = jnp.float32
BF16 = jnp.bfloat16
NT = (((1,), (1,)), ((), ()))
TN = (((0,), (0,)), ((), ()))


def iota(shape, dim):
    return lax.broadcasted_iota(jnp.int32, shape, dim)


def mm(a, b):
    return jnp.dot(a, b, preferred_element_type=F32)


def mm_nt(a, b):
    return lax.dot_general(a, b, NT, preferred_element_type=F32)


def onehot(mask):
    return jnp.where(mask, 1.0, 0.0).astype(BF16)


def split2(x):
    hi = x.astype(BF16)
    return hi, (x - hi.astype(F32)).astype(BF16)


def split3(x):
    hi = x.astype(BF16)
    rest = x - hi.astype(F32)
    mid = rest.astype(BF16)
    return hi, mid, (rest - mid.astype(F32)).astype(BF16)


def silu(x):
    return x / (1.0 + jnp.exp(-x))


def softplus(x):
    return jnp.maximum(x, 0.0) + jnp.log1p(jnp.exp(-jnp.abs(x)))


def expander(heads, width):
    return onehot(iota((heads, width), 1) // (width // heads) == iota((heads, width), 0))


def spread(x, expand):
    hi, lo = split2(x)
    return mm(hi, expand) + mm(lo, expand)


def ask_kernel(live_dev, readers, bc_ref, tgt_l_ref, tgt_r_ref, out_ref):
    steps = bc_ref.shape[0]
    slots = out_ref.shape[0]
    zeros_l = jnp.zeros((live_dev, STATE), F32)
    place = (iota((live_dev, STATE), 0) + 1).astype(F32)
    parts = [bc_ref[t, 1, 0:live_dev, :].astype(F32) for t in range(steps)]
    parts += [place] + [zeros_l] * (SUB - steps - 1)
    data_l = jnp.concatenate(parts, 0)
    data_l = jnp.concatenate([data_l, jnp.zeros_like(data_l)], 1).astype(BF16)
    parts = [
        bc_ref[t % steps, 1, live_dev : live_dev + readers, :].astype(F32) for t in range(SUB)
    ]
    data_r = jnp.concatenate(parts, 0)
    data_r = jnp.concatenate([jnp.zeros_like(data_r), data_r], 1).astype(BF16)
    pick_l = onehot(iota((slots, SUB * live_dev), 0) == tgt_l_ref[...])
    pick_r = onehot(iota((slots, SUB * readers), 0) == tgt_r_ref[...])
    out_ref[...] = (mm(pick_l, data_l) + mm(pick_r, data_r)).astype(BF16)


def state_kernel(
    len_ref,
    x_ref,
    bc_ref,
    raw_ref,
    rawt_ref,
    decay_ref,
    bias_ref,
    decayt_ref,
    biast_ref,
    cw_ref,
    cb_ref,
    xc_ref,
    cum_ref,
    cumt_ref,
    dtt_ref,
    st_ref,
    xf,
):
    span, width = x_ref.shape
    heads = raw_ref.shape[1]
    taps = cw_ref.shape[0]
    length = len_ref[0]
    xf[0:SUB, :] = jnp.zeros((SUB, width), F32)
    xf[SUB : SUB + span, :] = x_ref[...].astype(F32)
    dt = softplus(raw_ref[...].astype(F32) + bias_ref[...])
    dt = jnp.where(iota((span, heads), 0) < length, dt, 0.0)
    dtt = softplus(rawt_ref[...].astype(F32) + biast_ref[...])
    dtt = jnp.where(iota((heads, span), 1) < length, dtt, 0.0)
    dtt_ref[...] = dtt
    tri = onehot(iota((span, span), 0) >= iota((span, span), 1))
    pieces = split3(dtt * -decayt_ref[...])
    cum = mm_nt(tri, pieces[0]) + mm_nt(tri, pieces[1]) + mm_nt(tri, pieces[2])
    cumt = mm_nt(pieces[0], tri) + mm_nt(pieces[1], tri) + mm_nt(pieces[2], tri)
    cum_ref[...] = cum
    cumt_ref[...] = cumt
    weight = jnp.exp(cum[span - 1 : span, :] - cum) * dt
    expand = expander(heads, width)
    block = 128
    total = jnp.zeros((STATE, width), F32)
    for start in range(0, span, block):
        acc = cb_ref[...]
        for k in range(taps):
            first = SUB - taps + 1 + k + start
            acc = acc + xf[first : first + block, :] * cw_ref[k : k + 1, :]
        xc = silu(acc).astype(BF16)
        xc_ref[start : start + block, :] = xc
        weighted = xc.astype(F32) * spread(weight[start : start + block, :], expand)
        total = total + lax.dot_general(
            bc_ref[0, start : start + block, :],
            weighted.astype(BF16),
            TN,
            preferred_element_type=F32,
        )
    st_ref[0:STATE, :] = jnp.zeros((STATE, width), BF16)
    st_ref[STATE : 2 * STATE, :] = total.astype(BF16)


def prompt_kernel(
    xc_ref, z_ref, bc_ref, cum_ref, cumt_ref, dtt_ref, skip_ref, g_ref, ss_ref, scores
):
    span, width = xc_ref.shape
    heads = cum_ref.shape[1]
    block = 128
    ones = jnp.ones((SUB, block), BF16)
    lanes = iota((block, block), 1)
    causal = iota((block, block), 0) >= lanes
    for start in range(0, span, block):
        stop = start + block
        cmat = bc_ref[1, start:stop, :]
        scores[:, 0:stop] = mm_nt(cmat, bc_ref[0, 0:stop, :])
        square = jnp.zeros((block, block), F32)
        for lane in range(0, width, block):
            halves = []
            for half in range(2):
                head = lane * heads // width + half
                at = cum_ref[start:stop, head : head + 1]
                gap = jnp.where(causal, at - cumt_ref[head : head + 1, start:stop], -jnp.inf)
                near = scores[:, start:stop] * jnp.exp(gap) * dtt_ref[head : head + 1, start:stop]
                yhead = mm(near.astype(BF16), xc_ref[start:stop, lane : lane + block])
                if start:
                    gap = at - cumt_ref[head : head + 1, 0:start]
                    far = scores[:, 0:start] * jnp.exp(gap) * dtt_ref[head : head + 1, 0:start]
                    yhead = yhead + mm(far.astype(BF16), xc_ref[0:start, lane : lane + block])
                halves.append(yhead)
            y = jnp.where(lanes < block // 2, halves[0], halves[1])
            xin = xc_ref[start:stop, lane : lane + block].astype(F32)
            y = y + skip_ref[:, lane : lane + block] * xin
            gate = y * silu(z_ref[start:stop, lane : lane + block].astype(F32))
            g_ref[start:stop, lane : lane + block] = gate
            square = square + gate * gate
        hi, lo = split2(square)
        ss_ref[:, start:stop] = mm_nt(ones, hi) + mm_nt(ones, lo)


def answer_kernel(
    ask_ref, state_ref, conv_ref, prefix_ref, tail_a_ref, tail_b_ref, out_ref, cs, ys
):
    slots = ask_ref.shape[0]
    block = state_ref.shape[0]
    count = ys.shape[0]
    width = prefix_ref.shape[1]
    step = pl.program_id(0)
    ask = ask_ref[...]

    def places():
        row, col = iota((slots, slots), 0), iota((slots, slots), 1)
        return mm(onehot(col == (row // SUB) * SUB + 4), ask)

    @pl.when(step == 0)
    def _():
        place = places().astype(BF16)
        lane0 = onehot(iota((SUB, 2 * STATE), 1) == 0)
        across = mm_nt(lane0, place)[0:1, :].astype(jnp.int32)
        row, col = iota((count, slots), 0), iota((count, slots), 1)
        back = onehot(row + SUB - col % SUB == across * SUB)
        got = mm(back, ask)
        cs[...] = jnp.where(iota(got.shape, 0) % SUB < 4, got, 0.0)

    for k in range(block):
        first = pl.multiple_of((step * block + k) * SUB, SUB)
        cmat = cs[pl.ds(first, SUB), 0:STATE].astype(BF16)
        ys[pl.ds(first, SUB), :] = mm_nt(cmat, state_ref[k]) + conv_ref[k].astype(F32)

    @pl.when(step == pl.num_programs(0) - 1)
    def _():
        place = places()[:, 0:1].astype(jnp.int32)
        row, col = iota((slots, count), 0), iota((slots, count), 1)
        there = onehot(col + SUB - row % SUB == place * SUB)
        live = mm(there, ys[...].astype(BF16)).reshape(slots // SUB, SUB, width)
        live = live + tail_a_ref[...].astype(F32)[None]
        out_ref[:, 0:width] = live.reshape(slots, width).astype(BF16)
        new = mm(ask, prefix_ref[...])
        half = width // 2
        first = iota((slots, half), 0) % SUB < SUB // 2
        new = jnp.where(first, new[:, 0:half], new[:, half:width])
        out_ref[:, width : width + half] = new.astype(BF16)
        tail = jnp.broadcast_to(
            tail_b_ref[...].astype(F32)[None], (slots // SUB,) + tail_b_ref.shape
        )
        out_ref[:, width + half :] = tail.reshape(slots, tail_b_ref.shape[1]).astype(BF16)


def decode_kernel(
    live_dev,
    readers,
    got_ref,
    tgt_l_ref,
    tgt_r_ref,
    xz_ref,
    bc_ref,
    raw_ref,
    decay_ref,
    bias_ref,
    skip_ref,
    cw_ref,
    cb_ref,
    pre_ss_ref,
    g_ref,
    ss_ref,
):
    slots = got_ref.shape[0]
    steps, _, rows, width = xz_ref.shape
    heads = raw_ref.shape[1]
    span = pre_ss_ref.shape[1]
    taps = cw_ref.shape[0]
    half = width // 2
    part = width // 4
    pick_l = onehot(iota((SUB * live_dev, slots), 1) == tgt_l_ref[...])
    pick_r = onehot(iota((SUB * readers, slots), 1) == tgt_r_ref[...])
    live = mm(pick_l, got_ref[:, 0:width])
    new = mm(pick_r, got_ref[:, width:])
    old = mm(pick_r[(SUB - 1) * readers :, :], got_ref[:, 0:width])

    def live_row(r):
        return live[r * live_dev : (r + 1) * live_dev, :]

    def new_row(r, first, last):
        return new[r * readers : (r + 1) * readers, first:last]

    def tail_row(r):
        return jnp.concatenate(
            [new_row(r + i, half, half + part) for i in range(4)], 1
        )

    first = []
    for t in range(steps):
        wide = jnp.concatenate([new_row(t, 0, half), new_row(t + 4, 0, half)], 1)
        first.append(jnp.concatenate([live_row(t), wide], 0))
    inputs = [
        jnp.concatenate([live_row(4), old], 0),
        jnp.concatenate([live_row(5), tail_row(0)], 0),
        jnp.concatenate([live_row(6), tail_row(4)], 0),
    ]
    inputs += [xz_ref[t, 0].astype(F32) for t in range(steps)]
    expand = expander(heads, width)
    weights = [cw_ref[k : k + 1, :].astype(F32) for k in range(taps)]
    dts, logs, bmats, cmats, xcs, gates = [], [], [], [], [], []
    for t in range(steps):
        acc = cb_ref[...]
        for k in range(taps):
            acc = acc + inputs[t + k] * weights[k]
        xcs.append(silu(acc).astype(BF16).astype(F32))
        dt = softplus(raw_ref[t * rows : (t + 1) * rows, :].astype(F32) + bias_ref[...])
        dts.append(dt)
        decayed = -dt * decay_ref[...]
        logs.append(decayed if t == 0 else logs[-1] + decayed)
        bmats.append(bc_ref[t, 0].astype(F32))
        cmats.append(bc_ref[t, 1].astype(F32))
        y = spread(jnp.exp(logs[t]), expand) * first[t]
        for s in range(t + 1):
            score = jnp.sum(bmats[s] * cmats[t], axis=1, keepdims=True)
            factor = dts[s] * score
            if s < t:
                factor = jnp.exp(logs[t] - logs[s]) * factor
            else:
                factor = factor + skip_ref[...]
            y = y + spread(factor, expand) * xcs[s]
        gate = y * silu(xz_ref[t, 1].astype(F32))
        g_ref[t * rows : (t + 1) * rows, :] = gate
        gates.append(gate * gate)
    square = jnp.concatenate(gates, 0)
    hi, lo = split2(square)
    ones = jnp.ones((SUB, width), BF16)
    sums = mm_nt(ones, hi) + mm_nt(ones, lo)
    pad = ss_ref.shape[2] - span - sums.shape[1]
    sums = jnp.concatenate([sums, jnp.zeros((SUB, pad), F32)], 1)
    for i in range(ss_ref.shape[0]):
        ss_ref[i, :, 0:span] = pre_ss_ref[...]
        ss_ref[i, :, span:] = sums


def finish_kernel(width_all, ss_ref, pre_ref, step_ref, gain_ref, pre_out_ref, step_out_ref):
    total = ss_ref[0]
    for i in range(1, ss_ref.shape[0]):
        total = total + ss_ref[i]
    scale = lax.rsqrt(total[0:1, :] / width_all + EPS)
    gain = gain_ref[...]
    span = pre_ref.shape[0]
    block = 128

    def column(first, rows):
        row = jnp.broadcast_to(scale[:, first : first + block], (rows, block))
        diag = iota((rows, block), 0) == iota((rows, block), 1)
        return jnp.sum(jnp.where(diag, row, 0.0), axis=1, keepdims=True)

    for start in range(0, span, block):
        part = slice(start, start + block)
        pre_out_ref[part, :] = (pre_ref[part, :] * column(start, block) * gain).astype(BF16)
    count = step_ref.shape[0]
    for start in range(0, count, block):
        rows = min(block, count - start)
        part = slice(start, start + rows)
        step_out_ref[part, :] = (step_ref[part, :] * column(span + start, rows) * gain).astype(
            BF16
        )


def params(**more):
    return pltpu.CompilerParams(vmem_limit_bytes=40 * 1024 * 1024, **more)


def cost(flops, moved, special=0):
    return pl.CostEstimate(flops=flops, bytes_accessed=moved, transcendentals=special)


def vmem():
    return pl.BlockSpec(memory_space=pltpu.VMEM)


def shape(dims, kind):
    return jax.ShapeDtypeStruct(dims, kind)


def per_device(
    pre_x,
    pre_z,
    pre_bc,
    pre_raw,
    prompt_len,
    live_state,
    live_conv,
    source,
    reader,
    step_xz,
    step_bc,
    step_raw,
    decay,
    dt_bias,
    conv_weight,
    conv_bias,
    skip,
    norm_gain,
):
    _, span, width = pre_x.shape
    mp = lax.axis_size("mp")
    gens = lax.axis_size("gen")
    width_all = width * mp
    live_dev = source.shape[0]
    readers = reader.shape[0]
    heads = pre_raw.shape[2]
    steps, _, rows, _ = step_xz.shape
    slots = gens * SUB
    offset = jnp.arange(SUB, dtype=jnp.int32)[:, None]
    tgt_l = SUB * (source // live_dev)[None, :] + offset
    tgt_r = SUB * reader[None, :] + offset

    ask = pl.pallas_call(
        lambda *refs: ask_kernel(live_dev, readers, *refs),
        out_shape=shape((slots, 2 * STATE), BF16),
        in_specs=[vmem()] * 3,
        out_specs=vmem(),
        compiler_params=params(),
        cost_estimate=cost(2 * slots * 384 * 128, 400000),
        name="ask",
    )(step_bc, tgt_l.reshape(1, -1), tgt_r.reshape(1, -1))
    asked = lax.all_to_all(
        ask.reshape(gens, SUB, 2 * STATE), "gen", split_axis=0, concat_axis=0, tiled=True
    ).reshape(slots, 2 * STATE)

    length = prompt_len[0]
    raw = pre_raw[0]
    xconv, cum, cumt, dtt, prefix = pl.pallas_call(
        state_kernel,
        out_shape=(
            shape((span, width), BF16),
            shape((span, heads), F32),
            shape((heads, span), F32),
            shape((heads, span), F32),
            shape((2 * STATE, width), BF16),
        ),
        in_specs=[pl.BlockSpec(memory_space=pltpu.SMEM)] + [vmem()] * 10,
        out_specs=(vmem(),) * 5,
        scratch_shapes=[pltpu.VMEM((span + SUB, width), F32)],
        compiler_params=params(),
        cost_estimate=cost(2 * 10 * span * span * 64, 2 * span * width * 2, span * width * 2),
        name="state",
    )(
        prompt_len,
        pre_x[0],
        pre_bc[0],
        raw,
        raw.T,
        decay[None],
        dt_bias[None],
        decay[:, None],
        dt_bias[:, None],
        conv_weight.astype(F32),
        conv_bias[None],
    )
    taps = conv_weight.shape[0]
    spots = length - (taps - 1) + jnp.arange(taps - 1, dtype=jnp.int32)
    tails = jnp.where(
        (spots >= 0)[:, None], pre_x[0][jnp.maximum(spots, 0)], jnp.zeros((), BF16)
    )
    tail_a = jnp.concatenate([jnp.zeros((SUB - 1, width), BF16), tails[0:1]], 0)
    tail_b = tails[1:].reshape(SUB, width // 4)
    conv = jnp.pad(live_conv, ((0, 0), (steps, SUB - steps - (taps - 1)), (0, 0)))

    block = 8
    answer = pl.pallas_call(
        answer_kernel,
        grid=(live_dev // block,),
        out_shape=shape((slots, width + width // 2 + width // 4), BF16),
        in_specs=[
            pl.BlockSpec((slots, 2 * STATE), lambda i: (0, 0)),
            pl.BlockSpec((block, width, STATE), lambda i: (i, 0, 0)),
            pl.BlockSpec((block, SUB, width), lambda i: (i, 0, 0)),
            pl.BlockSpec((2 * STATE, width), lambda i: (0, 0)),
            pl.BlockSpec((SUB, width), lambda i: (0, 0)),
            pl.BlockSpec((SUB, width // 4), lambda i: (0, 0)),
        ],
        out_specs=pl.BlockSpec((slots, width + width // 2 + width // 4), lambda i: (0, 0)),
        scratch_shapes=[
            pltpu.VMEM((live_dev * SUB, 2 * STATE), F32),
            pltpu.VMEM((live_dev * SUB, width), F32),
        ],
        compiler_params=params(dimension_semantics=("arbitrary",)),
        cost_estimate=cost(2 * slots * 512 * 1024, 6000000),
        name="answer",
    )(asked, live_state.reshape(live_dev, width, STATE), conv, prefix, tail_a, tail_b)
    lanes = answer.shape[1]
    got = lax.all_to_all(
        answer.reshape(gens, SUB, lanes), "gen", split_axis=0, concat_axis=0, tiled=True
    ).reshape(slots, lanes)

    pre_gate, pre_ss = pl.pallas_call(
        prompt_kernel,
        out_shape=(shape((span, width), F32), shape((SUB, span), F32)),
        in_specs=[vmem()] * 7,
        out_specs=(vmem(), vmem()),
        scratch_shapes=[pltpu.VMEM((128, span), F32)],
        compiler_params=params(),
        cost_estimate=cost(2 * heads * span * span * 128, 2500000, heads * span * span),
        name="prompt",
    )(xconv, pre_z[0], pre_bc[0], cum, cumt, dtt, jnp.repeat(skip, width // heads)[None])

    count = steps * rows
    padded = -(-(span + count) // 128) * 128
    step_gate, sums = pl.pallas_call(
        lambda *refs: decode_kernel(live_dev, readers, *refs),
        out_shape=(shape((count, width), F32), shape((mp, SUB, padded), F32)),
        in_specs=[vmem()] * 12,
        out_specs=(vmem(), vmem()),
        compiler_params=params(),
        cost_estimate=cost(2 * 384 * 512 * 512, 2500000),
        name="decode",
    )(
        got,
        tgt_l.reshape(-1, 1),
        tgt_r.reshape(-1, 1),
        step_xz,
        step_bc,
        step_raw.reshape(count, heads),
        decay[None],
        dt_bias[None],
        skip[None],
        conv_weight,
        conv_bias[None],
        pre_ss,
    )
    sums = lax.all_to_all(sums, "mp", split_axis=0, concat_axis=0, tiled=True)

    prefill_out, decoded = pl.pallas_call(
        lambda *refs: finish_kernel(width_all, *refs),
        out_shape=(shape((span, width), BF16), shape((count, width), BF16)),
        in_specs=[vmem()] * 4,
        out_specs=(vmem(), vmem()),
        compiler_params=params(),
        cost_estimate=cost(1000000, 2500000),
        name="finish",
    )(sums, pre_gate, step_gate, norm_gain[None])
    return (prefill_out[None], decoded.reshape(steps, rows, width))


def solution(mesh):
    placed = (
        P("gen", None, "mp"),
        P("gen", None, "mp"),
        P("gen", None, None, "mp"),
        P("gen", None, "mp"),
        P("gen"),
        P("gen", "mp", None, None),
        P("gen", None, "mp"),
        P("gen"),
        P("gen"),
        P(None, None, "gen", "mp"),
        P(None, None, "gen", "mp"),
        P(None, "gen", "mp"),
        P("mp"),
        P("mp"),
        P(None, "mp"),
        P("mp"),
        P("mp"),
        P("mp"),
    )
    return jax.shard_map(
        per_device,
        mesh=mesh,
        in_specs=placed,
        out_specs=(P("gen", None, "mp"), P(None, "gen", "mp")),
        check_vma=False,
    )
```

time: 578 us -> 123 us (0.21)
  blocking collectives: 242 us -> 15.3 us
  matrix products: 169 us -> 0 us
  local copies, waits for them, and re-layouts: 88.6 us -> 17.8 us
  waiting for transfers between devices: 0.02 us -> 38.8 us
  other arithmetic: 23.8 us -> 2.13 us
  between operations: 16.1 us -> 1.5 us
  loops' own time: 13.8 us -> 0 us
  Pallas kernels: 0 us -> 12.3 us
  starting transfers between devices: 22.2 us -> 34 us
    all_gather x1 -> x0, blocking collectives: 190 us -> none  [per_device(): lax.all_gather(prefix_tail[None], 'gen', axis=0, tiled=True)]
    dot_general x27 -> x0, matrix products: 169 us -> none  [the longest x4 125 us: decode_local(): jnp.einsum('rhpn,rhn->rhp', state, cexp, precision=lax.Precision.HIGHEST)]
    all_to_all x2, waiting for transfers between devices: 0.01 us -> 38.8 us  [the longest x1 38.8 us: per_device(): lax.all_to_all(answer.reshape(gens, SUB, lanes), 'gen', split_axis=0, con...]
    unnamed x1 -> x0, blocking collectives: 30.4 us -> none
    reshape x15 -> x1, local copies, waits for them, and re-layouts: 27.6 us -> 0.01 us  [per_device(): tail_b = tails[1:].reshape(SUB, width // 4)]
    psum x1 -> x0, blocking collectives: 21.6 us -> none  [per_device(): pre_total = lax.psum(jnp.sum(pre_gate * pre_gate, axis=-1), 'mp')]
    unnamed x91 -> x49, local copies, waits for them, and re-layouts: 33.4 us -> 13.2 us
    all_to_all x0 -> x1, blocking collectives: none -> 15.3 us  [per_device(): sums = lax.all_to_all(sums, 'mp', split_axis=0, concat_axis=0, tiled=True)]
  transfers between devices with their start and end apart: 3 -> 2, of which waited for: 0 -> 1; matrix products, arithmetic and copies ran while one was open for 20% -> 6% of each run, Pallas kernels for 0% -> 4%
where the time goes in v1:
time: 123 us; the launch traced here: 122 us
  waiting for transfers between devices  38.8 us (32%)
  starting transfers between devices  34 us (28%)
  local copies, waits for them, and re-layouts  17.8 us (14%)
  blocking collectives  15.3 us (12%)
  Pallas kernels  12.3 us (10%)
  other arithmetic  2.13 us (2%)
  between operations  1.5 us (1%)
    all_to_all x1, waiting for transfers between devices, per_device(): lax.all_to_all(answer.reshape(gens, SUB, lanes), 'gen', split_axis=0, con...  38.8 us
    all_to_all x1, starting transfers between devices, per_device(): lax.all_to_all(ask.reshape(gens, SUB, 2 * STATE), 'gen', split_axis=0, co...  19.3 us
    all_to_all x1, blocking collectives, per_device(): sums = lax.all_to_all(sums, 'mp', split_axis=0, concat_axis=0, tiled=True)  15.3 us
    all_to_all x1, starting transfers between devices, per_device(): lax.all_to_all(answer.reshape(gens, SUB, lanes), 'gen', split_axis=0, con...  14.7 us
    unnamed x49, local copies, waits for them, and re-layouts  13.2 us
    pallas_call x1, Pallas kernels, per_device(): pl.pallas_call(answer_kernel, grid=(live_dev // block,), out_shape=shape(...  4.15 us
    pallas_call x1, Pallas kernels, per_device(): pl.pallas_call(state_kernel, out_shape=(shape((span, width), BF16), shape...  2.76 us
  transfers between devices with their start and end apart: 2, of which 1 were waited for; matrix products, arithmetic and copies ran while one was open for 6% of the time, Pallas kernels for 4%

profile of v1, /device:TPU:1, one launch (start us, length us, event | category | flops | bytes accessed | tf_op | source)
XLA Modules:
  0.0 121.9 jit_solution(15236495645259691118)
XLA Ops:
  0.6 0.7 fusion
  1.3 0.1 add.97.refs_1_
  1.4 0.7 broadcast_multiply_fusion
  2.0 0.1 add.101.refs_2_
  2.1 0.0 copy-start.2
  2.1 0.9 copy-done.2
  3.0 1.0 ask.1
  4.0 19.3 %all-to-all-start = ((bf16[64,8,128]{2,1,0:T(8,128)(2,1)}), bf16[64,8,128]{2,1,0:T(8,128)(2,1)S(1)}, u32[]{:S(2)}, u32[]{:S(2)}) async-start(bf16[64,8,128]{2,1,0:T(8,128)(2,1)} %bitcast), calls=%async_computation | async-start | bytes 262144 | tf_op jit(solution)/shard_map/all_to_all | solution.py:397
  24.0 1.7 %gather_fusion = bf16[3,512]{1,0:T(4,128)(2,1)S(1)} fusion(bf16[512,512]{1,0:T(8,128)(2,1)} %bitcast.42, s32[1024]{0:T(1024)S(1)} %pad_clamp_fusion), kind=kCustom, calls=%fused_computation | custom fusion | bytes 6156 | tf_op jit(solution)/shard_map/gather | solution.py:434
  25.6 0.1 broadcast_select_fusion
  25.7 1.1 copy.28
  26.8 0.9 copy.29.raw_ref
  27.7 0.7 convert_element_type.5.cw_ref
  28.4 0.7 copy.30.decayt_ref
  29.1 0.7 copy.31.biast_ref
  29.9 1.0 copy.27
  30.9 0.1 pad.5.conv_ref
  30.9 0.0 copy-start.5
  31.0 0.7 copy-done.5
  31.6 0.0 copy-start.6
  31.6 0.7 copy-done.6
  32.3 0.0 copy-start.9
  32.3 0.7 copy-done.9
  33.0 0.0 copy-start.11
  33.0 0.7 copy-done.11
  33.6 0.0 copy-start.14
  33.6 1.0 copy-done.14
  34.7 0.0 copy-start.13
  34.7 2.8 %state.1 = (bf16[512,512]{1,0:T(8,128)(2,1)S(1)}, f32[512,8]{1,0:T(8,128)S(1)}, f32[8,512]{1,0:T(8,128)S(1)}, f32[8,512]{1,0:T(8,128)S(1)}, bf16[128,512]{1,0:T(8,128)(2,1)S(1)}) custom-call(s32[1]{0:T(128)S(6)} %copy.35.len_ref, bf16[512,512]{1,0:T(8,128)(2,1)S(1)} %bitcast.43, bf16[2,512,64]{2,1,0:T(8,128)(2,1)S(1)} %bitcast.27, ...), custom_call_target="tpu_custom_call" | custom-call | flops 335544320 | bytes 1048576 | tf_op jit(solution)/shard_map/state/pallas_call | solution.py:403
  37.5 0.0 copy-start.16
  37.5 0.8 copy-done.16
  38.2 0.7 copy-done.18
  38.9 0.0 all-to-all-done
  39.0 2.2 %copy-done = bf16[32,8,64,64]{3,2,1,0:T(8,128)(2,1)S(1)} copy-done((bf16[32,8,64,64]{3,2,1,0:T(8,128)(2,1)S(1)}, bf16[32,8,64,64]{3,2,1,0:T(8,128)(2,1)}, u32[]{:S(2)}) %copy-start) | copy-done | bytes 2097176
  41.1 4.2 %answer.1 = bf16[512,896]{1,0:T(8,128)(2,1)} custom-call(bf16[512,128]{1,0:T(8,128)(2,1)S(1)} %bitcast.26, bf16[32,512,64]{2,1,0:T(8,128)(2,1)S(1)} %bitcast.24, bf16[32,8,512]{2,1,0:T(8,128)(2,1)S(1)} %pad.5.conv_ref, bf16[128,512]{1,0:T(8,128)(2,1)S(1)} %get-tuple-element.13.prefix_ref, bf16[8,512]{1,0:T(8,128)(2,1)S(1)} %concatenate.3.tail_a_ref, ...), custom_call_target="tpu_custom_call" | custom-call | flops 536870912 | bytes 6000000 | tf_op jit(solution)/shard_map/answer/pallas_call | solution.py:441
  45.3 0.0 copy-start.10
  45.3 0.0 copy-start.12
  45.3 0.0 copy-start.8
  45.3 14.7 %all-to-all-start.1 = ((bf16[64,8,896]{2,1,0:T(8,128)(2,1)}), bf16[64,8,896]{2,1,0:T(8,128)(2,1)S(1)}, u32[]{:S(2)}, u32[]{:S(2)}) async-start(bf16[64,8,896]{2,1,0:T(8,128)(2,1)} %bitcast.14), calls=%async_computation.1 | async-start | bytes 1835008 | tf_op jit(solution)/shard_map/all_to_all | solution.py:463
  60.1 0.1 add.108.refs_1_
  60.2 0.1 add.109.refs_2_
  60.3 0.0 copy-done.13
  60.3 0.1 broadcast_in_dim.56
  60.4 0.0 copy-done.20
  60.4 0.1 broadcast_in_dim_reshape.3.skip_ref
  60.5 0.0 copy-done.22
  60.5 0.1 copy.32
  60.6 0.0 copy-done.15
  60.6 0.0 copy-start.17
  60.6 1.0 copy-done.17
  61.6 0.9 copy-done.19
  62.6 0.7 copy-done.21
  63.3 2.2 %prompt.1 = (f32[512,512]{1,0:T(8,128)S(1)}, f32[8,512]{1,0:T(8,128)S(1)}) custom-call(bf16[512,512]{1,0:T(8,128)(2,1)S(1)} %copy-done.17, bf16[512,512]{1,0:T(8,128)(2,1)S(1)} %bitcast.44, bf16[2,512,64]{2,1,0:T(8,128)(2,1)S(1)} %bitcast.28, f32[512,8]{1,0:T(8,128)S(1)} %copy-done.19, f32[8,512]{1,0:T(8,128)S(1)} %get-tuple-element.16.cumt_ref, ...), custom_call_target="tpu_custom_call" | custom-call | flops 536870912 | bytes 2500000 | tf_op jit(solution)/shard_map/prompt/pallas_call | solution.py:467
  65.5 38.8 %all-to-all-done.1 = bf16[64,8,896]{2,1,0:T(8,128)(2,1)S(1)} async-done(((bf16[64,8,896]{2,1,0:T(8,128)(2,1)}), bf16[64,8,896]{2,1,0:T(8,128)(2,1)S(1)}, u32[]{:S(2)}, u32[]{:S(2)}) %all-to-all-start.1) | async-done | bytes 917536 | tf_op jit(solution)/shard_map/all_to_all | solution.py:463
  104.3 0.0 copy-done.1
  104.3 0.0 copy-done.3
  104.3 0.0 copy-done.4
  104.3 0.0 copy-done.7
  104.3 0.0 copy-done.10
  104.3 0.0 copy-done.12
  104.3 1.2 decode.1
  105.5 15.3 %all_to_all.15.refs_0_ = f32[8,8,768]{2,1,0:T(8,128)S(1)} all-to-all(f32[8,8,768]{2,1,0:T(8,128)S(1)} %get-tuple-element.19), channel_id=1, replica_groups=mesh['gen'=64,'mp'=8] {'mp'}, dimensions={0} | all-to-all | bytes 393216 | tf_op jit(solution)/shard_map/all_to_all | solution.py:502
  120.8 0.0 copy-done.8
  120.8 1.0 finish.1
  (20 shorter events, 0.1 us)
Async XLA Ops:
  2.1 0.9 copy-start.2
  4.0 35.0 %all-to-all-start = ((bf16[64,8,128]{2,1,0:T(8,128)(2,1)}), bf16[64,8,128]{2,1,0:T(8,128)(2,1)S(1)}, u32[]{:S(2)}, u32[]{:S(2)}) async-start(bf16[64,8,128]{2,1,0:T(8,128)(2,1)} %bitcast), calls=%async_computation | async-start | bytes 262144 | tf_op jit(solution)/shard_map/all_to_all | solution.py:397
  30.9 0.7 copy-start.5
  31.6 0.7 copy-start.6
  32.3 0.7 copy-start.9
  33.0 0.7 copy-start.11
  33.6 1.0 copy-start.14
  34.7 25.6 %copy-start.13 = (f32[8]{0:T(128)S(1)}, f32[8]{0:T(128)}, u32[]{:S(2)}) copy-start(f32[8]{0:T(128)} %param.34) | copy-start | bytes 100
  34.7 25.8 %copy-start.22 = (bf16[4,48,8]{1,2,0:T(8,128)(2,1)S(1)}, bf16[4,48,8]{1,2,0:T(8,128)(2,1)}, u32[]{:S(2)}) copy-start(bf16[4,48,8]{1,2,0:T(8,128)(2,1)} %param.29) | copy-start | bytes 9220
  34.7 25.9 %copy-start.15 = (bf16[1,512,512]{2,1,0:T(8,128)(2,1)S(1)}, bf16[1,512,512]{2,1,0:T(8,128)(2,1)}, u32[]{:S(2)}) copy-start(bf16[1,512,512]{2,1,0:T(8,128)(2,1)} %param.19) | copy-start | bytes 1572868
  37.5 0.8 copy-start.16
  38.2 0.7 copy-start.18
  38.9 21.4 %copy-start.20 = (f32[8,512]{1,0:T(8,128)}, f32[8,512]{1,0:T(8,128)S(1)}, u32[]{:S(2)}) copy-start(f32[8,512]{1,0:T(8,128)S(1)} %get-tuple-element.17.dtt_ref) | copy-start | bytes 49156
  38.9 2.2 %copy-start = (bf16[32,8,64,64]{3,2,1,0:T(8,128)(2,1)S(1)}, bf16[32,8,64,64]{3,2,1,0:T(8,128)(2,1)}, u32[]{:S(2)}) copy-start(bf16[32,8,64,64]{3,2,1,0:T(8,128)(2,1)} %param.23) | copy-start | bytes 6291460
  45.3 59.0 %copy-start.1 = (bf16[4,2,48,512]{3,2,1,0:T(8,128)(2,1)S(1)}, bf16[4,2,48,512]{3,2,1,0:T(8,128)(2,1)}, u32[]{:S(2)}) copy-start(bf16[4,2,48,512]{3,2,1,0:T(8,128)(2,1)} %refs_3_.1) | copy-start | bytes 1179652
  45.3 59.0 %copy-start.3 = (bf16[4,2,48,64]{3,2,1,0:T(8,128)(2,1)S(1)}, bf16[4,2,48,64]{3,2,1,0:T(8,128)(2,1)}, u32[]{:S(2)}) copy-start(bf16[4,2,48,64]{3,2,1,0:T(8,128)(2,1)} %refs_4_.1) | copy-start | bytes 147460
  45.3 59.0 %copy-start.4 = (bf16[4,512]{1,0:T(4,128)(2,1)S(1)}, bf16[4,512]{1,0:T(4,128)(2,1)}, u32[]{:S(2)}) copy-start(bf16[4,512]{1,0:T(4,128)(2,1)} %refs_9_.1) | copy-start | bytes 12292
  45.3 59.0 %copy-start.7 = (f32[512]{0:T(512)S(1)}, f32[512]{0:T(512)}, u32[]{:S(2)}) copy-start(f32[512]{0:T(512)} %param.33) | copy-start | bytes 6148
  45.3 59.0 %copy-start.10 = (f32[8]{0:T(128)S(1)}, f32[8]{0:T(128)}, u32[]{:S(2)}) copy-start(f32[8]{0:T(128)} %param.30) | copy-start | bytes 100
  45.3 59.0 %copy-start.12 = (f32[8]{0:T(128)S(1)}, f32[8]{0:T(128)}, u32[]{:S(2)}) copy-start(f32[8]{0:T(128)} %param.31) | copy-start | bytes 100
  45.3 75.5 %copy-start.8 = (f32[512]{0:T(512)S(1)}, f32[512]{0:T(512)}, u32[]{:S(2)}) copy-start(f32[512]{0:T(512)} %param.35) | copy-start | bytes 6148
  45.3 59.0 %all-to-all-start.1 = ((bf16[64,8,896]{2,1,0:T(8,128)(2,1)}), bf16[64,8,896]{2,1,0:T(8,128)(2,1)S(1)}, u32[]{:S(2)}, u32[]{:S(2)}) async-start(bf16[64,8,896]{2,1,0:T(8,128)(2,1)} %bitcast.14), calls=%async_computation.1 | async-start | bytes 1835008 | tf_op jit(solution)/shard_map/all_to_all | solution.py:463
  60.6 1.0 copy-start.17
  61.6 0.9 copy-start.19
  62.6 0.7 copy-start.21

commit v2 on v1

--- a/solution.py
+++ b/solution.py
@@ -59,9 +59,27 @@
     return mm(hi, expand) + mm(lo, expand)
 
 
-def ask_kernel(live_dev, readers, bc_ref, tgt_l_ref, tgt_r_ref, out_ref):
+def fetch(sources, targets, sems):
+    copies = [
+        pltpu.make_async_copy(source, target, sems.at[i])
+        for i, (source, target) in enumerate(zip(sources, targets))
+    ]
+    for copy in copies:
+        copy.start()
+    return copies
+
+
+def ask_kernel(*refs):
+    sources, out_ref, targets, sems = refs[:5], refs[5], refs[6:11], refs[11]
+    for copy in fetch(sources, targets, sems):
+        copy.wait()
+    bc_ref, source_ref, reader_ref, len_ref, x_ref = targets
     steps = bc_ref.shape[0]
     slots = out_ref.shape[0]
+    live_dev = source_ref.shape[1]
+    readers = reader_ref.shape[1]
+    span, width = x_ref.shape
+    part = width // 4
     zeros_l = jnp.zeros((live_dev, STATE), F32)
     place = (iota((live_dev, STATE), 0) + 1).astype(F32)
     parts = [bc_ref[t, 1, 0:live_dev, :].astype(F32) for t in range(steps)]
@@ -73,71 +91,84 @@
     ]
     data_r = jnp.concatenate(parts, 0)
     data_r = jnp.concatenate([jnp.zeros_like(data_r), data_r], 1).astype(BF16)
-    pick_l = onehot(iota((slots, SUB * live_dev), 0) == tgt_l_ref[...])
-    pick_r = onehot(iota((slots, SUB * readers), 0) == tgt_r_ref[...])
-    out_ref[...] = (mm(pick_l, data_l) + mm(pick_r, data_r)).astype(BF16)
-
-
-def state_kernel(
-    len_ref,
-    x_ref,
-    bc_ref,
-    raw_ref,
-    rawt_ref,
-    decay_ref,
-    bias_ref,
-    decayt_ref,
-    biast_ref,
-    cw_ref,
-    cb_ref,
-    xc_ref,
-    cum_ref,
-    cumt_ref,
-    dtt_ref,
-    st_ref,
-    xf,
-):
+    first_l = lax.div(source_ref[...], live_dev) * SUB
+    first_r = reader_ref[...] * SUB
+    tgt_l = jnp.concatenate([first_l + r for r in range(SUB)], 1)
+    tgt_r = jnp.concatenate([first_r + r for r in range(SUB)], 1)
+    pick_l = onehot(iota((slots, SUB * live_dev), 0) == tgt_l)
+    pick_r = onehot(iota((slots, SUB * readers), 0) == tgt_r)
+    out_ref[:, 0 : 2 * STATE] = (mm(pick_l, data_l) + mm(pick_r, data_r)).astype(BF16)
+    row, col = iota((2 * SUB, span), 0), iota((2 * SUB, span), 1)
+    last = onehot(col == len_ref[...] - 2 + row // SUB)
+    both = mm(last, x_ref[...])
+    lane_part = iota((SUB, part), 0) % 4
+    tail = jnp.zeros((SUB, part), F32)
+    for i in range(4):
+        lanes = slice(i * part, (i + 1) * part)
+        piece = jnp.where(iota((SUB, part), 0) < 4, both[0:SUB, lanes], both[SUB:, lanes])
+        tail = jnp.where(lane_part == i, piece, tail)
+    tail = jnp.broadcast_to(tail[None], (slots // SUB, SUB, part))
+    out_ref[:, 2 * STATE :] = tail.reshape(slots, part).astype(BF16)
+
+
+def state_kernel(*refs):
+    sources, outs, targets = refs[:10], refs[10:18], refs[18:26]
+    sems, xf = refs[26], refs[27]
+    xc_ref, cum_ref, cumt_ref, dtt_ref, st_ref, tail_ref, live_ref, conv_ref = outs
+    copies = fetch(sources, targets + (live_ref, conv_ref), sems)
+    for copy in copies[:8]:
+        copy.wait()
+    len_ref, rawt_ref, decay_ref, bias_ref, cw_ref, cb_ref, bct_ref, x_ref = targets
     span, width = x_ref.shape
-    heads = raw_ref.shape[1]
+    heads = rawt_ref.shape[0]
     taps = cw_ref.shape[0]
-    length = len_ref[0]
+    length = len_ref[...]
     xf[0:SUB, :] = jnp.zeros((SUB, width), F32)
     xf[SUB : SUB + span, :] = x_ref[...].astype(F32)
-    dt = softplus(raw_ref[...].astype(F32) + bias_ref[...])
-    dt = jnp.where(iota((span, heads), 0) < length, dt, 0.0)
-    dtt = softplus(rawt_ref[...].astype(F32) + biast_ref[...])
+    square = iota((heads, heads), 0) == iota((heads, heads), 1)
+
+    def column(row):
+        return jnp.sum(jnp.where(square, row, 0.0), axis=1, keepdims=True)
+
+    dtt = softplus(rawt_ref[...].astype(F32) + column(bias_ref[...]))
     dtt = jnp.where(iota((heads, span), 1) < length, dtt, 0.0)
     dtt_ref[...] = dtt
     tri = onehot(iota((span, span), 0) >= iota((span, span), 1))
-    pieces = split3(dtt * -decayt_ref[...])
-    cum = mm_nt(tri, pieces[0]) + mm_nt(tri, pieces[1]) + mm_nt(tri, pieces[2])
+    pieces = split3(dtt * -column(decay_ref[...]))
+    cum_ref[...] = mm_nt(tri, pieces[0]) + mm_nt(tri, pieces[1]) + mm_nt(tri, pieces[2])
     cumt = mm_nt(pieces[0], tri) + mm_nt(pieces[1], tri) + mm_nt(pieces[2], tri)
-    cum_ref[...] = cum
     cumt_ref[...] = cumt
-    weight = jnp.exp(cum[span - 1 : span, :] - cum) * dt
+    weight = jnp.exp(cumt[:, span - 1 : span] - cumt) * dtt
+    weight_hi, weight_lo = split2(weight)
     expand = expander(heads, width)
+    weights = [cw_ref[k : k + 1, :].astype(F32) for k in range(taps)]
     block = 128
     total = jnp.zeros((STATE, width), F32)
     for start in range(0, span, block):
+        part = slice(start, start + block)
         acc = cb_ref[...]
         for k in range(taps):
             first = SUB - taps + 1 + k + start
-            acc = acc + xf[first : first + block, :] * cw_ref[k : k + 1, :]
+            acc = acc + xf[first : first + block, :] * weights[k]
         xc = silu(acc).astype(BF16)
-        xc_ref[start : start + block, :] = xc
-        weighted = xc.astype(F32) * spread(weight[start : start + block, :], expand)
-        total = total + lax.dot_general(
-            bc_ref[0, start : start + block, :],
-            weighted.astype(BF16),
-            TN,
-            preferred_element_type=F32,
+        xc_ref[part, :] = xc
+        wide = lax.dot_general(weight_hi[:, part], expand, TN, preferred_element_type=F32)
+        wide = wide + lax.dot_general(
+            weight_lo[:, part], expand, TN, preferred_element_type=F32
         )
+        weighted = (xc.astype(F32) * wide).astype(BF16)
+        total = total + mm(bct_ref[0, :, part], weighted)
     st_ref[0:STATE, :] = jnp.zeros((STATE, width), BF16)
     st_ref[STATE : 2 * STATE, :] = total.astype(BF16)
+    row, col = iota((SUB, span), 0), iota((SUB, span), 1)
+    tail = onehot((col == length - (taps - 1)) & (row == SUB - 1))
+    tail_ref[...] = mm(tail, x_ref[...]).astype(BF16)
+    for copy in copies[8:]:
+        copy.wait()
 
 
 def prompt_kernel(
-    xc_ref, z_ref, bc_ref, cum_ref, cumt_ref, dtt_ref, skip_ref, g_ref, ss_ref, scores
+    xc_ref, z_ref, bct_ref, cum_ref, cumt_ref, dtt_ref, skip_ref, g_ref, ss_ref, scores
 ):
     span, width = xc_ref.shape
     heads = cum_ref.shape[1]
@@ -147,8 +178,9 @@
     causal = iota((block, block), 0) >= lanes
     for start in range(0, span, block):
         stop = start + block
-        cmat = bc_ref[1, start:stop, :]
-        scores[:, 0:stop] = mm_nt(cmat, bc_ref[0, 0:stop, :])
+        scores[:, 0:stop] = lax.dot_general(
+            bct_ref[1, :, start:stop], bct_ref[0, :, 0:stop], TN, preferred_element_type=F32
+        )
         square = jnp.zeros((block, block), F32)
         for lane in range(0, width, block):
             halves = []
@@ -173,58 +205,47 @@
         ss_ref[:, start:stop] = mm_nt(ones, hi) + mm_nt(ones, lo)
 
 
-def answer_kernel(
-    ask_ref, state_ref, conv_ref, prefix_ref, tail_a_ref, tail_b_ref, out_ref, cs, ys
-):
+def answer_kernel(ask_ref, state_ref, conv_ref, prefix_ref, tail_ref, out_ref, cs, ys):
     slots = ask_ref.shape[0]
-    block = state_ref.shape[0]
+    live_dev = state_ref.shape[0]
     count = ys.shape[0]
     width = prefix_ref.shape[1]
-    step = pl.program_id(0)
-    ask = ask_ref[...]
-
-    def places():
-        row, col = iota((slots, slots), 0), iota((slots, slots), 1)
-        return mm(onehot(col == (row // SUB) * SUB + 4), ask)
-
-    @pl.when(step == 0)
-    def _():
-        place = places().astype(BF16)
-        lane0 = onehot(iota((SUB, 2 * STATE), 1) == 0)
-        across = mm_nt(lane0, place)[0:1, :].astype(jnp.int32)
-        row, col = iota((count, slots), 0), iota((count, slots), 1)
-        back = onehot(row + SUB - col % SUB == across * SUB)
-        got = mm(back, ask)
-        cs[...] = jnp.where(iota(got.shape, 0) % SUB < 4, got, 0.0)
-
-    for k in range(block):
-        first = pl.multiple_of((step * block + k) * SUB, SUB)
-        cmat = cs[pl.ds(first, SUB), 0:STATE].astype(BF16)
-        ys[pl.ds(first, SUB), :] = mm_nt(cmat, state_ref[k]) + conv_ref[k].astype(F32)
-
-    @pl.when(step == pl.num_programs(0) - 1)
-    def _():
-        place = places()[:, 0:1].astype(jnp.int32)
-        row, col = iota((slots, count), 0), iota((slots, count), 1)
-        there = onehot(col + SUB - row % SUB == place * SUB)
-        live = mm(there, ys[...].astype(BF16)).reshape(slots // SUB, SUB, width)
-        live = live + tail_a_ref[...].astype(F32)[None]
-        out_ref[:, 0:width] = live.reshape(slots, width).astype(BF16)
-        new = mm(ask, prefix_ref[...])
-        half = width // 2
-        first = iota((slots, half), 0) % SUB < SUB // 2
-        new = jnp.where(first, new[:, 0:half], new[:, half:width])
-        out_ref[:, width : width + half] = new.astype(BF16)
-        tail = jnp.broadcast_to(
-            tail_b_ref[...].astype(F32)[None], (slots // SUB,) + tail_b_ref.shape
-        )
-        out_ref[:, width + half :] = tail.reshape(slots, tail_b_ref.shape[1]).astype(BF16)
+    half = width // 2
+    ask = ask_ref[:, 0 : 2 * STATE]
+    row, col = iota((slots, slots), 0), iota((slots, slots), 1)
+    place = mm(onehot(col == (row // SUB) * SUB + 4), ask)
+    lane0 = onehot(iota((SUB, 2 * STATE), 1) == 0)
+    across = mm_nt(lane0, place.astype(BF16))[0:1, :].astype(jnp.int32)
+    row, col = iota((count, slots), 0), iota((count, slots), 1)
+    back = onehot(row + SUB - col % SUB == across * SUB)
+    got = mm(back, ask)
+    cs[...] = jnp.where(iota(got.shape, 0) % SUB < 4, got, 0.0)
+    for k in range(live_dev):
+        rows = slice(k * SUB, (k + 1) * SUB)
+        ys[rows, :] = mm_nt(cs[rows, 0:STATE].astype(BF16), state_ref[k])
+    place = place[:, 0:1].astype(jnp.int32)
+    row, col = iota((slots, count), 0), iota((slots, count), 1)
+    there = onehot(col + SUB - row % SUB == place * SUB)
+    live = mm(there, ys[...].astype(BF16))
+    kept = conv_ref.shape[0]
+    row, col = iota((slots, kept), 0), iota((slots, kept), 1)
+    there = onehot(
+        (lax.div(col, live_dev) + 4 == row % SUB) & (col % live_dev + 1 == place)
+    )
+    live = (live + mm(there, conv_ref[...])).reshape(slots // SUB, SUB, width)
+    live = live + tail_ref[...].astype(F32)[None]
+    out_ref[:, 0:width] = live.reshape(slots, width).astype(BF16)
+    new = mm(ask, prefix_ref[...])
+    first = iota((slots, half), 0) % SUB < SUB // 2
+    new = jnp.where(first, new[:, 0:half], new[:, half:width])
+    out_ref[:, width : width + half] = new.astype(BF16)
 
 
 def decode_kernel(
     live_dev,
     readers,
     got_ref,
+    ask_ref,
     tgt_l_ref,
     tgt_r_ref,
     xz_ref,
@@ -245,12 +266,12 @@
     span = pre_ss_ref.shape[1]
     taps = cw_ref.shape[0]
     half = width // 2
-    part = width // 4
     pick_l = onehot(iota((SUB * live_dev, slots), 1) == tgt_l_ref[...])
     pick_r = onehot(iota((SUB * readers, slots), 1) == tgt_r_ref[...])
     live = mm(pick_l, got_ref[:, 0:width])
     new = mm(pick_r, got_ref[:, width:])
     old = mm(pick_r[(SUB - 1) * readers :, :], got_ref[:, 0:width])
+    late = mm(pick_r, ask_ref[:, 2 * STATE :])
 
     def live_row(r):
         return live[r * live_dev : (r + 1) * live_dev, :]
@@ -260,7 +281,7 @@
 
     def tail_row(r):
         return jnp.concatenate(
-            [new_row(r + i, half, half + part) for i in range(4)], 1
+            [late[(r + i) * readers : (r + i + 1) * readers, :] for i in range(4)], 1
         )
 
     first = []
@@ -337,7 +358,7 @@
 
 
 def params(**more):
-    return pltpu.CompilerParams(vmem_limit_bytes=40 * 1024 * 1024, **more)
+    return pltpu.CompilerParams(vmem_limit_bytes=24 * 1024 * 1024, **more)
 
 
 def cost(flops, moved, special=0):
@@ -346,6 +367,10 @@
 
 def vmem():
     return pl.BlockSpec(memory_space=pltpu.VMEM)
+
+
+def hbm():
+    return pl.BlockSpec(memory_space=pltpu.HBM)
 
 
 def shape(dims, kind):
@@ -385,22 +410,42 @@
     tgt_l = SUB * (source // live_dev)[None, :] + offset
     tgt_r = SUB * reader[None, :] + offset
 
+    length = prompt_len.reshape(1, 1)
+    conv_rows = jnp.transpose(live_conv, (1, 0, 2)).reshape(-1, width)
+    bct = jnp.swapaxes(pre_bc[0], 1, 2)
+    dma = pltpu.SemaphoreType.DMA
+
+    def staged(*arrays):
+        return [pltpu.VMEM(array.shape, array.dtype) for array in arrays]
+
+    operands = (step_bc, source[None], reader[None], length, pre_x[0])
     ask = pl.pallas_call(
-        lambda *refs: ask_kernel(live_dev, readers, *refs),
-        out_shape=shape((slots, 2 * STATE), BF16),
-        in_specs=[vmem()] * 3,
+        ask_kernel,
+        out_shape=shape((slots, 2 * STATE + width // 4), BF16),
+        in_specs=[hbm()] * len(operands),
         out_specs=vmem(),
+        scratch_shapes=staged(*operands) + [dma((len(operands),))],
         compiler_params=params(),
-        cost_estimate=cost(2 * slots * 384 * 128, 400000),
+        cost_estimate=cost(2 * slots * 384 * 128, 800000),
         name="ask",
-    )(step_bc, tgt_l.reshape(1, -1), tgt_r.reshape(1, -1))
+    )(*operands)
+    lanes = ask.shape[1]
     asked = lax.all_to_all(
-        ask.reshape(gens, SUB, 2 * STATE), "gen", split_axis=0, concat_axis=0, tiled=True
-    ).reshape(slots, 2 * STATE)
-
-    length = prompt_len[0]
-    raw = pre_raw[0]
-    xconv, cum, cumt, dtt, prefix = pl.pallas_call(
+        ask.reshape(gens, SUB, lanes), "gen", split_axis=0, concat_axis=0, tiled=True
+    ).reshape(slots, lanes)
+
+    live = live_state.reshape(live_dev, width, STATE)
+    operands = (
+        length,
+        pre_raw[0].T,
+        decay[None],
+        dt_bias[None],
+        conv_weight,
+        conv_bias[None],
+        bct,
+        pre_x[0],
+    )
+    xconv, cum, cumt, dtt, prefix, tail, live_near, conv_near = pl.pallas_call(
         state_kernel,
         out_shape=(
             shape((span, width), BF16),
@@ -408,57 +453,32 @@
             shape((heads, span), F32),
             shape((heads, span), F32),
             shape((2 * STATE, width), BF16),
+            shape((SUB, width), BF16),
+            shape(live.shape, BF16),
+            shape(conv_rows.shape, BF16),
         ),
-        in_specs=[pl.BlockSpec(memory_space=pltpu.SMEM)] + [vmem()] * 10,
-        out_specs=(vmem(),) * 5,
-        scratch_shapes=[pltpu.VMEM((span + SUB, width), F32)],
+        in_specs=[hbm()] * (len(operands) + 2),
+        out_specs=(vmem(),) * 8,
+        scratch_shapes=staged(*operands)
+        + [dma((len(operands) + 2,)), pltpu.VMEM((span + SUB, width), F32)],
         compiler_params=params(),
-        cost_estimate=cost(2 * 10 * span * span * 64, 2 * span * width * 2, span * width * 2),
+        cost_estimate=cost(2 * 10 * span * span * 64, 6000000, span * width * 2),
         name="state",
-    )(
-        prompt_len,
-        pre_x[0],
-        pre_bc[0],
-        raw,
-        raw.T,
-        decay[None],
-        dt_bias[None],
-        decay[:, None],
-        dt_bias[:, None],
-        conv_weight.astype(F32),
-        conv_bias[None],
-    )
-    taps = conv_weight.shape[0]
-    spots = length - (taps - 1) + jnp.arange(taps - 1, dtype=jnp.int32)
-    tails = jnp.where(
-        (spots >= 0)[:, None], pre_x[0][jnp.maximum(spots, 0)], jnp.zeros((), BF16)
-    )
-    tail_a = jnp.concatenate([jnp.zeros((SUB - 1, width), BF16), tails[0:1]], 0)
-    tail_b = tails[1:].reshape(SUB, width // 4)
-    conv = jnp.pad(live_conv, ((0, 0), (steps, SUB - steps - (taps - 1)), (0, 0)))
-
-    block = 8
+    )(*operands, live, conv_rows)
+
     answer = pl.pallas_call(
         answer_kernel,
-        grid=(live_dev // block,),
-        out_shape=shape((slots, width + width // 2 + width // 4), BF16),
-        in_specs=[
-            pl.BlockSpec((slots, 2 * STATE), lambda i: (0, 0)),
-            pl.BlockSpec((block, width, STATE), lambda i: (i, 0, 0)),
-            pl.BlockSpec((block, SUB, width), lambda i: (i, 0, 0)),
-            pl.BlockSpec((2 * STATE, width), lambda i: (0, 0)),
-            pl.BlockSpec((SUB, width), lambda i: (0, 0)),
-            pl.BlockSpec((SUB, width // 4), lambda i: (0, 0)),
-        ],
-        out_specs=pl.BlockSpec((slots, width + width // 2 + width // 4), lambda i: (0, 0)),
+        out_shape=shape((slots, width + width // 2), BF16),
+        in_specs=[vmem()] * 5,
+        out_specs=vmem(),
         scratch_shapes=[
             pltpu.VMEM((live_dev * SUB, 2 * STATE), F32),
             pltpu.VMEM((live_dev * SUB, width), F32),
         ],
-        compiler_params=params(dimension_semantics=("arbitrary",)),
-        cost_estimate=cost(2 * slots * 512 * 1024, 6000000),
+        compiler_params=params(),
+        cost_estimate=cost(2 * slots * 512 * 1024, 2000000),
         name="answer",
-    )(asked, live_state.reshape(live_dev, width, STATE), conv, prefix, tail_a, tail_b)
+    )(asked, live_near, conv_near, prefix, tail)
     lanes = answer.shape[1]
     got = lax.all_to_all(
         answer.reshape(gens, SUB, lanes), "gen", split_axis=0, concat_axis=0, tiled=True
@@ -473,20 +493,21 @@
         compiler_params=params(),
         cost_estimate=cost(2 * heads * span * span * 128, 2500000, heads * span * span),
         name="prompt",
-    )(xconv, pre_z[0], pre_bc[0], cum, cumt, dtt, jnp.repeat(skip, width // heads)[None])
+    )(xconv, pre_z[0], bct, cum, cumt, dtt, jnp.repeat(skip, width // heads)[None])
 
     count = steps * rows
     padded = -(-(span + count) // 128) * 128
     step_gate, sums = pl.pallas_call(
         lambda *refs: decode_kernel(live_dev, readers, *refs),
         out_shape=(shape((count, width), F32), shape((mp, SUB, padded), F32)),
-        in_specs=[vmem()] * 12,
+        in_specs=[vmem()] * 13,
         out_specs=(vmem(), vmem()),
         compiler_params=params(),
         cost_estimate=cost(2 * 384 * 512 * 512, 2500000),
         name="decode",
     )(
         got,
+        asked,
         tgt_l.reshape(-1, 1),
         tgt_r.reshape(-1, 1),
         step_xz,

time: 123 us -> 118 us (0.959)
  local copies, waits for them, and re-layouts: 17.8 us -> 21.1 us
  starting transfers between devices: 34 us -> 30.9 us
  waiting for transfers between devices: 38.8 us -> 36.3 us
  other arithmetic: 2.13 us -> 0.02 us
    unnamed x49 -> x69, local copies, waits for them, and re-layouts: 13.2 us -> 20.8 us
    all_to_all x1, waiting for transfers between devices: 38.8 us -> 33.2 us  [per_device(): lax.all_to_all(answer.reshape(gens, SUB, lanes), 'gen', split_axis=0, con...]
    all_to_all x1, waiting for transfers between devices: 0.01 us -> 3.13 us  [per_device(): lax.all_to_all(ask.reshape(gens, SUB, lanes), 'gen', split_axis=0, concat...]
    all_to_all x1, starting transfers between devices: 14.7 us -> 11.6 us  [per_device(): lax.all_to_all(answer.reshape(gens, SUB, lanes), 'gen', split_axis=0, con...]
    gather x1 -> x0, local copies, waits for them, and re-layouts: 1.68 us -> none  [per_device(): pre_x[0][jnp.maximum(spots, 0)]]
    broadcast_in_dim x2 -> x0, local copies, waits for them, and re-layouts: 1.46 us -> none  [the longest x1 0.73 us: per_device(): decay[:, None]]
  transfers between devices with their start and end apart: 2 -> 2, of which waited for: 1 -> 2; matrix products, arithmetic and copies ran while one was open for 6% -> 0% of each run, Pallas kernels for 4% -> 5%
where the time goes in v2:
time: 118 us; the launch traced here: 117 us
  waiting for transfers between devices  36.3 us (31%)
  starting transfers between devices  30.9 us (26%)
  local copies, waits for them, and re-layouts  21.1 us (18%)
  blocking collectives  14.8 us (13%)
  Pallas kernels  12.5 us (11%)
  between operations  1.51 us (1%)
    all_to_all x1, waiting for transfers between devices, per_device(): lax.all_to_all(answer.reshape(gens, SUB, lanes), 'gen', split_axis=0, con...  33.2 us
    unnamed x69, local copies, waits for them, and re-layouts  20.8 us
    all_to_all x1, starting transfers between devices, per_device(): lax.all_to_all(ask.reshape(gens, SUB, lanes), 'gen', split_axis=0, concat...  19.3 us
    all_to_all x1, blocking collectives, per_device(): sums = lax.all_to_all(sums, 'mp', split_axis=0, concat_axis=0, tiled=True)  14.8 us
    all_to_all x1, starting transfers between devices, per_device(): lax.all_to_all(answer.reshape(gens, SUB, lanes), 'gen', split_axis=0, con...  11.6 us
    pallas_call x1, Pallas kernels, per_device(): pl.pallas_call(state_kernel, out_shape=(shape((span, width), BF16), shape...  3.43 us
    pallas_call x1, Pallas kernels, per_device(): pl.pallas_call(answer_kernel, out_shape=shape((slots, width + width // 2)...  3.2 us
    all_to_all x1, waiting for transfers between devices, per_device(): lax.all_to_all(ask.reshape(gens, SUB, lanes), 'gen', split_axis=0, concat...  3.13 us
  transfers between devices with their start and end apart: 2, of which 2 were waited for; matrix products, arithmetic and copies ran while one was open for 0% of the time, Pallas kernels for 5%

profile of v2, /device:TPU:1, one launch (start us, length us, event | category | flops | bytes accessed | tf_op | source)
XLA Modules:
  0.0 117.1 jit_solution(14943215291945937306)
XLA Ops:
  1.3 0.0 copy-start.3
  1.3 1.0 copy-done.3
  2.3 0.0 copy-start.6
  2.3 0.9 copy-done.6
  3.2 0.0 copy-start.22
  3.2 0.7 copy-done.22
  3.9 0.0 copy-start.24
  3.9 0.7 copy-done.24
  4.5 1.3 %ask.1 = bf16[512,256]{1,0:T(8,128)(2,1)} custom-call(bf16[4,2,48,64]{3,2,1,0:T(8,128)(2,1)S(1)} %copy-done.6, s32[1,32]{1,0:T(1,128)S(1)} %bitcast.48, s32[1,16]{1,0:T(1,128)S(1)} %bitcast.49, s32[1,1]{1,0:T(1,128)} %bitcast.27.refs_3_, bf16[512,512]{1,0:T(8,128)(2,1)S(1)} %bitcast.33), custom_call_target="tpu_custom_call" | custom-call | flops 50331648 | bytes 800000 | tf_op jit(solution)/shard_map/ask/pallas_call | solution.py:422
  5.8 19.3 %all-to-all-start = ((bf16[64,8,256]{2,1,0:T(8,128)(2,1)}), bf16[64,8,256]{2,1,0:T(8,128)(2,1)S(1)}, u32[]{:S(2)}, u32[]{:S(2)}) async-start(bf16[64,8,256]{2,1,0:T(8,128)(2,1)} %bitcast.4), calls=%async_computation | async-start | bytes 524288 | tf_op jit(solution)/shard_map/all_to_all | solution.py:433
  25.1 0.0 copy-start
  25.1 2.2 %copy-done = bf16[32,8,64,64]{3,2,1,0:T(8,128)(2,1)S(1)} copy-done((bf16[32,8,64,64]{3,2,1,0:T(8,128)(2,1)S(1)}, bf16[32,8,64,64]{3,2,1,0:T(8,128)(2,1)}, u32[]{:S(2)}) %copy-start) | copy-done | bytes 2097176
  27.3 0.0 copy-start.4
  27.3 1.0 copy-done.4
  28.3 0.0 copy-start.8
  28.3 0.9 copy-done.8
  29.2 0.0 copy-start.10
  29.2 0.9 copy-done.10
  30.1 0.0 copy-start.11
  30.1 0.7 copy-done.11
  30.8 0.7 copy-done.13
  31.5 0.7 copy-done.14
  32.2 0.7 copy-done.17
  32.9 0.7 copy-done.19
  33.5 3.4 %state.1 = (bf16[512,512]{1,0:T(8,128)(2,1)S(1)}, f32[512,8]{1,0:T(8,128)S(1)}, f32[8,512]{1,0:T(8,128)S(1)}, f32[8,512]{1,0:T(8,128)S(1)}, bf16[128,512]{1,0:T(...) custom-call(s32[1,1]{1,0:T(1,128)} %bitcast.28.refs_0_, ...), custom_call_target="tpu_custom_call" | custom-call | flops 335544320 | bytes 6000000 | tf_op jit(solution)/shard_map/state/pallas_call | solution.py:448
  37.0 0.0 copy-start.1
  37.0 2.0 %copy-done.1 = bf16[32,512,64]{2,1,0:T(8,128)(2,1)} copy-done((bf16[32,512,64]{2,1,0:T(8,128)(2,1)}, bf16[32,512,64]{2,1,0:T(8,128)(2,1)S(1)}, u32[]{:S(2)}) %copy-start.1) | copy-done | bytes 2097176
  38.9 0.8 copy-done.27
  39.7 0.7 copy-done.29
  40.4 0.6 copy-done.31
  41.0 3.1 %all-to-all-done = bf16[64,8,256]{2,1,0:T(8,128)(2,1)S(1)} async-done(((bf16[64,8,256]{2,1,0:T(8,128)(2,1)}), bf16[64,8,256]{2,1,0:T(8,128)(2,1)S(1)}, u32[]{:S(2)}, u32[]{:S(2)}) %all-to-all-start) | async-done | bytes 262176 | tf_op jit(solution)/shard_map/all_to_all | solution.py:433
  44.2 2.2 %copy-done.2 = bf16[32,512,64]{2,1,0:T(8,128)(2,1)S(1)} copy-done((bf16[32,512,64]{2,1,0:T(8,128)(2,1)S(1)}, bf16[32,512,64]{2,1,0:T(8,128)(2,1)}, u32[]{:S(2)}) %copy-start.2) | copy-done | bytes 2097176
  46.4 3.2 %answer.1 = bf16[512,768]{1,0:T(8,128)(2,1)} custom-call(bf16[512,256]{1,0:T(8,128)(2,1)S(1)} %bitcast.31, bf16[32,512,64]{2,1,0:T(8,128)(2,1)S(1)} %copy-done.2, bf16[96,512]{1,0:T(8,128)(2,1)S(1)} %get-tuple-element.17.conv_ref, bf16[128,512]{1,0:T(8,128)(2,1)S(1)} %get-tuple-element.18.prefix_ref, bf16[8,512]{1,0:T(8,128)(2,1)S(1)} %get-tuple-element.19.tail_ref), custom_call_target="tpu_custom_call" | custom-call | flops 536870912 | bytes 2000000 | tf_op jit(solution)/shard_map/answer/pallas_call | solution.py:469
  49.6 0.0 copy-start.18
  49.6 0.0 copy-start.20
  49.6 0.0 copy-start.16
  49.6 11.6 %all-to-all-start.1 = ((bf16[64,8,768]{2,1,0:T(8,128)(2,1)}), bf16[64,8,768]{2,1,0:T(8,128)(2,1)S(1)}, u32[]{:S(2)}, u32[]{:S(2)}) async-start(bf16[64,8,768]{2,1,0:T(8,128)(2,1)} %bitcast.16), calls=%async_computation.1 | async-start | bytes 1572864 | tf_op jit(solution)/shard_map/all_to_all | solution.py:483
  61.2 0.0 copy-done.21
  61.2 0.1 broadcast_in_dim.39
  61.3 0.1 broadcast_in_dim_reshape.3.skip_ref
  61.4 0.0 copy-done.23
  61.4 0.1 add.55.refs_2_
  61.6 0.0 copy-done.25
  61.6 0.1 add.56.refs_3_
  61.7 0.0 copy-done.33
  61.7 0.1 copy.22
  61.8 0.0 copy-done.9
  61.8 0.0 copy-done.26
  61.8 0.0 copy-start.28
  61.8 1.0 copy-done.28
  62.9 0.9 copy-done.30
  63.8 0.7 copy-done.32
  64.5 2.3 %prompt.1 = (f32[512,512]{1,0:T(8,128)S(1)}, f32[8,512]{1,0:T(8,128)S(1)}) custom-call(bf16[512,512]{1,0:T(8,128)(2,1)S(1)} %copy-done.28, bf16[512,512]{1,0:T(8,128)(2,1)S(1)} %bitcast.50, bf16[2,64,512]{2,1,0:T(8,128)(2,1)S(1)} %bitcast.37, f32[512,8]{1,0:T(8,128)S(1)} %copy-done.30, f32[8,512]{1,0:T(8,128)S(1)} %get-tuple-element.22.cumt_ref, ...), custom_call_target="tpu_custom_call" | custom-call | flops 536870912 | bytes 2500000 | tf_op jit(solution)/shard_map/prompt/pallas_call | solution.py:487
  66.9 33.2 %all-to-all-done.1 = bf16[64,8,768]{2,1,0:T(8,128)(2,1)S(1)} async-done(((bf16[64,8,768]{2,1,0:T(8,128)(2,1)}), bf16[64,8,768]{2,1,0:T(8,128)(2,1)S(1)}, u32[]{:S(2)}, u32[]{:S(2)}) %all-to-all-start.1) | async-done | bytes 786464 | tf_op jit(solution)/shard_map/all_to_all | solution.py:483
  100.0 0.0 copy-done.5
  100.0 0.0 copy-done.7
  100.0 0.0 copy-done.12
  100.0 0.0 copy-done.15
  100.0 0.0 copy-done.18
  100.0 0.0 copy-done.20
  100.1 1.2 %decode.1 = (f32[192,512]{1,0:T(8,128)S(1)}, f32[8,8,768]{2,1,0:T(8,128)S(1)}) custom-call(bf16[512,768]{1,0:T(8,128)(2,1)S(1)} %bitcast.30, bf16[512,256]{1,0:T(8,128)(2,1)S(1)} %bitcast.32, s32[256,1]{1,0:T(8,128)S(1)} %add.55.refs_2_, s32[128,1]{1,0:T(8,128)S(1)} %add.56.refs_3_, bf16[4,2,48,512]{3,2,1,0:T(8,128)(2,1)S(1)} %copy-done.5, ...), custom_call_target="tpu_custom_call" | custom-call | flops 201326592 | bytes 2500000 | tf_op jit(solution)/shard_map/decode/pallas_call | solution.py:500
  101.3 14.8 %all_to_all.15.refs_0_ = f32[8,8,768]{2,1,0:T(8,128)S(1)} all-to-all(f32[8,8,768]{2,1,0:T(8,128)S(1)} %get-tuple-element.25), channel_id=1, replica_groups=mesh['gen'=64,'mp'=8] {'mp'}, dimensions={0} | all-to-all | bytes 393216 | tf_op jit(solution)/shard_map/all_to_all | solution.py:523
  116.1 0.0 copy-done.16
  116.1 1.0 finish.1
  (24 shorter events, 0.1 us)
Async XLA Ops:
  1.3 1.0 copy-start.3
  2.3 0.9 copy-start.6
  3.2 0.7 copy-start.22
  3.9 0.7 copy-start.24
  5.8 38.4 %all-to-all-start = ((bf16[64,8,256]{2,1,0:T(8,128)(2,1)}), bf16[64,8,256]{2,1,0:T(8,128)(2,1)S(1)}, u32[]{:S(2)}, u32[]{:S(2)}) async-start(bf16[64,8,256]{2,1,0:T(8,128)(2,1)} %bitcast.4), calls=%async_computation | async-start | bytes 524288 | tf_op jit(solution)/shard_map/all_to_all | solution.py:433
  25.1 2.2 %copy-start = (bf16[32,8,64,64]{3,2,1,0:T(8,128)(2,1)S(1)}, bf16[32,8,64,64]{3,2,1,0:T(8,128)(2,1)}, u32[]{:S(2)}) copy-start(bf16[32,8,64,64]{3,2,1,0:T(8,128)(2,1)} %param.23) | copy-start | bytes 6291460
  27.3 1.0 copy-start.4
  28.3 0.9 copy-start.8
  29.2 0.9 copy-start.10
  30.1 0.7 copy-start.11
  30.8 0.7 copy-start.13
  31.5 0.7 copy-start.14
  32.2 0.7 copy-start.17
  32.9 0.7 copy-start.19
  33.5 28.2 %copy-start.33 = (bf16[4,48,8]{1,2,0:T(8,128)(2,1)S(1)}, bf16[4,48,8]{1,2,0:T(8,128)(2,1)}, u32[]{:S(2)}) copy-start(bf16[4,48,8]{1,2,0:T(8,128)(2,1)} %param.29) | copy-start | bytes 9220
  33.5 28.3 %copy-start.9 = (bf16[1,2,512,64]{2,3,1,0:T(8,128)(2,1)S(1)}, bf16[1,2,512,64]{2,3,1,0:T(8,128)(2,1)}, u32[]{:S(2)}) copy-start(bf16[1,2,512,64]{2,3,1,0:T(8,128)(2,1)} %param.20) | copy-start | bytes 393220
  33.5 28.3 %copy-start.26 = (bf16[1,512,512]{2,1,0:T(8,128)(2,1)S(1)}, bf16[1,512,512]{2,1,0:T(8,128)(2,1)}, u32[]{:S(2)}) copy-start(bf16[1,512,512]{2,1,0:T(8,128)(2,1)} %param.19) | copy-start | bytes 1572868
  37.0 2.0 %copy-start.1 = (bf16[32,512,64]{2,1,0:T(8,128)(2,1)}, bf16[32,512,64]{2,1,0:T(8,128)(2,1)S(1)}, u32[]{:S(2)}) copy-start(bf16[32,512,64]{2,1,0:T(8,128)(2,1)S(1)} %get-tuple-element.16.state_ref) | copy-start | bytes 6291460
  38.9 0.8 copy-start.27
  39.7 0.7 copy-start.29
  40.4 0.6 copy-start.31
  41.0 20.2 %copy-start.21 = (f32[8]{0:T(128)S(1)}, f32[8]{0:T(128)}, u32[]{:S(2)}) copy-start(f32[8]{0:T(128)} %param.34) | copy-start | bytes 100
  41.0 20.4 %copy-start.23 = (s32[32]{0:T(128)S(1)}, s32[32]{0:T(128)}, u32[]{:S(2)}) copy-start(s32[32]{0:T(128)} %param.25) | copy-start | bytes 388
  41.0 20.5 %copy-start.25 = (s32[16]{0:T(128)S(1)}, s32[16]{0:T(128)}, u32[]{:S(2)}) copy-start(s32[16]{0:T(128)} %param.26) | copy-start | bytes 196
  44.2 2.2 %copy-start.2 = (bf16[32,512,64]{2,1,0:T(8,128)(2,1)S(1)}, bf16[32,512,64]{2,1,0:T(8,128)(2,1)}, u32[]{:S(2)}) copy-start(bf16[32,512,64]{2,1,0:T(8,128)(2,1)} %copy-done.1) | copy-start | bytes 6291460
  49.6 50.5 %copy-start.5 = (bf16[4,2,48,512]{3,2,1,0:T(8,128)(2,1)S(1)}, bf16[4,2,48,512]{3,2,1,0:T(8,128)(2,1)}, u32[]{:S(2)}) copy-start(bf16[4,2,48,512]{3,2,1,0:T(8,128)(2,1)} %refs_4_.3) | copy-start | bytes 1179652
  49.6 50.5 %copy-start.7 = (bf16[4,2,48,64]{3,2,1,0:T(8,128)(2,1)S(1)}, bf16[4,2,48,64]{3,2,1,0:T(8,128)(2,1)}, u32[]{:S(2)}) copy-start(bf16[4,2,48,64]{3,2,1,0:T(8,128)(2,1)} %refs_5_.1) | copy-start | bytes 147460
  49.6 50.5 %copy-start.12 = (bf16[4,512]{1,0:T(4,128)(2,1)S(1)}, bf16[4,512]{1,0:T(4,128)(2,1)}, u32[]{:S(2)}) copy-start(bf16[4,512]{1,0:T(4,128)(2,1)} %refs_10_.1) | copy-start | bytes 12292
  49.6 50.5 %copy-start.15 = (f32[512]{0:T(512)S(1)}, f32[512]{0:T(512)}, u32[]{:S(2)}) copy-start(f32[512]{0:T(512)} %param.33) | copy-start | bytes 6148
  49.6 50.5 %copy-start.18 = (f32[8]{0:T(128)S(1)}, f32[8]{0:T(128)}, u32[]{:S(2)}) copy-start(f32[8]{0:T(128)} %param.30) | copy-start | bytes 100
  49.6 50.5 %copy-start.20 = (f32[8]{0:T(128)S(1)}, f32[8]{0:T(128)}, u32[]{:S(2)}) copy-start(f32[8]{0:T(128)} %param.31) | copy-start | bytes 100
  49.6 66.5 %copy-start.16 = (f32[512]{0:T(512)S(1)}, f32[512]{0:T(512)}, u32[]{:S(2)}) copy-start(f32[512]{0:T(512)} %param.35) | copy-start | bytes 6148
  49.6 50.4 %all-to-all-start.1 = ((bf16[64,8,768]{2,1,0:T(8,128)(2,1)}), bf16[64,8,768]{2,1,0:T(8,128)(2,1)S(1)}, u32[]{:S(2)}, u32[]{:S(2)}) async-start(bf16[64,8,768]{2,1,0:T(8,128)(2,1)} %bitcast.16), calls=%async_computation.1 | async-start | bytes 1572864 | tf_op jit(solution)/shard_map/all_to_all | solution.py:483
  61.8 1.0 copy-start.28
  62.9 0.9 copy-start.30
  63.8 0.7 copy-start.32

commit v3 on v2

--- a/solution.py
+++ b/solution.py
@@ -8,6 +8,9 @@
 STATE = 64
 EPS = 1e-05
 SUB = 8
+RING = 16
+CHUNKS = 4
+WHOLE = 60 * 1024 * 1024
 F32 = jnp.float32
 BF16 = jnp.bfloat16
 NT = (((1,), (1,)), ((), ()))
@@ -69,7 +72,7 @@
     return copies
 
 
-def ask_kernel(*refs):
+def ask_kernel(ring, *refs):
     sources, out_ref, targets, sems = refs[:5], refs[5], refs[6:11], refs[11]
     for copy in fetch(sources, targets, sems):
         copy.wait()
@@ -91,8 +94,12 @@
     ]
     data_r = jnp.concatenate(parts, 0)
     data_r = jnp.concatenate([jnp.zeros_like(data_r), data_r], 1).astype(BF16)
-    first_l = lax.div(source_ref[...], live_dev) * SUB
-    first_r = reader_ref[...] * SUB
+
+    def slot(gen):
+        return (lax.rem(gen, ring) * (slots // SUB // ring) + lax.div(gen, ring)) * SUB
+
+    first_l = slot(lax.div(source_ref[...], live_dev))
+    first_r = slot(reader_ref[...])
     tgt_l = jnp.concatenate([first_l + r for r in range(SUB)], 1)
     tgt_r = jnp.concatenate([first_r + r for r in range(SUB)], 1)
     pick_l = onehot(iota((slots, SUB * live_dev), 0) == tgt_l)
@@ -112,11 +119,10 @@
 
 
 def state_kernel(*refs):
-    sources, outs, targets = refs[:10], refs[10:18], refs[18:26]
-    sems, xf = refs[26], refs[27]
-    xc_ref, cum_ref, cumt_ref, dtt_ref, st_ref, tail_ref, live_ref, conv_ref = outs
-    copies = fetch(sources, targets + (live_ref, conv_ref), sems)
-    for copy in copies[:8]:
+    sources, outs, targets = refs[:8], refs[8:14], refs[14:22]
+    sems, xf = refs[22], refs[23]
+    xc_ref, cum_ref, cumt_ref, dtt_ref, st_ref, tail_ref = outs
+    for copy in fetch(sources, targets, sems):
         copy.wait()
     len_ref, rawt_ref, decay_ref, bias_ref, cw_ref, cb_ref, bct_ref, x_ref = targets
     span, width = x_ref.shape
@@ -163,8 +169,6 @@
     row, col = iota((SUB, span), 0), iota((SUB, span), 1)
     tail = onehot((col == length - (taps - 1)) & (row == SUB - 1))
     tail_ref[...] = mm(tail, x_ref[...]).astype(BF16)
-    for copy in copies[8:]:
-        copy.wait()
 
 
 def prompt_kernel(
@@ -205,7 +209,19 @@
         ss_ref[:, start:stop] = mm_nt(ones, hi) + mm_nt(ones, lo)
 
 
-def answer_kernel(ask_ref, state_ref, conv_ref, prefix_ref, tail_ref, out_ref, cs, ys):
+def answer_kernel(*refs):
+    sources, live_hbm, out_ref, targets = refs[:4], refs[4], refs[5], refs[6:10]
+    state_ref, sems, cs, ys = refs[10:]
+    chunk = state_ref.shape[0] // CHUNKS
+    chunks = [slice(i * chunk, (i + 1) * chunk) for i in range(CHUNKS)]
+    copies = fetch(
+        sources + tuple(live_hbm.at[part] for part in chunks),
+        targets + tuple(state_ref.at[part] for part in chunks),
+        sems,
+    )
+    for copy in copies[:4]:
+        copy.wait()
+    ask_ref, conv_ref, prefix_ref, tail_ref = targets
     slots = ask_ref.shape[0]
     live_dev = state_ref.shape[0]
     count = ys.shape[0]
@@ -221,6 +237,8 @@
     got = mm(back, ask)
     cs[...] = jnp.where(iota(got.shape, 0) % SUB < 4, got, 0.0)
     for k in range(live_dev):
+        if k % chunk == 0:
+            copies[4 + k // chunk].wait()
         rows = slice(k * SUB, (k + 1) * SUB)
         ys[rows, :] = mm_nt(cs[rows, 0:STATE].astype(BF16), state_ref[k])
     place = place[:, 0:1].astype(jnp.int32)
@@ -324,24 +342,25 @@
     hi, lo = split2(square)
     ones = jnp.ones((SUB, width), BF16)
     sums = mm_nt(ones, hi) + mm_nt(ones, lo)
-    pad = ss_ref.shape[2] - span - sums.shape[1]
-    sums = jnp.concatenate([sums, jnp.zeros((SUB, pad), F32)], 1)
-    for i in range(ss_ref.shape[0]):
-        ss_ref[i, :, 0:span] = pre_ss_ref[...]
-        ss_ref[i, :, span:] = sums
+    lanes = ss_ref.shape[2]
+    pad = -sums.shape[1] % lanes
+    sums = jnp.concatenate([pre_ss_ref[...], sums, jnp.zeros((SUB, pad), F32)], 1)
+    parts = [sums[0:1, i : i + lanes] for i in range(0, sums.shape[1], lanes)]
+    parts += [jnp.zeros((SUB - len(parts), lanes), F32)]
+    ss_ref[...] = jnp.broadcast_to(jnp.concatenate(parts, 0)[None], ss_ref.shape)
 
 
 def finish_kernel(width_all, ss_ref, pre_ref, step_ref, gain_ref, pre_out_ref, step_out_ref):
     total = ss_ref[0]
     for i in range(1, ss_ref.shape[0]):
         total = total + ss_ref[i]
-    scale = lax.rsqrt(total[0:1, :] / width_all + EPS)
+    scale = lax.rsqrt(total / width_all + EPS)
     gain = gain_ref[...]
     span = pre_ref.shape[0]
     block = 128
 
     def column(first, rows):
-        row = jnp.broadcast_to(scale[:, first : first + block], (rows, block))
+        row = scale[first // block : first // block + 1, :]
         diag = iota((rows, block), 0) == iota((rows, block), 1)
         return jnp.sum(jnp.where(diag, row, 0.0), axis=1, keepdims=True)
 
@@ -357,8 +376,8 @@
         )
 
 
-def params(**more):
-    return pltpu.CompilerParams(vmem_limit_bytes=24 * 1024 * 1024, **more)
+def params(limit=24 * 1024 * 1024, **more):
+    return pltpu.CompilerParams(vmem_limit_bytes=limit, **more)
 
 
 def cost(flops, moved, special=0):
@@ -420,18 +439,25 @@
 
     operands = (step_bc, source[None], reader[None], length, pre_x[0])
     ask = pl.pallas_call(
-        ask_kernel,
+        lambda *refs: ask_kernel(RING, *refs),
         out_shape=shape((slots, 2 * STATE + width // 4), BF16),
         in_specs=[hbm()] * len(operands),
         out_specs=vmem(),
         scratch_shapes=staged(*operands) + [dma((len(operands),))],
-        compiler_params=params(),
+        compiler_params=params(WHOLE),
         cost_estimate=cost(2 * slots * 384 * 128, 800000),
         name="ask",
     )(*operands)
     lanes = ask.shape[1]
+    outer = gens // RING
+    along_z = [[y * RING + z for z in range(RING)] for y in range(outer)]
+    along_y = [[y * RING + z for y in range(outer)] for z in range(RING)]
     asked = lax.all_to_all(
-        ask.reshape(gens, SUB, lanes), "gen", split_axis=0, concat_axis=0, tiled=True
+        ask.reshape(gens, SUB, lanes), "gen", 0, 0, axis_index_groups=along_z, tiled=True
+    )
+    asked = jnp.swapaxes(asked.reshape(RING, outer, SUB, lanes), 0, 1)
+    asked = lax.all_to_all(
+        asked.reshape(gens, SUB, lanes), "gen", 0, 0, axis_index_groups=along_y, tiled=True
     ).reshape(slots, lanes)
 
     live = live_state.reshape(live_dev, width, STATE)
@@ -445,7 +471,7 @@
         bct,
         pre_x[0],
     )
-    xconv, cum, cumt, dtt, prefix, tail, live_near, conv_near = pl.pallas_call(
+    xconv, cum, cumt, dtt, prefix, tail = pl.pallas_call(
         state_kernel,
         out_shape=(
             shape((span, width), BF16),
@@ -454,31 +480,32 @@
             shape((heads, span), F32),
             shape((2 * STATE, width), BF16),
             shape((SUB, width), BF16),
-            shape(live.shape, BF16),
-            shape(conv_rows.shape, BF16),
         ),
-        in_specs=[hbm()] * (len(operands) + 2),
-        out_specs=(vmem(),) * 8,
+        in_specs=[hbm()] * len(operands),
+        out_specs=(vmem(),) * 6,
         scratch_shapes=staged(*operands)
-        + [dma((len(operands) + 2,)), pltpu.VMEM((span + SUB, width), F32)],
-        compiler_params=params(),
-        cost_estimate=cost(2 * 10 * span * span * 64, 6000000, span * width * 2),
+        + [dma((len(operands),)), pltpu.VMEM((span + SUB, width), F32)],
+        compiler_params=params(WHOLE),
+        cost_estimate=cost(2 * 10 * span * span * 64, 2000000, span * width * 2),
         name="state",
-    )(*operands, live, conv_rows)
-
+    )(*operands)
+
+    operands = (asked, conv_rows, prefix, tail)
     answer = pl.pallas_call(
         answer_kernel,
         out_shape=shape((slots, width + width // 2), BF16),
-        in_specs=[vmem()] * 5,
+        in_specs=[hbm()] * (len(operands) + 1),
         out_specs=vmem(),
-        scratch_shapes=[
+        scratch_shapes=staged(*operands, live)
+        + [
+            dma((len(operands) + CHUNKS,)),
             pltpu.VMEM((live_dev * SUB, 2 * STATE), F32),
             pltpu.VMEM((live_dev * SUB, width), F32),
         ],
-        compiler_params=params(),
-        cost_estimate=cost(2 * slots * 512 * 1024, 2000000),
+        compiler_params=params(WHOLE),
+        cost_estimate=cost(2 * slots * 512 * 1024, 6000000),
         name="answer",
-    )(asked, live_near, conv_near, prefix, tail)
+    )(*operands, live)
     lanes = answer.shape[1]
     got = lax.all_to_all(
         answer.reshape(gens, SUB, lanes), "gen", split_axis=0, concat_axis=0, tiled=True
@@ -496,10 +523,9 @@
     )(xconv, pre_z[0], bct, cum, cumt, dtt, jnp.repeat(skip, width // heads)[None])
 
     count = steps * rows
-    padded = -(-(span + count) // 128) * 128
     step_gate, sums = pl.pallas_call(
         lambda *refs: decode_kernel(live_dev, readers, *refs),
-        out_shape=(shape((count, width), F32), shape((mp, SUB, padded), F32)),
+        out_shape=(shape((count, width), F32), shape((mp, SUB, 128), F32)),
         in_specs=[vmem()] * 13,
         out_specs=(vmem(), vmem()),
         compiler_params=params(),

time: 118 us -> 118 us (level)
  blocking collectives: 14.8 us -> 42.6 us
  local copies, waits for them, and re-layouts: 21.1 us -> 4.68 us
  starting transfers between devices: 30.9 us -> 18.1 us
  Pallas kernels: 12.5 us -> 16.4 us
  waiting for transfers between devices: 36.3 us -> 33.8 us
    all_to_all x0 -> x1, blocking collectives: none -> 28.9 us  [per_device(): lax.all_to_all(ask.reshape(gens, SUB, lanes), 'gen', 0, 0, axis_index_gro...]
    unnamed x69 -> x39, local copies, waits for them, and re-layouts: 20.8 us -> 3.6 us
    all_to_all x1, starting transfers between devices: 19.3 us -> 4.18 us  [per_device(): lax.all_to_all(asked.reshape(gens, SUB, lanes), 'gen', 0, 0, axis_index_g...]
    all_to_all x1, waiting for transfers between devices: 3.13 us -> 0.73 us  [per_device(): lax.all_to_all(asked.reshape(gens, SUB, lanes), 'gen', 0, 0, axis_index_g...]
    all_to_all x1, starting transfers between devices: 11.6 us -> 13.9 us  [per_device(): lax.all_to_all(answer.reshape(gens, SUB, lanes), 'gen', split_axis=0, con...]
    pallas_call x1, Pallas kernels: 3.2 us -> 4.75 us  [per_device(): pl.pallas_call(answer_kernel, out_shape=shape((slots, width + width // 2)...]
    pallas_call x1, Pallas kernels: 3.43 us -> 4.73 us  [per_device(): pl.pallas_call(state_kernel, out_shape=(shape((span, width), BF16), shape...]
  transfers between devices with their start and end apart: 2 -> 2, of which waited for: 2 -> 2; matrix products, arithmetic and copies ran while one was open for 0% -> 0% of each run, Pallas kernels for 5% -> 6%
where the time goes in v3:
time: 118 us; the launch traced here: 117 us
  blocking collectives  42.6 us (36%)
  waiting for transfers between devices  33.8 us (29%)
  starting transfers between devices  18.1 us (15%)
  Pallas kernels  16.4 us (14%)
  local copies, waits for them, and re-layouts  4.68 us (4%)
  between operations  1.55 us (1%)
    all_to_all x1, waiting for transfers between devices, per_device(): lax.all_to_all(answer.reshape(gens, SUB, lanes), 'gen', split_axis=0, con...  33.1 us
    all_to_all x1, blocking collectives, per_device(): lax.all_to_all(ask.reshape(gens, SUB, lanes), 'gen', 0, 0, axis_index_gro...  28.9 us
    all_to_all x1, starting transfers between devices, per_device(): lax.all_to_all(answer.reshape(gens, SUB, lanes), 'gen', split_axis=0, con...  13.9 us
    all_to_all x1, blocking collectives, per_device(): sums = lax.all_to_all(sums, 'mp', split_axis=0, concat_axis=0, tiled=True)  13.7 us
    pallas_call x1, Pallas kernels, per_device(): pl.pallas_call(answer_kernel, out_shape=shape((slots, width + width // 2)...  4.75 us
    pallas_call x1, Pallas kernels, per_device(): pl.pallas_call(state_kernel, out_shape=(shape((span, width), BF16), shape...  4.73 us
    all_to_all x1, starting transfers between devices, per_device(): lax.all_to_all(asked.reshape(gens, SUB, lanes), 'gen', 0, 0, axis_index_g...  4.18 us
    unnamed x39, local copies, waits for them, and re-layouts  3.6 us
  transfers between devices with their start and end apart: 2, of which 2 were waited for; matrix products, arithmetic and copies ran while one was open for 0% of the time, Pallas kernels for 6%

profile of v3, /device:TPU:1, one launch (start us, length us, event | category | flops | bytes accessed | tf_op | source)
XLA Modules:
  0.0 117.1 jit_solution(8463256170586624645)
XLA Ops:
  1.3 2.3 %ask.1 = bf16[512,256]{1,0:T(8,128)(2,1)} custom-call(bf16[4,2,48,64]{3,2,1,0:T(8,128)(2,1)} %refs_5_.1, s32[1,32]{1,0:T(1,128)} %bitcast.55, s32[1,16]{1,0:T(1,128)} %bitcast.56, s32[1,1]{1,0:T(1,128)} %bitcast.31.refs_3_, bf16[512,512]{1,0:T(8,128)(2,1)} %bitcast.52), custom_call_target="tpu_custom_call" | custom-call | flops 50331648 | bytes 800000 | tf_op jit(solution)/shard_map/ask/pallas_call | solution.py:441
  3.6 28.9 %all_to_all.20 = bf16[64,8,256]{2,1,0:T(8,128)(2,1)S(1)} all-to-all(bf16[64,8,256]{2,1,0:T(8,128)(2,1)} %bitcast.51), channel_id=1, replica_groups={{0,8,16,24,32,40,48,56,64,72,80,88,96,104,112,120},{128,136,144,152,160..., dimensions={0} | all-to-all | bytes 524288 | tf_op jit(solution)/shard_map/all_to_all | solution.py:455
  32.5 0.7 copy.23
  33.2 4.2 %all-to-all-start.1 = ((bf16[64,8,256]{2,1,0:T(8,128)(2,1)}), bf16[64,8,256]{2,1,0:T(8,128)(2,1)S(1)}, u32[]{:S(2)}, u32[]{:S(2)}) async-start(bf16[64,8,256]{2,1,0:T(8,128)(2,1)} %bitcast.7), calls=%async_computation.1 | async-start | bytes 524288 | tf_op jit(solution)/shard_map/all_to_all | solution.py:459
  37.4 0.0 copy-start.7
  37.4 0.0 copy-start.17
  37.4 0.0 copy-start.18
  37.4 0.0 copy-start.16
  37.4 0.0 copy-start.10
  37.4 0.0 copy-start.11
  37.4 4.7 %state.1 = (bf16[512,512]{1,0:T(8,128)(2,1)}, f32[512,8]{1,0:T(8,128)}, f32[8,512]{1,0:T(8,128)}, f32[8,512]{1,0:T(8,128)}, bf16[128,512]{1,0:T(8,128)(2,1)}, /*index=5*/bf16[8,512]{1,0:T(8,128)(2,1)}) custom-call(s32[1,1]{1,0:T(1,128)} %bitcast.32.refs_0_, bf16[8,512]{1,0:T(8,128)(2,1)} %bitcast.59, f32[1,8]{1,0:T(1,128)} %bitcast.41, f32[1,8]{1,0:T(1,128)} %bitcast.43, ...), custom_call_target="tpu_custom_call" | custom-call | flops 335544320 | bytes 2000000 | tf_op jit(solution)/shard_map/state/pallas_call | solution.py:474
  42.1 0.0 copy-start.14
  42.2 0.7 all-to-all-done.1
  42.9 0.0 copy-start
  42.9 0.7 copy-done
  43.6 4.7 %answer.1 = bf16[512,768]{1,0:T(8,128)(2,1)} custom-call(bf16[512,256]{1,0:T(8,128)(2,1)} %bitcast.34, bf16[96,512]{1,0:T(8,128)(2,1)} %bitcast.54, bf16[128,512]{1,0:T(8,128)(2,1)} %get-tuple-element.14.refs_2_, bf16[8,512]{1,0:T(8,128)(2,1)} %get-tuple-element.15.refs_3_, bf16[32,512,64]{2,1,0:T(8,128)(2,1)} %bitcast.48), custom_call_target="tpu_custom_call" | custom-call | flops 536870912 | bytes 6000000 | tf_op jit(solution)/shard_map/answer/pallas_call | solution.py:494
  48.4 0.0 copy-start.1
  48.4 0.0 copy-start.2
  48.4 0.0 copy-start.3
  48.4 0.0 copy-start.4
  48.4 0.0 copy-start.5
  48.4 0.0 copy-start.8
  48.4 0.0 copy-start.9
  48.4 0.0 copy-start.6
  48.4 13.9 %all-to-all-start.2 = ((bf16[64,8,768]{2,1,0:T(8,128)(2,1)}), bf16[64,8,768]{2,1,0:T(8,128)(2,1)S(1)}, u32[]{:S(2)}, u32[]{:S(2)}) async-start(bf16[64,8,768]{2,1,0:T(8,128)(2,1)} %bitcast.49), calls=%async_computation.2 | async-start | bytes 1572864 | tf_op jit(solution)/shard_map/all_to_all | solution.py:510
  62.4 0.0 copy-done.7
  62.4 0.1 broadcast_in_dim.39
  62.5 0.1 broadcast_in_dim_reshape.3.skip_ref
  62.6 0.0 copy-done.17
  62.6 0.1 add.55.refs_2_
  62.7 0.0 copy-done.18
  62.8 0.1 add.56.refs_3_
  62.8 0.0 copy-done.16
  62.9 0.1 copy.24
  63.0 0.0 copy-done.10
  63.0 0.0 copy-done.11
  63.0 0.0 copy-done.14
  63.0 0.0 copy-start.12
  63.0 1.0 copy-done.12
  64.0 0.0 copy-start.13
  64.0 0.9 copy-done.13
  65.0 0.0 copy-start.15
  65.0 0.7 copy-done.15
  65.7 2.3 %prompt.1 = (f32[512,512]{1,0:T(8,128)S(1)}, f32[8,512]{1,0:T(8,128)S(1)}) custom-call(bf16[512,512]{1,0:T(8,128)(2,1)S(1)} %copy-done.12, bf16[512,512]{1,0:T(8,128)(2,1)S(1)} %bitcast.45, bf16[2,64,512]{2,1,0:T(8,128)(2,1)S(1)} %bitcast.47, f32[512,8]{1,0:T(8,128)S(1)} %copy-done.13, f32[8,512]{1,0:T(8,128)S(1)} %copy-done.14, f32[8,512]{1,0:T(8,128)S(1)} %copy-done.15, ...), custom_call_target="tpu_custom_call" | custom-call | flops 536870912 | bytes 2500000 | tf_op jit(solution)/shard_map/prompt/pallas_call | solution.py:514
  68.0 33.1 %all-to-all-done.2 = bf16[64,8,768]{2,1,0:T(8,128)(2,1)S(1)} async-done(((bf16[64,8,768]{2,1,0:T(8,128)(2,1)}), bf16[64,8,768]{2,1,0:T(8,128)(2,1)S(1)}, u32[]{:S(2)}, u32[]{:S(2)}) %all-to-all-start.2) | async-done | bytes 786464 | tf_op jit(solution)/shard_map/all_to_all | solution.py:510
  101.1 0.0 copy-done.1
  101.1 0.0 copy-done.2
  101.1 0.0 copy-done.3
  101.1 0.0 copy-done.4
  101.1 0.0 copy-done.5
  101.1 0.0 copy-done.8
  101.2 0.0 copy-done.9
  101.2 1.3 %decode.1 = (f32[192,512]{1,0:T(8,128)S(1)}, f32[8,8,128]{2,1,0:T(8,128)S(1)}) custom-call(bf16[512,768]{1,0:T(8,128)(2,1)S(1)} %bitcast.33, bf16[512,256]{1,0:T(8,128)(2,1)S(1)} %bitcast.35, s32[256,1]{1,0:T(8,128)S(1)} %add.55.refs_2_, s32[128,1]{1,0:T(8,128)S(1)} %add.56.refs_3_, bf16[4,2,48,512]{3,2,1,0:T(8,128)(2,1)S(1)} %copy-done.2, ...), custom_call_target="tpu_custom_call" | custom-call | flops 201326592 | bytes 2500000 | tf_op jit(solution)/shard_map/decode/pallas_call | solution.py:526
  102.4 13.7 %all_to_all.21.refs_0_ = f32[8,8,128]{2,1,0:T(8,128)S(1)} all-to-all(f32[8,8,128]{2,1,0:T(8,128)S(1)} %get-tuple-element.21), channel_id=1, replica_groups=mesh['gen'=64,'mp'=8] {'mp'}, dimensions={0} | all-to-all | bytes 65536 | tf_op jit(solution)/shard_map/all_to_all | solution.py:549
  116.1 0.0 copy-done.6
  116.1 1.0 finish.1
  (4 shorter events, 0.0 us)
Async XLA Ops:
  33.2 9.7 %all-to-all-start.1 = ((bf16[64,8,256]{2,1,0:T(8,128)(2,1)}), bf16[64,8,256]{2,1,0:T(8,128)(2,1)S(1)}, u32[]{:S(2)}, u32[]{:S(2)}) async-start(bf16[64,8,256]{2,1,0:T(8,128)(2,1)} %bitcast.7), calls=%async_computation.1 | async-start | bytes 524288 | tf_op jit(solution)/shard_map/all_to_all | solution.py:459
  37.4 25.0 %copy-start.7 = (f32[8]{0:T(128)S(1)}, f32[8]{0:T(128)}, u32[]{:S(2)}) copy-start(f32[8]{0:T(128)} %param.34) | copy-start | bytes 100
  37.4 25.2 %copy-start.17 = (s32[32]{0:T(128)S(1)}, s32[32]{0:T(128)}, u32[]{:S(2)}) copy-start(s32[32]{0:T(128)} %param.25) | copy-start | bytes 388
  37.4 25.4 %copy-start.18 = (s32[16]{0:T(128)S(1)}, s32[16]{0:T(128)}, u32[]{:S(2)}) copy-start(s32[16]{0:T(128)} %param.26) | copy-start | bytes 196
  37.4 25.5 %copy-start.16 = (bf16[4,48,8]{1,2,0:T(8,128)(2,1)S(1)}, bf16[4,48,8]{1,2,0:T(8,128)(2,1)}, u32[]{:S(2)}) copy-start(bf16[4,48,8]{1,2,0:T(8,128)(2,1)} %param.29) | copy-start | bytes 9220
  37.4 25.6 %copy-start.10 = (bf16[1,512,512]{2,1,0:T(8,128)(2,1)S(1)}, bf16[1,512,512]{2,1,0:T(8,128)(2,1)}, u32[]{:S(2)}) copy-start(bf16[1,512,512]{2,1,0:T(8,128)(2,1)} %param.19) | copy-start | bytes 1572868
  37.4 25.6 %copy-start.11 = (bf16[1,2,512,64]{2,3,1,0:T(8,128)(2,1)S(1)}, bf16[1,2,512,64]{2,3,1,0:T(8,128)(2,1)}, u32[]{:S(2)}) copy-start(bf16[1,2,512,64]{2,3,1,0:T(8,128)(2,1)} %param.20) | copy-start | bytes 393220
  42.1 20.8 %copy-start.14 = (f32[8,512]{1,0:T(8,128)S(1)}, f32[8,512]{1,0:T(8,128)}, u32[]{:S(2)}) copy-start(f32[8,512]{1,0:T(8,128)} %get-tuple-element.18.cumt_ref) | copy-start | bytes 49156
  42.9 0.7 copy-start
  48.4 52.8 %copy-start.1 = (bf16[64,8,256]{2,1,0:T(8,128)(2,1)S(1)}, bf16[64,8,256]{2,1,0:T(8,128)(2,1)}, u32[]{:S(2)}) copy-start(bf16[64,8,256]{2,1,0:T(8,128)(2,1)} %copy-done) | copy-start | bytes 786436
  48.4 52.8 %copy-start.2 = (bf16[4,2,48,512]{3,2,1,0:T(8,128)(2,1)S(1)}, bf16[4,2,48,512]{3,2,1,0:T(8,128)(2,1)}, u32[]{:S(2)}) copy-start(bf16[4,2,48,512]{3,2,1,0:T(8,128)(2,1)} %refs_4_.3) | copy-start | bytes 1179652
  48.4 52.7 %copy-start.3 = (bf16[4,2,48,64]{3,2,1,0:T(8,128)(2,1)S(1)}, bf16[4,2,48,64]{3,2,1,0:T(8,128)(2,1)}, u32[]{:S(2)}) copy-start(bf16[4,2,48,64]{3,2,1,0:T(8,128)(2,1)} %refs_5_.1) | copy-start | bytes 147460
  48.4 52.7 %copy-start.4 = (bf16[4,512]{1,0:T(4,128)(2,1)S(1)}, bf16[4,512]{1,0:T(4,128)(2,1)}, u32[]{:S(2)}) copy-start(bf16[4,512]{1,0:T(4,128)(2,1)} %refs_10_.1) | copy-start | bytes 12292
  48.4 52.7 %copy-start.5 = (f32[512]{0:T(512)S(1)}, f32[512]{0:T(512)}, u32[]{:S(2)}) copy-start(f32[512]{0:T(512)} %param.33) | copy-start | bytes 6148
  48.4 52.7 %copy-start.8 = (f32[8]{0:T(128)S(1)}, f32[8]{0:T(128)}, u32[]{:S(2)}) copy-start(f32[8]{0:T(128)} %param.30) | copy-start | bytes 100
  48.4 52.7 %copy-start.9 = (f32[8]{0:T(128)S(1)}, f32[8]{0:T(128)}, u32[]{:S(2)}) copy-start(f32[8]{0:T(128)} %param.31) | copy-start | bytes 100
  48.4 67.7 %copy-start.6 = (f32[512]{0:T(512)S(1)}, f32[512]{0:T(512)}, u32[]{:S(2)}) copy-start(f32[512]{0:T(512)} %param.35) | copy-start | bytes 6148
  48.4 52.7 %all-to-all-start.2 = ((bf16[64,8,768]{2,1,0:T(8,128)(2,1)}), bf16[64,8,768]{2,1,0:T(8,128)(2,1)S(1)}, u32[]{:S(2)}, u32[]{:S(2)}) async-start(bf16[64,8,768]{2,1,0:T(8,128)(2,1)} %bitcast.49), calls=%async_computation.2 | async-start | bytes 1572864 | tf_op jit(solution)/shard_map/all_to_all | solution.py:510
  63.0 1.0 copy-start.12
  64.0 0.9 copy-start.13
  65.0 0.7 copy-start.15

commit v4 on v3

--- a/solution.py
+++ b/solution.py
@@ -8,7 +8,6 @@
 STATE = 64
 EPS = 1e-05
 SUB = 8
-RING = 16
 CHUNKS = 4
 WHOLE = 60 * 1024 * 1024
 F32 = jnp.float32
@@ -72,7 +71,7 @@
     return copies
 
 
-def ask_kernel(ring, *refs):
+def ask_kernel(*refs):
     sources, out_ref, targets, sems = refs[:5], refs[5], refs[6:11], refs[11]
     for copy in fetch(sources, targets, sems):
         copy.wait()
@@ -94,12 +93,8 @@
     ]
     data_r = jnp.concatenate(parts, 0)
     data_r = jnp.concatenate([jnp.zeros_like(data_r), data_r], 1).astype(BF16)
-
-    def slot(gen):
-        return (lax.rem(gen, ring) * (slots // SUB // ring) + lax.div(gen, ring)) * SUB
-
-    first_l = slot(lax.div(source_ref[...], live_dev))
-    first_r = slot(reader_ref[...])
+    first_l = lax.div(source_ref[...], live_dev) * SUB
+    first_r = reader_ref[...] * SUB
     tgt_l = jnp.concatenate([first_l + r for r in range(SUB)], 1)
     tgt_r = jnp.concatenate([first_r + r for r in range(SUB)], 1)
     pick_l = onehot(iota((slots, SUB * live_dev), 0) == tgt_l)
@@ -172,8 +167,29 @@
 
 
 def prompt_kernel(
-    xc_ref, z_ref, bct_ref, cum_ref, cumt_ref, dtt_ref, skip_ref, g_ref, ss_ref, scores
+    xc_ref,
+    z_ref,
+    bct_ref,
+    cum_ref,
+    cumt_ref,
+    dtt_ref,
+    skip_ref,
+    ask_ref,
+    tgt_r_ref,
+    g_ref,
+    ss_ref,
+    late_ref,
+    scores,
 ):
+    readers = late_ref.shape[0] // 2
+    part = ask_ref.shape[1] - 2 * STATE
+    pick_r = onehot(iota((SUB * readers, ask_ref.shape[0]), 1) == tgt_r_ref[...])
+    late = mm(pick_r, ask_ref[:, 2 * STATE :])
+    for r in range(SUB):
+        rows = slice(r // 4 * readers, (r // 4 + 1) * readers)
+        late_ref[rows, r % 4 * part : (r % 4 + 1) * part] = late[
+            r * readers : (r + 1) * readers, :
+        ]
     span, width = xc_ref.shape
     heads = cum_ref.shape[1]
     block = 128
@@ -263,7 +279,7 @@
     live_dev,
     readers,
     got_ref,
-    ask_ref,
+    late_ref,
     tgt_l_ref,
     tgt_r_ref,
     xz_ref,
@@ -289,18 +305,12 @@
     live = mm(pick_l, got_ref[:, 0:width])
     new = mm(pick_r, got_ref[:, width:])
     old = mm(pick_r[(SUB - 1) * readers :, :], got_ref[:, 0:width])
-    late = mm(pick_r, ask_ref[:, 2 * STATE :])
 
     def live_row(r):
         return live[r * live_dev : (r + 1) * live_dev, :]
 
     def new_row(r, first, last):
         return new[r * readers : (r + 1) * readers, first:last]
-
-    def tail_row(r):
-        return jnp.concatenate(
-            [late[(r + i) * readers : (r + i + 1) * readers, :] for i in range(4)], 1
-        )
 
     first = []
     for t in range(steps):
@@ -308,8 +318,8 @@
         first.append(jnp.concatenate([live_row(t), wide], 0))
     inputs = [
         jnp.concatenate([live_row(4), old], 0),
-        jnp.concatenate([live_row(5), tail_row(0)], 0),
-        jnp.concatenate([live_row(6), tail_row(4)], 0),
+        jnp.concatenate([live_row(5), late_ref[0:readers, :]], 0),
+        jnp.concatenate([live_row(6), late_ref[readers:, :]], 0),
     ]
     inputs += [xz_ref[t, 0].astype(F32) for t in range(steps)]
     expand = expander(heads, width)
@@ -342,18 +352,19 @@
     hi, lo = split2(square)
     ones = jnp.ones((SUB, width), BF16)
     sums = mm_nt(ones, hi) + mm_nt(ones, lo)
-    lanes = ss_ref.shape[2]
+    lanes = ss_ref.shape[1]
     pad = -sums.shape[1] % lanes
     sums = jnp.concatenate([pre_ss_ref[...], sums, jnp.zeros((SUB, pad), F32)], 1)
     parts = [sums[0:1, i : i + lanes] for i in range(0, sums.shape[1], lanes)]
     parts += [jnp.zeros((SUB - len(parts), lanes), F32)]
-    ss_ref[...] = jnp.broadcast_to(jnp.concatenate(parts, 0)[None], ss_ref.shape)
-
-
-def finish_kernel(width_all, ss_ref, pre_ref, step_ref, gain_ref, pre_out_ref, step_out_ref):
-    total = ss_ref[0]
-    for i in range(1, ss_ref.shape[0]):
-        total = total + ss_ref[i]
+    ss_ref[...] = jnp.concatenate(parts, 0)
+
+
+def finish_kernel(width_all, *refs):
+    sums, (pre_ref, step_ref, gain_ref, pre_out_ref, step_out_ref) = refs[:-5], refs[-5:]
+    total = sums[0][...]
+    for part in sums[1:]:
+        total = total + part[...]
     scale = lax.rsqrt(total / width_all + EPS)
     gain = gain_ref[...]
     span = pre_ref.shape[0]
@@ -439,7 +450,7 @@
 
     operands = (step_bc, source[None], reader[None], length, pre_x[0])
     ask = pl.pallas_call(
-        lambda *refs: ask_kernel(RING, *refs),
+        ask_kernel,
         out_shape=shape((slots, 2 * STATE + width // 4), BF16),
         in_specs=[hbm()] * len(operands),
         out_specs=vmem(),
@@ -449,15 +460,8 @@
         name="ask",
     )(*operands)
     lanes = ask.shape[1]
-    outer = gens // RING
-    along_z = [[y * RING + z for z in range(RING)] for y in range(outer)]
-    along_y = [[y * RING + z for y in range(outer)] for z in range(RING)]
     asked = lax.all_to_all(
-        ask.reshape(gens, SUB, lanes), "gen", 0, 0, axis_index_groups=along_z, tiled=True
-    )
-    asked = jnp.swapaxes(asked.reshape(RING, outer, SUB, lanes), 0, 1)
-    asked = lax.all_to_all(
-        asked.reshape(gens, SUB, lanes), "gen", 0, 0, axis_index_groups=along_y, tiled=True
+        ask.reshape(gens, SUB, lanes), "gen", split_axis=0, concat_axis=0, tiled=True
     ).reshape(slots, lanes)
 
     live = live_state.reshape(live_dev, width, STATE)
@@ -511,21 +515,25 @@
         answer.reshape(gens, SUB, lanes), "gen", split_axis=0, concat_axis=0, tiled=True
     ).reshape(slots, lanes)
 
-    pre_gate, pre_ss = pl.pallas_call(
+    pre_gate, pre_ss, late = pl.pallas_call(
         prompt_kernel,
-        out_shape=(shape((span, width), F32), shape((SUB, span), F32)),
-        in_specs=[vmem()] * 7,
-        out_specs=(vmem(), vmem()),
+        out_shape=(
+            shape((span, width), F32),
+            shape((SUB, span), F32),
+            shape((2 * readers, width), F32),
+        ),
+        in_specs=[vmem()] * 9,
+        out_specs=(vmem(),) * 3,
         scratch_shapes=[pltpu.VMEM((128, span), F32)],
-        compiler_params=params(),
+        compiler_params=params(WHOLE),
         cost_estimate=cost(2 * heads * span * span * 128, 2500000, heads * span * span),
         name="prompt",
-    )(xconv, pre_z[0], bct, cum, cumt, dtt, jnp.repeat(skip, width // heads)[None])
+    )(xconv, pre_z[0], bct, cum, cumt, dtt, jnp.repeat(skip, width // heads)[None], asked, tgt_r.reshape(-1, 1))
 
     count = steps * rows
     step_gate, sums = pl.pallas_call(
         lambda *refs: decode_kernel(live_dev, readers, *refs),
-        out_shape=(shape((count, width), F32), shape((mp, SUB, 128), F32)),
+        out_shape=(shape((count, width), F32), shape((SUB, 128), F32)),
         in_specs=[vmem()] * 13,
         out_specs=(vmem(), vmem()),
         compiler_params=params(),
@@ -533,7 +541,7 @@
         name="decode",
     )(
         got,
-        asked,
+        late,
         tgt_l.reshape(-1, 1),
         tgt_r.reshape(-1, 1),
         step_xz,
@@ -546,17 +554,20 @@
         conv_bias[None],
         pre_ss,
     )
-    sums = lax.all_to_all(sums, "mp", split_axis=0, concat_axis=0, tiled=True)
+    sums = [sums] + [
+        lax.ppermute(sums, "mp", [(i, (i + shift) % mp) for i in range(mp)])
+        for shift in range(1, mp)
+    ]
 
     prefill_out, decoded = pl.pallas_call(
         lambda *refs: finish_kernel(width_all, *refs),
         out_shape=(shape((span, width), BF16), shape((count, width), BF16)),
-        in_specs=[vmem()] * 4,
+        in_specs=[vmem()] * (mp + 3),
         out_specs=(vmem(), vmem()),
         compiler_params=params(),
         cost_estimate=cost(1000000, 2500000),
         name="finish",
-    )(sums, pre_gate, step_gate, norm_gain[None])
+    )(*sums, pre_gate, step_gate, norm_gain[None])
     return (prefill_out[None], decoded.reshape(steps, rows, width))
 
 

time: 118 us -> 124 us (1.051)
  blocking collectives: 42.6 us -> 0 us
  starting transfers between devices: 18.1 us -> 50.1 us
  waiting for transfers between devices: 33.8 us -> 48.3 us
  Pallas kernels: 16.4 us -> 18.5 us
    all_to_all x2 -> x0, blocking collectives: 42.6 us -> none  [the longest x1 28.9 us: per_device(): lax.all_to_all(ask.reshape(gens, SUB, lanes), 'gen', 0, 0, axis_index_gro...]
    ppermute x0 -> x7, starting transfers between devices: none -> 23.1 us  [per_device(): lax.ppermute(sums, 'mp', [(i, (i + shift) % mp) for i in range(mp)])]
    all_to_all x1, starting transfers between devices: 4.18 us -> 19.3 us  [per_device(): lax.all_to_all(ask.reshape(gens, SUB, lanes), 'gen', split_axis=0, concat...]
    all_to_all x1, waiting for transfers between devices: 0.73 us -> 14.3 us  [per_device(): lax.all_to_all(ask.reshape(gens, SUB, lanes), 'gen', split_axis=0, concat...]
    all_to_all x1, starting transfers between devices: 13.9 us -> 7.75 us  [per_device(): lax.all_to_all(answer.reshape(gens, SUB, lanes), 'gen', split_axis=0, con...]
    pallas_call x1, Pallas kernels: 2.31 us -> 4.64 us  [per_device(): pl.pallas_call(prompt_kernel, out_shape=(shape((span, width), F32), shape...]
    ppermute x0 -> x7, waiting for transfers between devices: none -> 1.72 us  [per_device(): lax.ppermute(sums, 'mp', [(i, (i + shift) % mp) for i in range(mp)])]
    unnamed x39 -> x33, local copies, waits for them, and re-layouts: 3.6 us -> 3.66 us
  transfers between devices with their start and end apart: 2 -> 9, of which waited for: 2 -> 4; matrix products, arithmetic and copies ran while one was open for 0% -> 1% of each run, Pallas kernels for 6% -> 8%
where the time goes in v4:
time: 124 us
  starting transfers between devices  50.1 us (40%)
  waiting for transfers between devices  48.3 us (39%)
  Pallas kernels  18.5 us (15%)
  local copies, waits for them, and re-layouts  5.24 us (4%)
  between operations  1.57 us (1%)
    all_to_all x1, waiting for transfers between devices, per_device(): lax.all_to_all(answer.reshape(gens, SUB, lanes), 'gen', split_axis=0, con...  32.2 us
    ppermute x7, starting transfers between devices, per_device(): lax.ppermute(sums, 'mp', [(i, (i + shift) % mp) for i in range(mp)])  23.1 us
    all_to_all x1, starting transfers between devices, per_device(): lax.all_to_all(ask.reshape(gens, SUB, lanes), 'gen', split_axis=0, concat...  19.3 us
    all_to_all x1, waiting for transfers between devices, per_device(): lax.all_to_all(ask.reshape(gens, SUB, lanes), 'gen', split_axis=0, concat...  14.3 us
    all_to_all x1, starting transfers between devices, per_device(): lax.all_to_all(answer.reshape(gens, SUB, lanes), 'gen', split_axis=0, con...  7.75 us
    pallas_call x1, Pallas kernels, per_device(): pl.pallas_call(answer_kernel, out_shape=shape((slots, width + width // 2)...  4.74 us
    pallas_call x1, Pallas kernels, per_device(): pl.pallas_call(state_kernel, out_shape=(shape((span, width), BF16), shape...  4.67 us
    pallas_call x1, Pallas kernels, per_device(): pl.pallas_call(prompt_kernel, out_shape=(shape((span, width), F32), shape...  4.64 us
  transfers between devices with their start and end apart: 9, of which 4 were waited for; matrix products, arithmetic and copies ran while one was open for 1% of the time, Pallas kernels for 8%

profile of v4, /device:TPU:1, one launch (start us, length us, event | category | flops | bytes accessed | tf_op | source)
XLA Modules:
  0.0 123.8 jit_solution(4984410499106017603)
XLA Ops:
  1.3 2.3 %ask.1 = bf16[512,256]{1,0:T(8,128)(2,1)} custom-call(bf16[4,2,48,64]{3,2,1,0:T(8,128)(2,1)} %refs_5_.1, s32[1,32]{1,0:T(1,128)} %bitcast.48, s32[1,16]{1,0:T(1,128)} %bitcast.47, s32[1,1]{1,0:T(1,128)} %bitcast.27.refs_3_, bf16[512,512]{1,0:T(8,128)(2,1)} %bitcast.44), custom_call_target="tpu_custom_call" | custom-call | flops 50331648 | bytes 800000 | tf_op jit(solution)/shard_map/ask/pallas_call | solution.py:452
  3.5 19.3 %all-to-all-start = ((bf16[64,8,256]{2,1,0:T(8,128)(2,1)}), bf16[64,8,256]{2,1,0:T(8,128)(2,1)S(1)}, u32[]{:S(2)}, u32[]{:S(2)}) async-start(bf16[64,8,256]{2,1,0:T(8,128)(2,1)} %bitcast.41), calls=%async_computation | async-start | bytes 524288 | tf_op jit(solution)/shard_map/all_to_all | solution.py:463
  22.8 0.0 copy-start.14
  22.9 0.0 copy-start.9
  22.9 0.0 copy-start.15
  22.9 0.0 copy-start.13
  22.9 4.7 %state.1 = (bf16[512,512]{1,0:T(8,128)(2,1)}, f32[512,8]{1,0:T(8,128)}, f32[8,512]{1,0:T(8,128)}, f32[8,512]{1,0:T(8,128)}, bf16[128,512]{1,0:T(8,128)(2,1)}, /*index=5*/bf16[8,512]{1,0:T(8,128)(2,1)}) custom-call(s32[1,1]{1,0:T(1,128)} %bitcast.28.refs_0_, bf16[8,512]{1,0:T(8,128)(2,1)} %bitcast.54, f32[1,8]{1,0:T(1,128)} %bitcast.35, f32[1,8]{1,0:T(1,128)} %bitcast.37, ...), custom_call_target="tpu_custom_call" | custom-call | flops 335544320 | bytes 2000000 | tf_op jit(solution)/shard_map/state/pallas_call | solution.py:478
  27.6 14.3 %all-to-all-done = bf16[64,8,256]{2,1,0:T(8,128)(2,1)S(1)} async-done(((bf16[64,8,256]{2,1,0:T(8,128)(2,1)}), bf16[64,8,256]{2,1,0:T(8,128)(2,1)S(1)}, u32[]{:S(2)}, u32[]{:S(2)}) %all-to-all-start) | async-done | bytes 262176 | tf_op jit(solution)/shard_map/all_to_all | solution.py:463
  41.9 0.0 copy-start.12
  41.9 0.7 copy-done.12
  42.6 4.7 %answer.1 = bf16[512,768]{1,0:T(8,128)(2,1)} custom-call(bf16[512,256]{1,0:T(8,128)(2,1)} %bitcast.42, bf16[96,512]{1,0:T(8,128)(2,1)} %bitcast.46, bf16[128,512]{1,0:T(8,128)(2,1)} %get-tuple-element.15.refs_2_, bf16[8,512]{1,0:T(8,128)(2,1)} %get-tuple-element.16.refs_3_, bf16[32,512,64]{2,1,0:T(8,128)(2,1)} %bitcast.39), custom_call_target="tpu_custom_call" | custom-call | flops 536870912 | bytes 6000000 | tf_op jit(solution)/shard_map/answer/pallas_call | solution.py:498
  47.4 0.0 copy-start.1
  47.4 0.0 copy-start.2
  47.4 0.0 copy-start.6
  47.4 0.0 copy-start.7
  47.4 0.0 copy-start.10
  47.4 0.0 copy-start.11
  47.4 0.0 copy-start.8
  47.4 7.7 %all-to-all-start.1 = ((bf16[64,8,768]{2,1,0:T(8,128)(2,1)}), bf16[64,8,768]{2,1,0:T(8,128)(2,1)S(1)}, u32[]{:S(2)}, u32[]{:S(2)}) async-start(bf16[64,8,768]{2,1,0:T(8,128)(2,1)} %bitcast.40), calls=%async_computation.1 | async-start | bytes 1572864 | tf_op jit(solution)/shard_map/all_to_all | solution.py:514
  55.2 0.0 copy-done.14
  55.2 0.7 add.55.tgt_r_ref.refs_3_
  55.9 0.0 copy-done.9
  55.9 0.0 copy-start.3
  55.9 0.1 broadcast_in_dim.38
  56.0 0.7 broadcast_in_dim_reshape.3.skip_ref
  56.7 0.0 copy-done.15
  56.7 0.1 add.56.refs_2_
  56.8 0.0 copy-done.13
  56.9 0.1 copy.24
  57.0 4.6 %prompt.1 = (f32[512,512]{1,0:T(8,128)}, f32[8,512]{1,0:T(8,128)}, f32[32,512]{1,0:T(8,128)}) custom-call(bf16[512,512]{1,0:T(8,128)(2,1)} %get-tuple-element.17.xc_ref, bf16[512,512]{1,0:T(8,128)(2,1)} %bitcast.49, bf16[2,64,512]{2,1,0:T(8,128)(2,1)} %bitcast.53, f32[512,8]{1,0:T(8,128)} %get-tuple-element.18.cum_ref, f32[8,512]{1,0:T(8,128)} %get-tuple-element.19.cumt_ref, ...), custom_call_target="tpu_custom_call" | custom-call | flops 536870912 | bytes 2500000 | tf_op jit(solution)/shard_map/prompt/pallas_call | solution.py:518
  61.6 32.2 %all-to-all-done.1 = bf16[64,8,768]{2,1,0:T(8,128)(2,1)S(1)} async-done(((bf16[64,8,768]{2,1,0:T(8,128)(2,1)}), bf16[64,8,768]{2,1,0:T(8,128)(2,1)S(1)}, u32[]{:S(2)}, u32[]{:S(2)}) %all-to-all-start.1) | async-done | bytes 786464 | tf_op jit(solution)/shard_map/all_to_all | solution.py:514
  93.8 0.0 copy-done.1
  93.8 0.0 copy-done.2
  93.8 0.0 copy-done.6
  93.8 0.0 copy-done.7
  93.9 0.0 copy-done.10
  93.9 0.0 copy-done.11
  93.9 0.0 copy-done.3
  93.9 0.0 copy-start.4
  93.9 0.8 copy-done.4
  94.7 0.0 copy-start.5
  94.7 0.7 copy-done.5
  95.4 1.2 decode.1
  96.7 6.0 %collective-permute-start = (f32[8,128]{1,0:T(8,128)S(1)}, f32[8,128]{1,0:T(8,128)S(1)}, u32[]{:S(2)}, u32[]{:S(2)}) collective-permute-start(f32[8,128]{1,0:T(8,128)S(1)} %get-tuple-element.23.refs_0_), channel_id=1, source_target_pairs={{0,1},{1,2},{2,3},{3,4},{4,5},{5,6},{6,7},{7,0},{8,9},{9,10},{10,1... | collective-permute-start | bytes 12296 | tf_op jit(solution)/shard_map/ppermute | solution.py:558
  102.7 3.1 %collective-permute-start.1 = (f32[8,128]{1,0:T(8,128)S(1)}, f32[8,128]{1,0:T(8,128)S(1)}, u32[]{:S(2)}, u32[]{:S(2)}) collective-permute-start(f32[8,128]{1,0:T(8,128)S(1)} %get-tuple-element.23.refs_0_), channel_id=1, source_target_pairs={{0,2},{1,3},{2,4},{3,5},{4,6},{5,7},{6,0},{7,1},{8,10},{9,11},{10,... | collective-permute-start | bytes 12296 | tf_op jit(solution)/shard_map/ppermute | solution.py:558
  105.8 3.4 %collective-permute-start.2 = (f32[8,128]{1,0:T(8,128)S(1)}, f32[8,128]{1,0:T(8,128)S(1)}, u32[]{:S(2)}, u32[]{:S(2)}) collective-permute-start(f32[8,128]{1,0:T(8,128)S(1)} %get-tuple-element.23.refs_0_), channel_id=1, source_target_pairs={{0,3},{1,4},{2,5},{3,6},{4,7},{5,0},{6,1},{7,2},{8,11},{9,12},{10,... | collective-permute-start | bytes 12296 | tf_op jit(solution)/shard_map/ppermute | solution.py:558
  109.2 2.4 %collective-permute-start.3 = (f32[8,128]{1,0:T(8,128)S(1)}, f32[8,128]{1,0:T(8,128)S(1)}, u32[]{:S(2)}, u32[]{:S(2)}) collective-permute-start(f32[8,128]{1,0:T(8,128)S(1)} %get-tuple-element.23.refs_0_), channel_id=1, source_target_pairs={{0,4},{1,5},{2,6},{3,7},{4,0},{5,1},{6,2},{7,3},{8,12},{9,13},{10,... | collective-permute-start | bytes 12296 | tf_op jit(solution)/shard_map/ppermute | solution.py:558
  111.7 3.9 %collective-permute-start.4 = (f32[8,128]{1,0:T(8,128)S(1)}, f32[8,128]{1,0:T(8,128)S(1)}, u32[]{:S(2)}, u32[]{:S(2)}) collective-permute-start(f32[8,128]{1,0:T(8,128)S(1)} %get-tuple-element.23.refs_0_), channel_id=1, source_target_pairs={{0,5},{1,6},{2,7},{3,0},{4,1},{5,2},{6,3},{7,4},{8,13},{9,14},{10,... | collective-permute-start | bytes 12296 | tf_op jit(solution)/shard_map/ppermute | solution.py:558
  115.6 0.0 collective-permute-done.refs_1_
  115.6 2.6 %collective-permute-start.5 = (f32[8,128]{1,0:T(8,128)S(1)}, f32[8,128]{1,0:T(8,128)S(1)}, u32[]{:S(2)}, u32[]{:S(2)}) collective-permute-start(f32[8,128]{1,0:T(8,128)S(1)} %get-tuple-element.23.refs_0_), channel_id=1, source_target_pairs={{0,6},{1,7},{2,0},{3,1},{4,2},{5,3},{6,4},{7,5},{8,14},{9,15},{10,... | collective-permute-start | bytes 12296 | tf_op jit(solution)/shard_map/ppermute | solution.py:558
  118.2 0.0 collective-permute-done.1.refs_2_
  118.2 1.6 %collective-permute-start.6 = (f32[8,128]{1,0:T(8,128)S(1)}, f32[8,128]{1,0:T(8,128)S(1)}, u32[]{:S(2)}, u32[]{:S(2)}) collective-permute-start(f32[8,128]{1,0:T(8,128)S(1)} %get-tuple-element.23.refs_0_), channel_id=1, source_target_pairs={{0,7},{1,0},{2,1},{3,2},{4,3},{5,4},{6,5},{7,6},{8,15},{9,8},{10,9... | collective-permute-start | bytes 12296 | tf_op jit(solution)/shard_map/ppermute | solution.py:558
  119.8 0.0 collective-permute-done.2.refs_3_
  119.8 0.0 collective-permute-done.3.refs_4_
  119.8 0.0 collective-permute-done.4.refs_5_
  119.8 0.2 collective-permute-done.5.refs_6_
  120.0 1.6 %collective-permute-done.6.refs_7_ = f32[8,128]{1,0:T(8,128)S(1)} collective-permute-done((f32[8,128]{1,0:T(8,128)S(1)}, f32[8,128]{1,0:T(8,128)S(1)}, u32[]{:S(2)}, u32[]{:S(2)}) %collective-permute-start.6) | collective-permute-done | bytes 4128 | tf_op jit(solution)/shard_map/ppermute | solution.py:558
  121.5 0.0 copy-done.8
  121.5 0.0 copy-start
  121.5 1.2 copy-done
  122.8 1.0 finish.1
  (4 shorter events, 0.0 us)
Async XLA Ops:
  3.5 38.4 %all-to-all-start = ((bf16[64,8,256]{2,1,0:T(8,128)(2,1)}), bf16[64,8,256]{2,1,0:T(8,128)(2,1)S(1)}, u32[]{:S(2)}, u32[]{:S(2)}) async-start(bf16[64,8,256]{2,1,0:T(8,128)(2,1)} %bitcast.41), calls=%async_computation | async-start | bytes 524288 | tf_op jit(solution)/shard_map/all_to_all | solution.py:463
  22.8 32.3 %copy-start.14 = (s32[16]{0:T(128)S(1)}, s32[16]{0:T(128)}, u32[]{:S(2)}) copy-start(s32[16]{0:T(128)} %param.26) | copy-start | bytes 196
  22.9 33.1 %copy-start.9 = (f32[8]{0:T(128)S(1)}, f32[8]{0:T(128)}, u32[]{:S(2)}) copy-start(f32[8]{0:T(128)} %param.34) | copy-start | bytes 100
  22.9 33.8 %copy-start.15 = (s32[32]{0:T(128)S(1)}, s32[32]{0:T(128)}, u32[]{:S(2)}) copy-start(s32[32]{0:T(128)} %param.25) | copy-start | bytes 388
  22.9 34.0 %copy-start.13 = (bf16[4,48,8]{1,2,0:T(8,128)(2,1)S(1)}, bf16[4,48,8]{1,2,0:T(8,128)(2,1)}, u32[]{:S(2)}) copy-start(bf16[4,48,8]{1,2,0:T(8,128)(2,1)} %param.29) | copy-start | bytes 9220
  41.9 0.7 copy-start.12
  47.4 46.5 %copy-start.1 = (bf16[4,2,48,512]{3,2,1,0:T(8,128)(2,1)S(1)}, bf16[4,2,48,512]{3,2,1,0:T(8,128)(2,1)}, u32[]{:S(2)}) copy-start(bf16[4,2,48,512]{3,2,1,0:T(8,128)(2,1)} %refs_4_.3) | copy-start | bytes 1179652
  47.4 46.5 %copy-start.2 = (bf16[4,2,48,64]{3,2,1,0:T(8,128)(2,1)S(1)}, bf16[4,2,48,64]{3,2,1,0:T(8,128)(2,1)}, u32[]{:S(2)}) copy-start(bf16[4,2,48,64]{3,2,1,0:T(8,128)(2,1)} %refs_5_.1) | copy-start | bytes 147460
  47.4 46.5 %copy-start.6 = (bf16[4,512]{1,0:T(4,128)(2,1)S(1)}, bf16[4,512]{1,0:T(4,128)(2,1)}, u32[]{:S(2)}) copy-start(bf16[4,512]{1,0:T(4,128)(2,1)} %refs_10_.1) | copy-start | bytes 12292
  47.4 46.5 %copy-start.7 = (f32[512]{0:T(512)S(1)}, f32[512]{0:T(512)}, u32[]{:S(2)}) copy-start(f32[512]{0:T(512)} %param.33) | copy-start | bytes 6148
  47.4 46.5 %copy-start.10 = (f32[8]{0:T(128)S(1)}, f32[8]{0:T(128)}, u32[]{:S(2)}) copy-start(f32[8]{0:T(128)} %param.30) | copy-start | bytes 100
  47.4 46.5 %copy-start.11 = (f32[8]{0:T(128)S(1)}, f32[8]{0:T(128)}, u32[]{:S(2)}) copy-start(f32[8]{0:T(128)} %param.31) | copy-start | bytes 100
  47.4 74.1 %copy-start.8 = (f32[512]{0:T(512)S(1)}, f32[512]{0:T(512)}, u32[]{:S(2)}) copy-start(f32[512]{0:T(512)} %param.35) | copy-start | bytes 6148
  47.4 46.4 %all-to-all-start.1 = ((bf16[64,8,768]{2,1,0:T(8,128)(2,1)}), bf16[64,8,768]{2,1,0:T(8,128)(2,1)S(1)}, u32[]{:S(2)}, u32[]{:S(2)}) async-start(bf16[64,8,768]{2,1,0:T(8,128)(2,1)} %bitcast.40), calls=%async_computation.1 | async-start | bytes 1572864 | tf_op jit(solution)/shard_map/all_to_all | solution.py:514
  55.9 37.9 %copy-start.3 = (s32[128,1]{1,0:T(8,128)S(1)}, s32[128,1]{1,0:T(8,128)}, u32[]{:S(2)}) copy-start(s32[128,1]{1,0:T(8,128)} %add.55.tgt_r_ref.refs_3_) | copy-start | bytes 1540
  93.9 0.8 copy-start.4
  94.7 0.7 copy-start.5
  96.7 19.0 %collective-permute-start = (f32[8,128]{1,0:T(8,128)S(1)}, f32[8,128]{1,0:T(8,128)S(1)}, u32[]{:S(2)}, u32[]{:S(2)}) collective-permute-start(f32[8,128]{1,0:T(8,128)S(1)} %get-tuple-element.23.refs_0_), channel_id=1, source_target_pairs={{0,1},{1,2},{2,3},{3,4},{4,5},{5,6},{6,7},{7,0},{8,9},{9,10},{10,1... | collective-permute-start | bytes 12296 | tf_op jit(solution)/shard_map/ppermute | solution.py:558
  102.7 15.5 %collective-permute-start.1 = (f32[8,128]{1,0:T(8,128)S(1)}, f32[8,128]{1,0:T(8,128)S(1)}, u32[]{:S(2)}, u32[]{:S(2)}) collective-permute-start(f32[8,128]{1,0:T(8,128)S(1)} %get-tuple-element.23.refs_0_), channel_id=1, source_target_pairs={{0,2},{1,3},{2,4},{3,5},{4,6},{5,7},{6,0},{7,1},{8,10},{9,11},{10,... | collective-permute-start | bytes 12296 | tf_op jit(solution)/shard_map/ppermute | solution.py:558
  105.8 14.0 %collective-permute-start.2 = (f32[8,128]{1,0:T(8,128)S(1)}, f32[8,128]{1,0:T(8,128)S(1)}, u32[]{:S(2)}, u32[]{:S(2)}) collective-permute-start(f32[8,128]{1,0:T(8,128)S(1)} %get-tuple-element.23.refs_0_), channel_id=1, source_target_pairs={{0,3},{1,4},{2,5},{3,6},{4,7},{5,0},{6,1},{7,2},{8,11},{9,12},{10,... | collective-permute-start | bytes 12296 | tf_op jit(solution)/shard_map/ppermute | solution.py:558
  109.2 10.6 %collective-permute-start.3 = (f32[8,128]{1,0:T(8,128)S(1)}, f32[8,128]{1,0:T(8,128)S(1)}, u32[]{:S(2)}, u32[]{:S(2)}) collective-permute-start(f32[8,128]{1,0:T(8,128)S(1)} %get-tuple-element.23.refs_0_), channel_id=1, source_target_pairs={{0,4},{1,5},{2,6},{3,7},{4,0},{5,1},{6,2},{7,3},{8,12},{9,13},{10,... | collective-permute-start | bytes 12296 | tf_op jit(solution)/shard_map/ppermute | solution.py:558
  111.7 8.2 %collective-permute-start.4 = (f32[8,128]{1,0:T(8,128)S(1)}, f32[8,128]{1,0:T(8,128)S(1)}, u32[]{:S(2)}, u32[]{:S(2)}) collective-permute-start(f32[8,128]{1,0:T(8,128)S(1)} %get-tuple-element.23.refs_0_), channel_id=1, source_target_pairs={{0,5},{1,6},{2,7},{3,0},{4,1},{5,2},{6,3},{7,4},{8,13},{9,14},{10,... | collective-permute-start | bytes 12296 | tf_op jit(solution)/shard_map/ppermute | solution.py:558
  115.6 4.4 %collective-permute-start.5 = (f32[8,128]{1,0:T(8,128)S(1)}, f32[8,128]{1,0:T(8,128)S(1)}, u32[]{:S(2)}, u32[]{:S(2)}) collective-permute-start(f32[8,128]{1,0:T(8,128)S(1)} %get-tuple-element.23.refs_0_), channel_id=1, source_target_pairs={{0,6},{1,7},{2,0},{3,1},{4,2},{5,3},{6,4},{7,5},{8,14},{9,15},{10,... | collective-permute-start | bytes 12296 | tf_op jit(solution)/shard_map/ppermute | solution.py:558
  118.2 3.3 %collective-permute-start.6 = (f32[8,128]{1,0:T(8,128)S(1)}, f32[8,128]{1,0:T(8,128)S(1)}, u32[]{:S(2)}, u32[]{:S(2)}) collective-permute-start(f32[8,128]{1,0:T(8,128)S(1)} %get-tuple-element.23.refs_0_), channel_id=1, source_target_pairs={{0,7},{1,0},{2,1},{3,2},{4,3},{5,4},{6,5},{7,6},{8,15},{9,8},{10,9... | collective-permute-start | bytes 12296 | tf_op jit(solution)/shard_map/ppermute | solution.py:558
  121.5 1.2 copy-start

commit v5 on v4

--- a/solution.py
+++ b/solution.py
@@ -244,34 +244,32 @@
     width = prefix_ref.shape[1]
     half = width // 2
     ask = ask_ref[:, 0 : 2 * STATE]
-    row, col = iota((slots, slots), 0), iota((slots, slots), 1)
-    place = mm(onehot(col == (row // SUB) * SUB + 4), ask)
+    down, lane = iota((slots, 1), 0), iota((1, slots), 1)
+    in_slot = jnp.bitwise_and(down, SUB - 1)
+    place = mm(onehot(lane == down - in_slot + 4), ask)
     lane0 = onehot(iota((SUB, 2 * STATE), 1) == 0)
     across = mm_nt(lane0, place.astype(BF16))[0:1, :].astype(jnp.int32)
-    row, col = iota((count, slots), 0), iota((count, slots), 1)
-    back = onehot(row + SUB - col % SUB == across * SUB)
-    got = mm(back, ask)
-    cs[...] = jnp.where(iota(got.shape, 0) % SUB < 4, got, 0.0)
+    back = (across - 1) * SUB + jnp.bitwise_and(lane, SUB - 1)
+    got = mm(onehot(iota((count, 1), 0) == back), ask)
+    first = jnp.bitwise_and(iota((count, 1), 0), SUB - 1) < 4
+    cs[...] = jnp.where(first, got, 0.0)
     for k in range(live_dev):
         if k % chunk == 0:
             copies[4 + k // chunk].wait()
         rows = slice(k * SUB, (k + 1) * SUB)
         ys[rows, :] = mm_nt(cs[rows, 0:STATE].astype(BF16), state_ref[k])
     place = place[:, 0:1].astype(jnp.int32)
-    row, col = iota((slots, count), 0), iota((slots, count), 1)
-    there = onehot(col + SUB - row % SUB == place * SUB)
+    there = onehot(iota((1, count), 1) == (place - 1) * SUB + in_slot)
     live = mm(there, ys[...].astype(BF16))
     kept = conv_ref.shape[0]
-    row, col = iota((slots, kept), 0), iota((slots, kept), 1)
-    there = onehot(
-        (lax.div(col, live_dev) + 4 == row % SUB) & (col % live_dev + 1 == place)
-    )
+    conv_row = (in_slot - 4) * live_dev + place - 1
+    conv_row = jnp.where((place > 0) & (in_slot >= 4), conv_row, -1)
+    there = onehot(iota((1, kept), 1) == conv_row)
     live = (live + mm(there, conv_ref[...])).reshape(slots // SUB, SUB, width)
     live = live + tail_ref[...].astype(F32)[None]
     out_ref[:, 0:width] = live.reshape(slots, width).astype(BF16)
     new = mm(ask, prefix_ref[...])
-    first = iota((slots, half), 0) % SUB < SUB // 2
-    new = jnp.where(first, new[:, 0:half], new[:, half:width])
+    new = jnp.where(in_slot < SUB // 2, new[:, 0:half], new[:, half:width])
     out_ref[:, width : width + half] = new.astype(BF16)
 
 
@@ -296,7 +294,8 @@
 ):
     slots = got_ref.shape[0]
     steps, _, rows, width = xz_ref.shape
-    heads = raw_ref.shape[1]
+    heads = raw_ref.shape[0] // steps
+    raws = raw_ref[...].astype(F32).T
     span = pre_ss_ref.shape[1]
     taps = cw_ref.shape[0]
     half = width // 2
@@ -330,7 +329,7 @@
         for k in range(taps):
             acc = acc + inputs[t + k] * weights[k]
         xcs.append(silu(acc).astype(BF16).astype(F32))
-        dt = softplus(raw_ref[t * rows : (t + 1) * rows, :].astype(F32) + bias_ref[...])
+        dt = softplus(raws[:, t * heads : (t + 1) * heads] + bias_ref[...])
         dts.append(dt)
         decayed = -dt * decay_ref[...]
         logs.append(decayed if t == 0 else logs[-1] + decayed)
@@ -352,19 +351,18 @@
     hi, lo = split2(square)
     ones = jnp.ones((SUB, width), BF16)
     sums = mm_nt(ones, hi) + mm_nt(ones, lo)
-    lanes = ss_ref.shape[1]
+    lanes = ss_ref.shape[2]
     pad = -sums.shape[1] % lanes
     sums = jnp.concatenate([pre_ss_ref[...], sums, jnp.zeros((SUB, pad), F32)], 1)
     parts = [sums[0:1, i : i + lanes] for i in range(0, sums.shape[1], lanes)]
     parts += [jnp.zeros((SUB - len(parts), lanes), F32)]
-    ss_ref[...] = jnp.concatenate(parts, 0)
-
-
-def finish_kernel(width_all, *refs):
-    sums, (pre_ref, step_ref, gain_ref, pre_out_ref, step_out_ref) = refs[:-5], refs[-5:]
-    total = sums[0][...]
-    for part in sums[1:]:
-        total = total + part[...]
+    ss_ref[...] = jnp.broadcast_to(jnp.concatenate(parts, 0)[None], ss_ref.shape)
+
+
+def finish_kernel(width_all, ss_ref, pre_ref, step_ref, gain_ref, pre_out_ref, step_out_ref):
+    total = ss_ref[0]
+    for i in range(1, ss_ref.shape[0]):
+        total = total + ss_ref[i]
     scale = lax.rsqrt(total / width_all + EPS)
     gain = gain_ref[...]
     span = pre_ref.shape[0]
@@ -525,7 +523,7 @@
         in_specs=[vmem()] * 9,
         out_specs=(vmem(),) * 3,
         scratch_shapes=[pltpu.VMEM((128, span), F32)],
-        compiler_params=params(WHOLE),
+        compiler_params=params(),
         cost_estimate=cost(2 * heads * span * span * 128, 2500000, heads * span * span),
         name="prompt",
     )(xconv, pre_z[0], bct, cum, cumt, dtt, jnp.repeat(skip, width // heads)[None], asked, tgt_r.reshape(-1, 1))
@@ -533,7 +531,7 @@
     count = steps * rows
     step_gate, sums = pl.pallas_call(
         lambda *refs: decode_kernel(live_dev, readers, *refs),
-        out_shape=(shape((count, width), F32), shape((SUB, 128), F32)),
+        out_shape=(shape((count, width), F32), shape((mp, SUB, 128), F32)),
         in_specs=[vmem()] * 13,
         out_specs=(vmem(), vmem()),
         compiler_params=params(),
@@ -546,7 +544,7 @@
         tgt_r.reshape(-1, 1),
         step_xz,
         step_bc,
-        step_raw.reshape(count, heads),
+        jnp.swapaxes(step_raw, 1, 2).reshape(steps * heads, rows),
         decay[None],
         dt_bias[None],
         skip[None],
@@ -554,20 +552,17 @@
         conv_bias[None],
         pre_ss,
     )
-    sums = [sums] + [
-        lax.ppermute(sums, "mp", [(i, (i + shift) % mp) for i in range(mp)])
-        for shift in range(1, mp)
-    ]
+    sums = lax.all_to_all(sums, "mp", split_axis=0, concat_axis=0, tiled=True)
 
     prefill_out, decoded = pl.pallas_call(
         lambda *refs: finish_kernel(width_all, *refs),
         out_shape=(shape((span, width), BF16), shape((count, width), BF16)),
-        in_specs=[vmem()] * (mp + 3),
+        in_specs=[vmem()] * 4,
         out_specs=(vmem(), vmem()),
         compiler_params=params(),
         cost_estimate=cost(1000000, 2500000),
         name="finish",
-    )(*sums, pre_gate, step_gate, norm_gain[None])
+    )(sums, pre_gate, step_gate, norm_gain[None])
     return (prefill_out[None], decoded.reshape(steps, rows, width))
 
 

time: 124 us -> 111 us (0.90)
  starting transfers between devices: 50.1 us -> 27 us
  blocking collectives: 0 us -> 13.7 us
  Pallas kernels: 18.5 us -> 16.5 us
    ppermute x7 -> x0, starting transfers between devices: 23.1 us -> none  [per_device(): lax.ppermute(sums, 'mp', [(i, (i + shift) % mp) for i in range(mp)])]
    all_to_all x0 -> x1, blocking collectives: none -> 13.7 us  [per_device(): sums = lax.all_to_all(sums, 'mp', split_axis=0, concat_axis=0, tiled=True)]
    pallas_call x1, Pallas kernels: 4.64 us -> 2.36 us  [per_device(): pl.pallas_call(prompt_kernel, out_shape=(shape((span, width), F32), shape...]
    ppermute x7 -> x0, waiting for transfers between devices: 1.72 us -> none  [per_device(): lax.ppermute(sums, 'mp', [(i, (i + shift) % mp) for i in range(mp)])]
    unnamed x33 -> x38, local copies, waits for them, and re-layouts: 3.66 us -> 3.73 us
  transfers between devices with their start and end apart: 9 -> 2, of which waited for: 4 -> 2; matrix products, arithmetic and copies ran while one was open for 1% -> 0% of each run, Pallas kernels for 8% -> 6%
where the time goes in v5:
time: 111 us; the launch traced here: 110 us
  waiting for transfers between devices  47.1 us (42%)
  starting transfers between devices  27 us (24%)
  Pallas kernels  16.5 us (15%)
  blocking collectives  13.7 us (12%)
  local copies, waits for them, and re-layouts  4.09 us (4%)
  between operations  1.57 us (1%)
    all_to_all x1, waiting for transfers between devices, per_device(): lax.all_to_all(answer.reshape(gens, SUB, lanes), 'gen', split_axis=0, con...  32.9 us
    all_to_all x1, starting transfers between devices, per_device(): lax.all_to_all(ask.reshape(gens, SUB, lanes), 'gen', split_axis=0, concat...  19.3 us
    all_to_all x1, waiting for transfers between devices, per_device(): lax.all_to_all(ask.reshape(gens, SUB, lanes), 'gen', split_axis=0, concat...  14.2 us
    all_to_all x1, blocking collectives, per_device(): sums = lax.all_to_all(sums, 'mp', split_axis=0, concat_axis=0, tiled=True)  13.7 us
    all_to_all x1, starting transfers between devices, per_device(): lax.all_to_all(answer.reshape(gens, SUB, lanes), 'gen', split_axis=0, con...  7.74 us
    pallas_call x1, Pallas kernels, per_device(): pl.pallas_call(answer_kernel, out_shape=shape((slots, width + width // 2)...  4.75 us
    pallas_call x1, Pallas kernels, per_device(): pl.pallas_call(state_kernel, out_shape=(shape((span, width), BF16), shape...  4.73 us
    unnamed x38, local copies, waits for them, and re-layouts  3.73 us
  transfers between devices with their start and end apart: 2, of which 2 were waited for; matrix products, arithmetic and copies ran while one was open for 0% of the time, Pallas kernels for 6%

profile of v5, /device:TPU:1, one launch (start us, length us, event | category | flops | bytes accessed | tf_op | source)
XLA Modules:
  0.0 110.1 jit_solution(14712159461486626252)
XLA Ops:
  1.3 2.3 %ask.1 = bf16[512,256]{1,0:T(8,128)(2,1)} custom-call(bf16[4,2,48,64]{3,2,1,0:T(8,128)(2,1)} %refs_5_.1, s32[1,32]{1,0:T(1,128)} %bitcast.53, s32[1,16]{1,0:T(1,128)} %bitcast.52, s32[1,1]{1,0:T(1,128)} %bitcast.29.refs_3_, bf16[512,512]{1,0:T(8,128)(2,1)} %bitcast.49), custom_call_target="tpu_custom_call" | custom-call | flops 50331648 | bytes 800000 | tf_op jit(solution)/shard_map/ask/pallas_call | solution.py:450
  3.5 19.3 %all-to-all-start = ((bf16[64,8,256]{2,1,0:T(8,128)(2,1)}), bf16[64,8,256]{2,1,0:T(8,128)(2,1)S(1)}, u32[]{:S(2)}, u32[]{:S(2)}) async-start(bf16[64,8,256]{2,1,0:T(8,128)(2,1)} %bitcast.48), calls=%async_computation | async-start | bytes 524288 | tf_op jit(solution)/shard_map/all_to_all | solution.py:461
  22.8 0.0 copy-start.17
  22.9 0.0 copy-start.6
  22.9 0.0 copy-start.18
  22.9 0.0 copy-start.11
  22.9 0.0 copy-start.12
  22.9 4.7 %state.1 = (bf16[512,512]{1,0:T(8,128)(2,1)}, f32[512,8]{1,0:T(8,128)}, f32[8,512]{1,0:T(8,128)}, f32[8,512]{1,0:T(8,128)}, bf16[128,512]{1,0:T(8,128)(2,1)}, /*index=5*/bf16[8,512]{1,0:T(8,128)(2,1)}) custom-call(s32[1,1]{1,0:T(1,128)} %bitcast.30.refs_0_, bf16[8,512]{1,0:T(8,128)(2,1)} %bitcast.56, f32[1,8]{1,0:T(1,128)} %bitcast.39, f32[1,8]{1,0:T(1,128)} %bitcast.41, ...), custom_call_target="tpu_custom_call" | custom-call | flops 335544320 | bytes 2000000 | tf_op jit(solution)/shard_map/state/pallas_call | solution.py:476
  27.6 0.0 copy-start.15
  27.7 0.0 copy-start.16
  27.7 14.2 %all-to-all-done = bf16[64,8,256]{2,1,0:T(8,128)(2,1)S(1)} async-done(((bf16[64,8,256]{2,1,0:T(8,128)(2,1)}), bf16[64,8,256]{2,1,0:T(8,128)(2,1)S(1)}, u32[]{:S(2)}, u32[]{:S(2)}) %all-to-all-start) | async-done | bytes 262176 | tf_op jit(solution)/shard_map/all_to_all | solution.py:461
  41.9 0.0 copy-start
  41.9 0.7 copy-done
  42.6 4.7 %answer.1 = bf16[512,768]{1,0:T(8,128)(2,1)} custom-call(bf16[512,256]{1,0:T(8,128)(2,1)} %bitcast.32, bf16[96,512]{1,0:T(8,128)(2,1)} %bitcast.51, bf16[128,512]{1,0:T(8,128)(2,1)} %get-tuple-element.15.refs_2_, bf16[8,512]{1,0:T(8,128)(2,1)} %get-tuple-element.16.refs_3_, bf16[32,512,64]{2,1,0:T(8,128)(2,1)} %bitcast.46), custom_call_target="tpu_custom_call" | custom-call | flops 536870912 | bytes 6000000 | tf_op jit(solution)/shard_map/answer/pallas_call | solution.py:496
  47.4 0.0 copy-start.2
  47.4 0.0 copy-start.3
  47.4 0.0 copy-start.4
  47.4 0.0 copy-start.5
  47.4 0.0 copy-start.7
  47.4 0.0 copy-start.9
  47.4 0.0 copy-start.10
  47.5 0.0 copy-start.8
  47.5 7.7 %all-to-all-start.1 = ((bf16[64,8,768]{2,1,0:T(8,128)(2,1)}), bf16[64,8,768]{2,1,0:T(8,128)(2,1)S(1)}, u32[]{:S(2)}, u32[]{:S(2)}) async-start(bf16[64,8,768]{2,1,0:T(8,128)(2,1)} %bitcast.47), calls=%async_computation.1 | async-start | bytes 1572864 | tf_op jit(solution)/shard_map/all_to_all | solution.py:512
  55.2 0.0 copy-done.17
  55.2 0.1 add.55.tgt_r_ref.refs_3_
  55.3 0.0 copy-done.6
  55.3 0.1 broadcast_in_dim.38
  55.4 0.1 broadcast_in_dim_reshape.3.skip_ref
  55.5 0.0 copy-done.18
  55.5 0.1 add.56.refs_2_
  55.7 0.0 copy-done.11
  55.7 0.0 copy-done.12
  55.7 0.0 copy-done.15
  55.7 0.0 copy-done.16
  55.7 0.0 copy-start.1
  55.7 0.9 copy-done.1
  56.7 0.0 copy-start.13
  56.7 1.0 copy-done.13
  57.7 0.0 copy-start.14
  57.7 0.9 copy-done.14
  58.6 2.4 %prompt.1 = (f32[512,512]{1,0:T(8,128)S(1)}, f32[8,512]{1,0:T(8,128)S(1)}, f32[32,512]{1,0:T(8,128)S(1)}) custom-call(bf16[512,512]{1,0:T(8,128)(2,1)S(1)} %copy-done.13, bf16[512,512]{1,0:T(8,128)(2,1)S(1)} %bitcast.43, bf16[2,64,512]{2,1,0:T(8,128)(2,1)S(1)} %bitcast.45, f32[512,8]{1,0:T(8,128)S(1)} %copy-done.14, f32[8,512]{1,0:T(8,128)S(1)} %copy-done.15, ...), custom_call_target="tpu_custom_call" | custom-call | flops 536870912 | bytes 2500000 | tf_op jit(solution)/shard_map/prompt/pallas_call | solution.py:516
  61.0 32.9 %all-to-all-done.1 = bf16[64,8,768]{2,1,0:T(8,128)(2,1)S(1)} async-done(((bf16[64,8,768]{2,1,0:T(8,128)(2,1)}), bf16[64,8,768]{2,1,0:T(8,128)(2,1)S(1)}, u32[]{:S(2)}, u32[]{:S(2)}) %all-to-all-start.1) | async-done | bytes 786464 | tf_op jit(solution)/shard_map/all_to_all | solution.py:512
  93.9 0.0 copy-done.2
  93.9 0.0 copy-done.3
  93.9 0.0 copy-done.4
  93.9 0.0 copy-done.5
  93.9 0.0 copy-done.7
  93.9 0.0 copy-done.9
  93.9 0.0 copy-done.10
  93.9 1.4 %decode.1 = (f32[192,512]{1,0:T(8,128)S(1)}, f32[8,8,128]{2,1,0:T(8,128)S(1)}) custom-call(bf16[512,768]{1,0:T(8,128)(2,1)S(1)} %bitcast.31, f32[32,512]{1,0:T(8,128)S(1)} %get-tuple-element.21.refs_1_, s32[256,1]{1,0:T(8,128)S(1)} %add.56.refs_2_, s32[128,1]{1,0:T(8,128)S(1)} %add.55.tgt_r_ref.refs_3_, bf16[4,2,48,512]{3,2,1,0:T(8,128)(2,1)S(1)} %copy-done.2, ...), custom_call_target="tpu_custom_call" | custom-call | flops 201326592 | bytes 2500000 | tf_op jit(solution)/shard_map/decode/pallas_call | solution.py:532
  95.3 13.7 %all_to_all.15.refs_0_ = f32[8,8,128]{2,1,0:T(8,128)S(1)} all-to-all(f32[8,8,128]{2,1,0:T(8,128)S(1)} %get-tuple-element.23), channel_id=1, replica_groups=mesh['gen'=64,'mp'=8] {'mp'}, dimensions={0} | all-to-all | bytes 65536 | tf_op jit(solution)/shard_map/all_to_all | solution.py:555
  109.0 0.0 copy-done.8
  109.0 1.0 finish.1
  (4 shorter events, 0.0 us)
Async XLA Ops:
  3.5 38.4 %all-to-all-start = ((bf16[64,8,256]{2,1,0:T(8,128)(2,1)}), bf16[64,8,256]{2,1,0:T(8,128)(2,1)S(1)}, u32[]{:S(2)}, u32[]{:S(2)}) async-start(bf16[64,8,256]{2,1,0:T(8,128)(2,1)} %bitcast.48), calls=%async_computation | async-start | bytes 524288 | tf_op jit(solution)/shard_map/all_to_all | solution.py:461
  22.8 32.4 %copy-start.17 = (s32[16]{0:T(128)S(1)}, s32[16]{0:T(128)}, u32[]{:S(2)}) copy-start(s32[16]{0:T(128)} %param.26) | copy-start | bytes 196
  22.9 32.5 %copy-start.6 = (f32[8]{0:T(128)S(1)}, f32[8]{0:T(128)}, u32[]{:S(2)}) copy-start(f32[8]{0:T(128)} %param.34) | copy-start | bytes 100
  22.9 32.6 %copy-start.18 = (s32[32]{0:T(128)S(1)}, s32[32]{0:T(128)}, u32[]{:S(2)}) copy-start(s32[32]{0:T(128)} %param.25) | copy-start | bytes 388
  22.9 32.8 %copy-start.11 = (bf16[1,512,512]{2,1,0:T(8,128)(2,1)S(1)}, bf16[1,512,512]{2,1,0:T(8,128)(2,1)}, u32[]{:S(2)}) copy-start(bf16[1,512,512]{2,1,0:T(8,128)(2,1)} %param.19) | copy-start | bytes 1572868
  22.9 32.8 %copy-start.12 = (bf16[1,2,512,64]{2,3,1,0:T(8,128)(2,1)S(1)}, bf16[1,2,512,64]{2,3,1,0:T(8,128)(2,1)}, u32[]{:S(2)}) copy-start(bf16[1,2,512,64]{2,3,1,0:T(8,128)(2,1)} %param.20) | copy-start | bytes 393220
  27.6 28.0 %copy-start.15 = (f32[8,512]{1,0:T(8,128)S(1)}, f32[8,512]{1,0:T(8,128)}, u32[]{:S(2)}) copy-start(f32[8,512]{1,0:T(8,128)} %get-tuple-element.19.cumt_ref) | copy-start | bytes 49156
  27.7 28.0 %copy-start.16 = (f32[8,512]{1,0:T(8,128)S(1)}, f32[8,512]{1,0:T(8,128)}, u32[]{:S(2)}) copy-start(f32[8,512]{1,0:T(8,128)} %get-tuple-element.20.dtt_ref) | copy-start | bytes 49156
  41.9 0.7 copy-start
  47.4 46.5 %copy-start.2 = (bf16[4,2,48,512]{3,2,1,0:T(8,128)(2,1)S(1)}, bf16[4,2,48,512]{3,2,1,0:T(8,128)(2,1)}, u32[]{:S(2)}) copy-start(bf16[4,2,48,512]{3,2,1,0:T(8,128)(2,1)} %refs_4_.3) | copy-start | bytes 1179652
  47.4 46.5 %copy-start.3 = (bf16[4,2,48,64]{3,2,1,0:T(8,128)(2,1)S(1)}, bf16[4,2,48,64]{3,2,1,0:T(8,128)(2,1)}, u32[]{:S(2)}) copy-start(bf16[4,2,48,64]{3,2,1,0:T(8,128)(2,1)} %refs_5_.1) | copy-start | bytes 147460
  47.4 46.5 %copy-start.4 = (bf16[4,48,8]{1,2,0:T(8,128)(2,1)S(1)}, bf16[4,48,8]{1,2,0:T(8,128)(2,1)}, u32[]{:S(2)}) copy-start(bf16[4,48,8]{1,2,0:T(8,128)(2,1)} %param.29) | copy-start | bytes 9220
  47.4 46.5 %copy-start.5 = (bf16[4,512]{1,0:T(4,128)(2,1)S(1)}, bf16[4,512]{1,0:T(4,128)(2,1)}, u32[]{:S(2)}) copy-start(bf16[4,512]{1,0:T(4,128)(2,1)} %refs_10_.1) | copy-start | bytes 12292
  47.4 46.5 %copy-start.7 = (f32[512]{0:T(512)S(1)}, f32[512]{0:T(512)}, u32[]{:S(2)}) copy-start(f32[512]{0:T(512)} %param.33) | copy-start | bytes 6148
  47.4 46.5 %copy-start.9 = (f32[8]{0:T(128)S(1)}, f32[8]{0:T(128)}, u32[]{:S(2)}) copy-start(f32[8]{0:T(128)} %param.30) | copy-start | bytes 100
  47.4 46.5 %copy-start.10 = (f32[8]{0:T(128)S(1)}, f32[8]{0:T(128)}, u32[]{:S(2)}) copy-start(f32[8]{0:T(128)} %param.31) | copy-start | bytes 100
  47.5 61.6 %copy-start.8 = (f32[512]{0:T(512)S(1)}, f32[512]{0:T(512)}, u32[]{:S(2)}) copy-start(f32[512]{0:T(512)} %param.35) | copy-start | bytes 6148
  47.5 46.4 %all-to-all-start.1 = ((bf16[64,8,768]{2,1,0:T(8,128)(2,1)}), bf16[64,8,768]{2,1,0:T(8,128)(2,1)S(1)}, u32[]{:S(2)}, u32[]{:S(2)}) async-start(bf16[64,8,768]{2,1,0:T(8,128)(2,1)} %bitcast.47), calls=%async_computation.1 | async-start | bytes 1572864 | tf_op jit(solution)/shard_map/all_to_all | solution.py:512
  55.7 1.0 copy-start.1
  56.7 1.0 copy-start.13
  57.7 0.9 copy-start.14

commit v6 on v5

--- a/solution.py
+++ b/solution.py
@@ -9,6 +9,7 @@
 EPS = 1e-05
 SUB = 8
 CHUNKS = 4
+GROUP_ROWS = 4
 WHOLE = 60 * 1024 * 1024
 F32 = jnp.float32
 BF16 = jnp.bfloat16
@@ -114,10 +115,17 @@
 
 
 def state_kernel(*refs):
-    sources, outs, targets = refs[:8], refs[8:14], refs[14:22]
-    sems, xf = refs[22], refs[23]
-    xc_ref, cum_ref, cumt_ref, dtt_ref, st_ref, tail_ref = outs
-    for copy in fetch(sources, targets, sems):
+    sources, live_hbm, outs, targets = refs[:8], refs[8], refs[9:16], refs[16:24]
+    live_ref, sems, xf = refs[24:]
+    xc_ref, cum_ref, cumt_ref, dtt_ref, st_ref, tail_ref, turned_ref = outs
+    chunk = live_ref.shape[0] // CHUNKS
+    chunks = [slice(i * chunk, (i + 1) * chunk) for i in range(CHUNKS)]
+    copies = fetch(
+        sources + tuple(live_hbm.at[part] for part in chunks),
+        targets + tuple(live_ref.at[part] for part in chunks),
+        sems,
+    )
+    for copy in copies[:8]:
         copy.wait()
     len_ref, rawt_ref, decay_ref, bias_ref, cw_ref, cb_ref, bct_ref, x_ref = targets
     span, width = x_ref.shape
@@ -164,6 +172,11 @@
     row, col = iota((SUB, span), 0), iota((SUB, span), 1)
     tail = onehot((col == length - (taps - 1)) & (row == SUB - 1))
     tail_ref[...] = mm(tail, x_ref[...]).astype(BF16)
+    unit = onehot(iota((STATE, STATE), 0) == iota((STATE, STATE), 1))
+    for k in range(live_ref.shape[0]):
+        if k % chunk == 0:
+            copies[8 + k // chunk].wait()
+        turned_ref[k * STATE : (k + 1) * STATE, :] = mm_nt(unit, live_ref[k]).astype(BF16)
 
 
 def prompt_kernel(
@@ -226,12 +239,12 @@
 
 
 def answer_kernel(*refs):
-    sources, live_hbm, out_ref, targets = refs[:4], refs[4], refs[5], refs[6:10]
-    state_ref, sems, cs, ys = refs[10:]
+    sources, turned_hbm, out_ref, targets = refs[:4], refs[4], refs[5], refs[6:10]
+    state_ref, sems, ys = refs[10:]
     chunk = state_ref.shape[0] // CHUNKS
     chunks = [slice(i * chunk, (i + 1) * chunk) for i in range(CHUNKS)]
     copies = fetch(
-        sources + tuple(live_hbm.at[part] for part in chunks),
+        sources + tuple(turned_hbm.at[part] for part in chunks),
         targets + tuple(state_ref.at[part] for part in chunks),
         sems,
     )
@@ -239,8 +252,8 @@
         copy.wait()
     ask_ref, conv_ref, prefix_ref, tail_ref = targets
     slots = ask_ref.shape[0]
-    live_dev = state_ref.shape[0]
     count = ys.shape[0]
+    live_dev = count // SUB
     width = prefix_ref.shape[1]
     half = width // 2
     ask = ask_ref[:, 0 : 2 * STATE]
@@ -250,17 +263,24 @@
     lane0 = onehot(iota((SUB, 2 * STATE), 1) == 0)
     across = mm_nt(lane0, place.astype(BF16))[0:1, :].astype(jnp.int32)
     back = (across - 1) * SUB + jnp.bitwise_and(lane, SUB - 1)
-    got = mm(onehot(iota((count, 1), 0) == back), ask)
-    first = jnp.bitwise_and(iota((count, 1), 0), SUB - 1) < 4
-    cs[...] = jnp.where(first, got, 0.0)
-    for k in range(live_dev):
-        if k % chunk == 0:
-            copies[4 + k // chunk].wait()
-        rows = slice(k * SUB, (k + 1) * SUB)
-        ys[rows, :] = mm_nt(cs[rows, 0:STATE].astype(BF16), state_ref[k])
+    got = mm(onehot(iota((count, 1), 0) == back), ask).astype(BF16)
+    deep = GROUP_ROWS * STATE
+    copy_of = jnp.bitwise_and(iota((1, deep), 1), STATE - 1)
+    wide = mm(got, onehot(iota((2 * STATE, 1), 0) == copy_of))
+    row, col = iota((count, 1), 0), iota((1, deep), 1)
+    wanted = jnp.where(jnp.bitwise_and(row, SUB - 1) < 4, lax.div(row, SUB), -1)
+    wanted = jnp.where(wanted >= 0, jnp.bitwise_and(wanted, GROUP_ROWS - 1), -1)
+    wide = jnp.where(wanted == lax.div(col, STATE), wide, 0.0).astype(BF16)
+    tall = GROUP_ROWS * SUB
+    for group in range(live_dev // GROUP_ROWS):
+        first = group * deep
+        if first % chunk == 0:
+            copies[4 + first // chunk].wait()
+        rows = slice(group * tall, (group + 1) * tall)
+        ys[rows, :] = mm(wide[rows, :], state_ref[first : first + deep, :]).astype(BF16)
     place = place[:, 0:1].astype(jnp.int32)
     there = onehot(iota((1, count), 1) == (place - 1) * SUB + in_slot)
-    live = mm(there, ys[...].astype(BF16))
+    live = mm(there, ys[...])
     kept = conv_ref.shape[0]
     conv_row = (in_slot - 4) * live_dev + place - 1
     conv_row = jnp.where((place > 0) & (in_slot >= 4), conv_row, -1)
@@ -473,7 +493,7 @@
         bct,
         pre_x[0],
     )
-    xconv, cum, cumt, dtt, prefix, tail = pl.pallas_call(
+    xconv, cum, cumt, dtt, prefix, tail, turned = pl.pallas_call(
         state_kernel,
         out_shape=(
             shape((span, width), BF16),
@@ -482,32 +502,32 @@
             shape((heads, span), F32),
             shape((2 * STATE, width), BF16),
             shape((SUB, width), BF16),
+            shape((live_dev * STATE, width), BF16),
         ),
-        in_specs=[hbm()] * len(operands),
-        out_specs=(vmem(),) * 6,
-        scratch_shapes=staged(*operands)
-        + [dma((len(operands),)), pltpu.VMEM((span + SUB, width), F32)],
+        in_specs=[hbm()] * (len(operands) + 1),
+        out_specs=(vmem(),) * 7,
+        scratch_shapes=staged(*operands, live)
+        + [dma((len(operands) + CHUNKS,)), pltpu.VMEM((span + SUB, width), F32)],
         compiler_params=params(WHOLE),
-        cost_estimate=cost(2 * 10 * span * span * 64, 2000000, span * width * 2),
+        cost_estimate=cost(2 * 10 * span * span * 64, 8000000, span * width * 2),
         name="state",
-    )(*operands)
+    )(*operands, live)
 
     operands = (asked, conv_rows, prefix, tail)
     answer = pl.pallas_call(
         answer_kernel,
         out_shape=shape((slots, width + width // 2), BF16),
-        in_specs=[hbm()] * (len(operands) + 1),
+        in_specs=[pl.BlockSpec(memory_space=pl.ANY)] + [hbm()] * len(operands),
         out_specs=vmem(),
-        scratch_shapes=staged(*operands, live)
+        scratch_shapes=staged(*operands, turned)
         + [
             dma((len(operands) + CHUNKS,)),
-            pltpu.VMEM((live_dev * SUB, 2 * STATE), F32),
-            pltpu.VMEM((live_dev * SUB, width), F32),
+            pltpu.VMEM((live_dev * SUB, width), BF16),
         ],
         compiler_params=params(WHOLE),
-        cost_estimate=cost(2 * slots * 512 * 1024, 6000000),
+        cost_estimate=cost(2 * slots * 512 * 1024, 4000000),
         name="answer",
-    )(*operands, live)
+    )(*operands, turned)
     lanes = answer.shape[1]
     got = lax.all_to_all(
         answer.reshape(gens, SUB, lanes), "gen", split_axis=0, concat_axis=0, tiled=True

time: 111 us -> 110 us (level)
  waiting for transfers between devices: 47.1 us -> 44.6 us
  Pallas kernels: 16.5 us -> 18.4 us
    pallas_call x1, Pallas kernels: 4.73 us -> 7.27 us  [per_device(): pl.pallas_call(state_kernel, out_shape=(shape((span, width), BF16), shape...]
    all_to_all x1, waiting for transfers between devices: 14.2 us -> 11.7 us  [per_device(): lax.all_to_all(ask.reshape(gens, SUB, lanes), 'gen', split_axis=0, concat...]
  transfers between devices with their start and end apart: 2 -> 2, of which waited for: 2 -> 2; matrix products, arithmetic and copies ran while one was open for 0% -> 0% of each run, Pallas kernels for 6% -> 9%
where the time goes in v6:
time: 110 us; the launch traced here: 109 us
  waiting for transfers between devices  44.6 us (41%)
  starting transfers between devices  26.9 us (24%)
  Pallas kernels  18.4 us (17%)
  blocking collectives  13.8 us (13%)
  local copies, waits for them, and re-layouts  4.08 us (4%)
  between operations  1.54 us (1%)
    all_to_all x1, waiting for transfers between devices, per_device(): lax.all_to_all(answer.reshape(gens, SUB, lanes), 'gen', split_axis=0, con...  32.9 us
    all_to_all x1, starting transfers between devices, per_device(): lax.all_to_all(ask.reshape(gens, SUB, lanes), 'gen', split_axis=0, concat...  19.3 us
    all_to_all x1, blocking collectives, per_device(): sums = lax.all_to_all(sums, 'mp', split_axis=0, concat_axis=0, tiled=True)  13.8 us
    all_to_all x1, waiting for transfers between devices, per_device(): lax.all_to_all(ask.reshape(gens, SUB, lanes), 'gen', split_axis=0, concat...  11.7 us
    all_to_all x1, starting transfers between devices, per_device(): lax.all_to_all(answer.reshape(gens, SUB, lanes), 'gen', split_axis=0, con...  7.62 us
    pallas_call x1, Pallas kernels, per_device(): pl.pallas_call(state_kernel, out_shape=(shape((span, width), BF16), shape...  7.27 us
    pallas_call x1, Pallas kernels, per_device(): pl.pallas_call(answer_kernel, out_shape=shape((slots, width + width // 2)...  4.15 us
    unnamed x38, local copies, waits for them, and re-layouts  3.72 us
  transfers between devices with their start and end apart: 2, of which 2 were waited for; matrix products, arithmetic and copies ran while one was open for 0% of the time, Pallas kernels for 9%

profile of v6, /device:TPU:1, one launch (start us, length us, event | category | flops | bytes accessed | tf_op | source)
XLA Modules:
  0.0 109.3 jit_solution(6118298109474733722)
XLA Ops:
  1.3 2.3 %ask.1 = bf16[512,256]{1,0:T(8,128)(2,1)} custom-call(bf16[4,2,48,64]{3,2,1,0:T(8,128)(2,1)} %refs_5_.1, s32[1,32]{1,0:T(1,128)} %bitcast.54, s32[1,16]{1,0:T(1,128)} %bitcast.53, s32[1,1]{1,0:T(1,128)} %bitcast.29.refs_3_, bf16[512,512]{1,0:T(8,128)(2,1)} %bitcast.48), custom_call_target="tpu_custom_call" | custom-call | flops 50331648 | bytes 800000 | tf_op jit(solution)/shard_map/ask/pallas_call | solution.py:470
  3.5 19.3 %all-to-all-start = ((bf16[64,8,256]{2,1,0:T(8,128)(2,1)}), bf16[64,8,256]{2,1,0:T(8,128)(2,1)S(1)}, u32[]{:S(2)}, u32[]{:S(2)}) async-start(bf16[64,8,256]{2,1,0:T(8,128)(2,1)} %bitcast.50), calls=%async_computation | async-start | bytes 524288 | tf_op jit(solution)/shard_map/all_to_all | solution.py:481
  22.8 0.0 copy-start.10
  22.9 0.0 copy-start.17
  22.9 0.0 copy-start.18
  22.9 0.0 copy-start.4
  22.9 0.0 copy-start.12
  22.9 7.3 %state.1 = (bf16[512,512]{1,0:T(8,128)(2,1)}, f32[512,8]{1,0:T(8,128)}, f32[8,512]{1,0:T(8,128)}, f32[8,512]{1,0:T(8,128)}, bf16[128,512]{1,0:T(8,128)(2,1)}, /*...) custom-call(s32[1,1]{1,0:T(1,128)} %bitcast.30.refs_0_, bf16[8,512]{1,0:T(8,128)(2,1)} %bitcast.52, f32[1,8]{1,0:T(1,128)} %bitcast.39, ...), custom_call_target="tpu_custom_call" | custom-call | flops 335544320 | bytes 8000000 | tf_op jit(solution)/shard_map/state/pallas_call | solution.py:496
  30.2 0.0 copy-start.15
  30.2 0.0 copy-start.16
  30.2 11.7 %all-to-all-done = bf16[64,8,256]{2,1,0:T(8,128)(2,1)S(1)} async-done(((bf16[64,8,256]{2,1,0:T(8,128)(2,1)}), bf16[64,8,256]{2,1,0:T(8,128)(2,1)S(1)}, u32[]{:S(2)}, u32[]{:S(2)}) %all-to-all-start) | async-done | bytes 262176 | tf_op jit(solution)/shard_map/all_to_all | solution.py:481
  41.9 0.0 copy-start
  41.9 0.7 copy-done
  42.6 0.0 copy-start.2
  42.6 0.0 copy-start.3
  42.6 0.0 copy-start.5
  42.6 0.0 copy-start.6
  42.6 0.0 copy-start.7
  42.6 0.0 copy-start.8
  42.6 0.0 copy-start.9
  42.7 4.2 %answer.1 = bf16[512,768]{1,0:T(8,128)(2,1)} custom-call(bf16[512,256]{1,0:T(8,128)(2,1)} %bitcast.32, bf16[96,512]{1,0:T(8,128)(2,1)} %bitcast.51, bf16[128,512]{1,0:T(8,128)(2,1)} %get-tuple-element.16.refs_2_, bf16[8,512]{1,0:T(8,128)(2,1)} %get-tuple-element.17.refs_3_, bf16[2048,512]{1,0:T(8,128)(2,1)} %get-tuple-element.18.refs_4_), custom_call_target="tpu_custom_call" | custom-call | flops 536870912 | bytes 4000000 | tf_op jit(solution)/shard_map/answer/pallas_call | solution.py:517
  46.8 0.0 copy-start.11
  46.8 7.6 %all-to-all-start.1 = ((bf16[64,8,768]{2,1,0:T(8,128)(2,1)}), bf16[64,8,768]{2,1,0:T(8,128)(2,1)S(1)}, u32[]{:S(2)}, u32[]{:S(2)}) async-start(bf16[64,8,768]{2,1,0:T(8,128)(2,1)} %bitcast.47), calls=%async_computation.1 | async-start | bytes 1572864 | tf_op jit(solution)/shard_map/all_to_all | solution.py:532
  54.5 0.0 copy-done.10
  54.5 0.1 broadcast_in_dim.38
  54.5 0.1 broadcast_in_dim_reshape.3.skip_ref
  54.6 0.0 copy-done.17
  54.6 0.1 add.55.tgt_r_ref.refs_3_
  54.7 0.0 copy-done.18
  54.8 0.1 add.56.refs_2_
  54.9 0.0 copy-done.4
  54.9 0.0 copy-done.12
  54.9 0.0 copy-done.15
  54.9 0.0 copy-done.16
  54.9 0.0 copy-start.1
  54.9 0.9 copy-done.1
  55.9 0.0 copy-start.13
  55.9 1.0 copy-done.13
  56.9 0.0 copy-start.14
  56.9 0.9 copy-done.14
  57.9 2.3 %prompt.1 = (f32[512,512]{1,0:T(8,128)S(1)}, f32[8,512]{1,0:T(8,128)S(1)}, f32[32,512]{1,0:T(8,128)S(1)}) custom-call(bf16[512,512]{1,0:T(8,128)(2,1)S(1)} %copy-done.13, bf16[512,512]{1,0:T(8,128)(2,1)S(1)} %bitcast.45, bf16[2,64,512]{2,1,0:T(8,128)(2,1)S(1)} %bitcast.35, f32[512,8]{1,0:T(8,128)S(1)} %copy-done.14, f32[8,512]{1,0:T(8,128)S(1)} %copy-done.15, ...), custom_call_target="tpu_custom_call" | custom-call | flops 536870912 | bytes 2500000 | tf_op jit(solution)/shard_map/prompt/pallas_call | solution.py:536
  60.2 32.9 %all-to-all-done.1 = bf16[64,8,768]{2,1,0:T(8,128)(2,1)S(1)} async-done(((bf16[64,8,768]{2,1,0:T(8,128)(2,1)}), bf16[64,8,768]{2,1,0:T(8,128)(2,1)S(1)}, u32[]{:S(2)}, u32[]{:S(2)}) %all-to-all-start.1) | async-done | bytes 786464 | tf_op jit(solution)/shard_map/all_to_all | solution.py:532
  93.1 0.0 copy-done.2
  93.1 0.0 copy-done.3
  93.1 0.0 copy-done.5
  93.1 0.0 copy-done.6
  93.1 0.0 copy-done.7
  93.1 0.0 copy-done.8
  93.1 0.0 copy-done.9
  93.1 1.4 %decode.1 = (f32[192,512]{1,0:T(8,128)S(1)}, f32[8,8,128]{2,1,0:T(8,128)S(1)}) custom-call(bf16[512,768]{1,0:T(8,128)(2,1)S(1)} %bitcast.31, f32[32,512]{1,0:T(8,128)S(1)} %get-tuple-element.23.refs_1_, s32[256,1]{1,0:T(8,128)S(1)} %add.56.refs_2_, s32[128,1]{1,0:T(8,128)S(1)} %add.55.tgt_r_ref.refs_3_, bf16[4,2,48,512]{3,2,1,0:T(8,128)(2,1)S(1)} %copy-done.2, ...), custom_call_target="tpu_custom_call" | custom-call | flops 201326592 | bytes 2500000 | tf_op jit(solution)/shard_map/decode/pallas_call | solution.py:552
  94.5 13.8 %all_to_all.15.refs_0_ = f32[8,8,128]{2,1,0:T(8,128)S(1)} all-to-all(f32[8,8,128]{2,1,0:T(8,128)S(1)} %get-tuple-element.25), channel_id=1, replica_groups=mesh['gen'=64,'mp'=8] {'mp'}, dimensions={0} | all-to-all | bytes 65536 | tf_op jit(solution)/shard_map/all_to_all | solution.py:575
  108.3 0.0 copy-done.11
  108.3 1.0 finish.1
  (4 shorter events, 0.0 us)
Async XLA Ops:
  3.5 38.4 %all-to-all-start = ((bf16[64,8,256]{2,1,0:T(8,128)(2,1)}), bf16[64,8,256]{2,1,0:T(8,128)(2,1)S(1)}, u32[]{:S(2)}, u32[]{:S(2)}) async-start(bf16[64,8,256]{2,1,0:T(8,128)(2,1)} %bitcast.50), calls=%async_computation | async-start | bytes 524288 | tf_op jit(solution)/shard_map/all_to_all | solution.py:481
  22.8 31.6 %copy-start.10 = (f32[8]{0:T(128)S(1)}, f32[8]{0:T(128)}, u32[]{:S(2)}) copy-start(f32[8]{0:T(128)} %param.34) | copy-start | bytes 100
  22.9 31.8 %copy-start.17 = (s32[16]{0:T(128)S(1)}, s32[16]{0:T(128)}, u32[]{:S(2)}) copy-start(s32[16]{0:T(128)} %param.26) | copy-start | bytes 196
  22.9 31.8 %copy-start.18 = (s32[32]{0:T(128)S(1)}, s32[32]{0:T(128)}, u32[]{:S(2)}) copy-start(s32[32]{0:T(128)} %param.25) | copy-start | bytes 388
  22.9 32.0 %copy-start.4 = (bf16[1,2,512,64]{2,3,1,0:T(8,128)(2,1)S(1)}, bf16[1,2,512,64]{2,3,1,0:T(8,128)(2,1)}, u32[]{:S(2)}) copy-start(bf16[1,2,512,64]{2,3,1,0:T(8,128)(2,1)} %param.20) | copy-start | bytes 393220
  22.9 32.0 %copy-start.12 = (bf16[1,512,512]{2,1,0:T(8,128)(2,1)S(1)}, bf16[1,512,512]{2,1,0:T(8,128)(2,1)}, u32[]{:S(2)}) copy-start(bf16[1,512,512]{2,1,0:T(8,128)(2,1)} %param.19) | copy-start | bytes 1572868
  30.2 24.7 %copy-start.15 = (f32[8,512]{1,0:T(8,128)S(1)}, f32[8,512]{1,0:T(8,128)}, u32[]{:S(2)}) copy-start(f32[8,512]{1,0:T(8,128)} %get-tuple-element.21.cumt_ref) | copy-start | bytes 49156
  30.2 24.7 %copy-start.16 = (f32[8,512]{1,0:T(8,128)S(1)}, f32[8,512]{1,0:T(8,128)}, u32[]{:S(2)}) copy-start(f32[8,512]{1,0:T(8,128)} %get-tuple-element.22.dtt_ref) | copy-start | bytes 49156
  41.9 0.7 copy-start
  42.6 50.5 %copy-start.2 = (bf16[4,2,48,512]{3,2,1,0:T(8,128)(2,1)S(1)}, bf16[4,2,48,512]{3,2,1,0:T(8,128)(2,1)}, u32[]{:S(2)}) copy-start(bf16[4,2,48,512]{3,2,1,0:T(8,128)(2,1)} %refs_4_.3) | copy-start | bytes 1179652
  42.6 50.5 %copy-start.3 = (bf16[4,2,48,64]{3,2,1,0:T(8,128)(2,1)S(1)}, bf16[4,2,48,64]{3,2,1,0:T(8,128)(2,1)}, u32[]{:S(2)}) copy-start(bf16[4,2,48,64]{3,2,1,0:T(8,128)(2,1)} %refs_5_.1) | copy-start | bytes 147460
  42.6 50.5 %copy-start.5 = (bf16[4,512]{1,0:T(4,128)(2,1)S(1)}, bf16[4,512]{1,0:T(4,128)(2,1)}, u32[]{:S(2)}) copy-start(bf16[4,512]{1,0:T(4,128)(2,1)} %refs_10_.1) | copy-start | bytes 12292
  42.6 50.5 %copy-start.6 = (bf16[4,48,8]{1,2,0:T(8,128)(2,1)S(1)}, bf16[4,48,8]{1,2,0:T(8,128)(2,1)}, u32[]{:S(2)}) copy-start(bf16[4,48,8]{1,2,0:T(8,128)(2,1)} %param.29) | copy-start | bytes 9220
  42.6 50.5 %copy-start.7 = (f32[512]{0:T(512)S(1)}, f32[512]{0:T(512)}, u32[]{:S(2)}) copy-start(f32[512]{0:T(512)} %param.33) | copy-start | bytes 6148
  42.6 50.5 %copy-start.8 = (f32[8]{0:T(128)S(1)}, f32[8]{0:T(128)}, u32[]{:S(2)}) copy-start(f32[8]{0:T(128)} %param.30) | copy-start | bytes 100
  42.6 50.5 %copy-start.9 = (f32[8]{0:T(128)S(1)}, f32[8]{0:T(128)}, u32[]{:S(2)}) copy-start(f32[8]{0:T(128)} %param.31) | copy-start | bytes 100
  46.8 61.5 %copy-start.11 = (f32[512]{0:T(512)S(1)}, f32[512]{0:T(512)}, u32[]{:S(2)}) copy-start(f32[512]{0:T(512)} %param.35) | copy-start | bytes 6148
  46.8 46.3 %all-to-all-start.1 = ((bf16[64,8,768]{2,1,0:T(8,128)(2,1)}), bf16[64,8,768]{2,1,0:T(8,128)(2,1)S(1)}, u32[]{:S(2)}, u32[]{:S(2)}) async-start(bf16[64,8,768]{2,1,0:T(8,128)(2,1)} %bitcast.47), calls=%async_computation.1 | async-start | bytes 1572864 | tf_op jit(solution)/shard_map/all_to_all | solution.py:532
  54.9 1.0 copy-start.1
  55.9 1.0 copy-start.13
  56.9 0.9 copy-start.14

commit v7 on v6

--- a/solution.py
+++ b/solution.py
@@ -73,16 +73,14 @@
 
 
 def ask_kernel(*refs):
-    sources, out_ref, targets, sems = refs[:5], refs[5], refs[6:11], refs[11]
+    sources, out_ref, targets, sems = refs[:3], refs[3], refs[4:7], refs[7]
     for copy in fetch(sources, targets, sems):
         copy.wait()
-    bc_ref, source_ref, reader_ref, len_ref, x_ref = targets
+    bc_ref, source_ref, reader_ref = targets
     steps = bc_ref.shape[0]
     slots = out_ref.shape[0]
     live_dev = source_ref.shape[1]
     readers = reader_ref.shape[1]
-    span, width = x_ref.shape
-    part = width // 4
     zeros_l = jnp.zeros((live_dev, STATE), F32)
     place = (iota((live_dev, STATE), 0) + 1).astype(F32)
     parts = [bc_ref[t, 1, 0:live_dev, :].astype(F32) for t in range(steps)]
@@ -100,24 +98,13 @@
     tgt_r = jnp.concatenate([first_r + r for r in range(SUB)], 1)
     pick_l = onehot(iota((slots, SUB * live_dev), 0) == tgt_l)
     pick_r = onehot(iota((slots, SUB * readers), 0) == tgt_r)
-    out_ref[:, 0 : 2 * STATE] = (mm(pick_l, data_l) + mm(pick_r, data_r)).astype(BF16)
-    row, col = iota((2 * SUB, span), 0), iota((2 * SUB, span), 1)
-    last = onehot(col == len_ref[...] - 2 + row // SUB)
-    both = mm(last, x_ref[...])
-    lane_part = iota((SUB, part), 0) % 4
-    tail = jnp.zeros((SUB, part), F32)
-    for i in range(4):
-        lanes = slice(i * part, (i + 1) * part)
-        piece = jnp.where(iota((SUB, part), 0) < 4, both[0:SUB, lanes], both[SUB:, lanes])
-        tail = jnp.where(lane_part == i, piece, tail)
-    tail = jnp.broadcast_to(tail[None], (slots // SUB, SUB, part))
-    out_ref[:, 2 * STATE :] = tail.reshape(slots, part).astype(BF16)
+    out_ref[...] = (mm(pick_l, data_l) + mm(pick_r, data_r)).astype(BF16)
 
 
 def state_kernel(*refs):
-    sources, live_hbm, outs, targets = refs[:8], refs[8], refs[9:16], refs[16:24]
-    live_ref, sems, xf = refs[24:]
-    xc_ref, cum_ref, cumt_ref, dtt_ref, st_ref, tail_ref, turned_ref = outs
+    sources, live_hbm, outs, targets = refs[:8], refs[8], refs[9:17], refs[17:25]
+    live_ref, sems, xf = refs[25:]
+    xc_ref, cum_ref, cumt_ref, dtt_ref, st_ref, tail_ref, late_ref, turned_ref = outs
     chunk = live_ref.shape[0] // CHUNKS
     chunks = [slice(i * chunk, (i + 1) * chunk) for i in range(CHUNKS)]
     copies = fetch(
@@ -131,7 +118,7 @@
     span, width = x_ref.shape
     heads = rawt_ref.shape[0]
     taps = cw_ref.shape[0]
-    length = len_ref[...]
+    length = len_ref[0]
     xf[0:SUB, :] = jnp.zeros((SUB, width), F32)
     xf[SUB : SUB + span, :] = x_ref[...].astype(F32)
     square = iota((heads, heads), 0) == iota((heads, heads), 1)
@@ -172,6 +159,16 @@
     row, col = iota((SUB, span), 0), iota((SUB, span), 1)
     tail = onehot((col == length - (taps - 1)) & (row == SUB - 1))
     tail_ref[...] = mm(tail, x_ref[...]).astype(BF16)
+    row, col = iota((2 * SUB, span), 0), iota((2 * SUB, span), 1)
+    both = mm(onehot(col == length - 2 + jnp.where(row < SUB, 0, 1)), x_ref[...])
+    part = width // 4
+    row = iota((SUB, part), 0)
+    late = jnp.zeros((SUB, part), F32)
+    for i in range(4):
+        lanes = slice(i * part, (i + 1) * part)
+        piece = jnp.where(row < 4, both[0:SUB, lanes], both[SUB:, lanes])
+        late = jnp.where(jnp.bitwise_and(row, 3) == i, piece, late)
+    late_ref[...] = late.astype(BF16)
     unit = onehot(iota((STATE, STATE), 0) == iota((STATE, STATE), 1))
     for k in range(live_ref.shape[0]):
         if k % chunk == 0:
@@ -187,22 +184,10 @@
     cumt_ref,
     dtt_ref,
     skip_ref,
-    ask_ref,
-    tgt_r_ref,
     g_ref,
     ss_ref,
-    late_ref,
     scores,
 ):
-    readers = late_ref.shape[0] // 2
-    part = ask_ref.shape[1] - 2 * STATE
-    pick_r = onehot(iota((SUB * readers, ask_ref.shape[0]), 1) == tgt_r_ref[...])
-    late = mm(pick_r, ask_ref[:, 2 * STATE :])
-    for r in range(SUB):
-        rows = slice(r // 4 * readers, (r // 4 + 1) * readers)
-        late_ref[rows, r % 4 * part : (r % 4 + 1) * part] = late[
-            r * readers : (r + 1) * readers, :
-        ]
     span, width = xc_ref.shape
     heads = cum_ref.shape[1]
     block = 128
@@ -239,8 +224,8 @@
 
 
 def answer_kernel(*refs):
-    sources, turned_hbm, out_ref, targets = refs[:4], refs[4], refs[5], refs[6:10]
-    state_ref, sems, ys = refs[10:]
+    sources, turned_hbm, out_ref, targets = refs[:5], refs[5], refs[6], refs[7:12]
+    state_ref, sems, ys = refs[12:]
     chunk = state_ref.shape[0] // CHUNKS
     chunks = [slice(i * chunk, (i + 1) * chunk) for i in range(CHUNKS)]
     copies = fetch(
@@ -248,18 +233,19 @@
         targets + tuple(state_ref.at[part] for part in chunks),
         sems,
     )
-    for copy in copies[:4]:
+    for copy in copies[:5]:
         copy.wait()
-    ask_ref, conv_ref, prefix_ref, tail_ref = targets
+    ask_ref, conv_ref, prefix_ref, tail_ref, late_ref = targets
     slots = ask_ref.shape[0]
     count = ys.shape[0]
     live_dev = count // SUB
     width = prefix_ref.shape[1]
     half = width // 2
-    ask = ask_ref[:, 0 : 2 * STATE]
+    ask = ask_ref[...]
     down, lane = iota((slots, 1), 0), iota((1, slots), 1)
     in_slot = jnp.bitwise_and(down, SUB - 1)
-    place = mm(onehot(lane == down - in_slot + 4), ask)
+    place = ask.astype(F32).reshape(slots // SUB, SUB, 2 * STATE)
+    place = jnp.broadcast_to(place[:, 4:5, :], place.shape).reshape(slots, 2 * STATE)
     lane0 = onehot(iota((SUB, 2 * STATE), 1) == 0)
     across = mm_nt(lane0, place.astype(BF16))[0:1, :].astype(jnp.int32)
     back = (across - 1) * SUB + jnp.bitwise_and(lane, SUB - 1)
@@ -275,7 +261,7 @@
     for group in range(live_dev // GROUP_ROWS):
         first = group * deep
         if first % chunk == 0:
-            copies[4 + first // chunk].wait()
+            copies[5 + first // chunk].wait()
         rows = slice(group * tall, (group + 1) * tall)
         ys[rows, :] = mm(wide[rows, :], state_ref[first : first + deep, :]).astype(BF16)
     place = place[:, 0:1].astype(jnp.int32)
@@ -291,13 +277,15 @@
     new = mm(ask, prefix_ref[...])
     new = jnp.where(in_slot < SUB // 2, new[:, 0:half], new[:, half:width])
     out_ref[:, width : width + half] = new.astype(BF16)
+    part = late_ref.shape[1]
+    late = jnp.broadcast_to(late_ref[...].astype(F32)[None], (slots // SUB, SUB, part))
+    out_ref[:, width + half :] = late.reshape(slots, part).astype(BF16)
 
 
 def decode_kernel(
     live_dev,
     readers,
     got_ref,
-    late_ref,
     tgt_l_ref,
     tgt_r_ref,
     xz_ref,
@@ -331,14 +319,17 @@
     def new_row(r, first, last):
         return new[r * readers : (r + 1) * readers, first:last]
 
+    def tail_row(r):
+        return jnp.concatenate([new_row(r + i, half, half + width // 4) for i in range(4)], 1)
+
     first = []
     for t in range(steps):
         wide = jnp.concatenate([new_row(t, 0, half), new_row(t + 4, 0, half)], 1)
         first.append(jnp.concatenate([live_row(t), wide], 0))
     inputs = [
         jnp.concatenate([live_row(4), old], 0),
-        jnp.concatenate([live_row(5), late_ref[0:readers, :]], 0),
-        jnp.concatenate([live_row(6), late_ref[readers:, :]], 0),
+        jnp.concatenate([live_row(5), tail_row(0)], 0),
+        jnp.concatenate([live_row(6), tail_row(4)], 0),
     ]
     inputs += [xz_ref[t, 0].astype(F32) for t in range(steps)]
     expand = expander(heads, width)
@@ -458,7 +449,6 @@
     tgt_l = SUB * (source // live_dev)[None, :] + offset
     tgt_r = SUB * reader[None, :] + offset
 
-    length = prompt_len.reshape(1, 1)
     conv_rows = jnp.transpose(live_conv, (1, 0, 2)).reshape(-1, width)
     bct = jnp.swapaxes(pre_bc[0], 1, 2)
     dma = pltpu.SemaphoreType.DMA
@@ -466,15 +456,15 @@
     def staged(*arrays):
         return [pltpu.VMEM(array.shape, array.dtype) for array in arrays]
 
-    operands = (step_bc, source[None], reader[None], length, pre_x[0])
+    operands = (step_bc, source[None], reader[None])
     ask = pl.pallas_call(
         ask_kernel,
-        out_shape=shape((slots, 2 * STATE + width // 4), BF16),
+        out_shape=shape((slots, 2 * STATE), BF16),
         in_specs=[hbm()] * len(operands),
         out_specs=vmem(),
         scratch_shapes=staged(*operands) + [dma((len(operands),))],
         compiler_params=params(WHOLE),
-        cost_estimate=cost(2 * slots * 384 * 128, 800000),
+        cost_estimate=cost(2 * slots * 384 * 128, 300000),
         name="ask",
     )(*operands)
     lanes = ask.shape[1]
@@ -484,7 +474,7 @@
 
     live = live_state.reshape(live_dev, width, STATE)
     operands = (
-        length,
+        prompt_len,
         pre_raw[0].T,
         decay[None],
         dt_bias[None],
@@ -493,7 +483,7 @@
         bct,
         pre_x[0],
     )
-    xconv, cum, cumt, dtt, prefix, tail, turned = pl.pallas_call(
+    xconv, cum, cumt, dtt, prefix, tail, late, turned = pl.pallas_call(
         state_kernel,
         out_shape=(
             shape((span, width), BF16),
@@ -502,21 +492,23 @@
             shape((heads, span), F32),
             shape((2 * STATE, width), BF16),
             shape((SUB, width), BF16),
+            shape((SUB, width // 4), BF16),
             shape((live_dev * STATE, width), BF16),
         ),
         in_specs=[hbm()] * (len(operands) + 1),
-        out_specs=(vmem(),) * 7,
-        scratch_shapes=staged(*operands, live)
+        out_specs=(vmem(),) * 8,
+        scratch_shapes=[pltpu.SMEM((1,), jnp.int32)]
+        + staged(*operands[1:], live)
         + [dma((len(operands) + CHUNKS,)), pltpu.VMEM((span + SUB, width), F32)],
         compiler_params=params(WHOLE),
         cost_estimate=cost(2 * 10 * span * span * 64, 8000000, span * width * 2),
         name="state",
     )(*operands, live)
 
-    operands = (asked, conv_rows, prefix, tail)
+    operands = (asked, conv_rows, prefix, tail, late)
     answer = pl.pallas_call(
         answer_kernel,
-        out_shape=shape((slots, width + width // 2), BF16),
+        out_shape=shape((slots, width + width // 2 + width // 4), BF16),
         in_specs=[pl.BlockSpec(memory_space=pl.ANY)] + [hbm()] * len(operands),
         out_specs=vmem(),
         scratch_shapes=staged(*operands, turned)
@@ -533,33 +525,31 @@
         answer.reshape(gens, SUB, lanes), "gen", split_axis=0, concat_axis=0, tiled=True
     ).reshape(slots, lanes)
 
-    pre_gate, pre_ss, late = pl.pallas_call(
+    pre_gate, pre_ss = pl.pallas_call(
         prompt_kernel,
         out_shape=(
             shape((span, width), F32),
             shape((SUB, span), F32),
-            shape((2 * readers, width), F32),
         ),
-        in_specs=[vmem()] * 9,
-        out_specs=(vmem(),) * 3,
+        in_specs=[vmem()] * 7,
+        out_specs=(vmem(),) * 2,
         scratch_shapes=[pltpu.VMEM((128, span), F32)],
         compiler_params=params(),
         cost_estimate=cost(2 * heads * span * span * 128, 2500000, heads * span * span),
         name="prompt",
-    )(xconv, pre_z[0], bct, cum, cumt, dtt, jnp.repeat(skip, width // heads)[None], asked, tgt_r.reshape(-1, 1))
+    )(xconv, pre_z[0], bct, cum, cumt, dtt, jnp.repeat(skip, width // heads)[None])
 
     count = steps * rows
     step_gate, sums = pl.pallas_call(
         lambda *refs: decode_kernel(live_dev, readers, *refs),
         out_shape=(shape((count, width), F32), shape((mp, SUB, 128), F32)),
-        in_specs=[vmem()] * 13,
+        in_specs=[vmem()] * 12,
         out_specs=(vmem(), vmem()),
         compiler_params=params(),
         cost_estimate=cost(2 * 384 * 512 * 512, 2500000),
         name="decode",
     )(
         got,
-        late,
         tgt_l.reshape(-1, 1),
         tgt_r.reshape(-1, 1),
         step_xz,

time: 110 us -> 110 us (level)
  starting transfers between devices: 26.9 us -> 28 us
    all_to_all x1, waiting for transfers between devices: 32.9 us -> 39.5 us  [per_device(): lax.all_to_all(answer.reshape(gens, SUB, lanes), 'gen', split_axis=0, con...]
    all_to_all x1, waiting for transfers between devices: 11.7 us -> 5.87 us  [per_device(): lax.all_to_all(ask.reshape(gens, SUB, lanes), 'gen', split_axis=0, concat...]
    all_to_all x1, starting transfers between devices: 7.62 us -> 8.74 us  [per_device(): lax.all_to_all(answer.reshape(gens, SUB, lanes), 'gen', split_axis=0, con...]
    unnamed x38 -> x36, local copies, waits for them, and re-layouts: 3.72 us -> 2.72 us
where the time goes in v7:
time: 110 us
  waiting for transfers between devices  45.3 us (41%)
  starting transfers between devices  28 us (25%)
  Pallas kernels  17.7 us (16%)
  blocking collectives  14.1 us (13%)
  local copies, waits for them, and re-layouts  3.08 us (3%)
  between operations  1.54 us (1%)
    all_to_all x1, waiting for transfers between devices, per_device(): lax.all_to_all(answer.reshape(gens, SUB, lanes), 'gen', split_axis=0, con...  39.5 us
    all_to_all x1, starting transfers between devices, per_device(): lax.all_to_all(ask.reshape(gens, SUB, lanes), 'gen', split_axis=0, concat...  19.3 us
    all_to_all x1, blocking collectives, per_device(): sums = lax.all_to_all(sums, 'mp', split_axis=0, concat_axis=0, tiled=True)  14.1 us
    all_to_all x1, starting transfers between devices, per_device(): lax.all_to_all(answer.reshape(gens, SUB, lanes), 'gen', split_axis=0, con...  8.74 us
    pallas_call x1, Pallas kernels, per_device(): pl.pallas_call(state_kernel, out_shape=(shape((span, width), BF16), shape...  7.36 us
    all_to_all x1, waiting for transfers between devices, per_device(): lax.all_to_all(ask.reshape(gens, SUB, lanes), 'gen', split_axis=0, concat...  5.87 us
    pallas_call x1, Pallas kernels, per_device(): pl.pallas_call(answer_kernel, out_shape=shape((slots, width + width // 2...  3.82 us
    unnamed x36, local copies, waits for them, and re-layouts  2.72 us
  transfers between devices with their start and end apart: 2, of which 2 were waited for; matrix products, arithmetic and copies ran while one was open for 0% of the time, Pallas kernels for 9%

profile of v7, /device:TPU:1, one launch (start us, length us, event | category | flops | bytes accessed | tf_op | source)
XLA Modules:
  0.0 109.8 jit_solution(11526286921229185096)
XLA Ops:
  0.6 1.9 %ask.1 = bf16[512,128]{1,0:T(8,128)(2,1)} custom-call(bf16[4,2,48,64]{3,2,1,0:T(8,128)(2,1)} %refs_4_.3, s32[1,32]{1,0:T(1,128)} %bitcast.48, s32[1,16]{1,0:T(1,128)} %bitcast.49), custom_call_target="tpu_custom_call" | custom-call | flops 50331648 | bytes 300000 | tf_op jit(solution)/shard_map/ask/pallas_call | solution.py:460
  2.5 19.3 %all-to-all-start = ((bf16[64,8,128]{2,1,0:T(8,128)(2,1)}), bf16[64,8,128]{2,1,0:T(8,128)(2,1)S(1)}, u32[]{:S(2)}, u32[]{:S(2)}) async-start(bf16[64,8,128]{2,1,0:T(8,128)(2,1)} %bitcast.45), calls=%async_computation | async-start | bytes 262144 | tf_op jit(solution)/shard_map/all_to_all | solution.py:471
  22.5 0.0 copy-start.16
  22.5 0.0 copy-start.17
  22.5 0.0 copy-start.9
  22.5 0.0 copy-start.2
  22.5 0.0 copy-start.10
  22.6 7.4 %state.1 = (bf16[512,512]{1,0:T(8,128)(2,1)}, f32[512,8]{1,0:T(8,128)}, f32[8,512]{1,0:T(8,128)}, f32[8,512]{1,0:T(8,128)}, bf16[128,512]{1,0:T(8,128)(2,1)}, /*...) custom-call(s32[1]{0:T(128)S(6)} %copy.23.refs_0_, bf16[8,512]{1,0:T(8,128)(2,1)} %bitcast.47, ...), custom_call_target="tpu_custom_call" | custom-call | flops 335544320 | bytes 8000000 | tf_op jit(solution)/shard_map/state/pallas_call | solution.py:486
  29.9 0.0 copy-start.13
  29.9 0.0 copy-start.14
  29.9 5.9 %all-to-all-done = bf16[64,8,128]{2,1,0:T(8,128)(2,1)S(1)} async-done(((bf16[64,8,128]{2,1,0:T(8,128)(2,1)}), bf16[64,8,128]{2,1,0:T(8,128)(2,1)S(1)}, u32[]{:S(2)}, u32[]{:S(2)}) %all-to-all-start) | async-done | bytes 131104 | tf_op jit(solution)/shard_map/all_to_all | solution.py:471
  35.8 0.0 copy-start.15
  35.8 0.7 copy-done.15
  36.5 0.0 copy-start
  36.5 0.0 copy-start.1
  36.5 0.0 copy-start.3
  36.5 0.0 copy-start.4
  36.5 0.0 copy-start.5
  36.5 0.0 copy-start.7
  36.5 0.0 copy-start.8
  36.5 3.8 %answer.1 = bf16[512,896]{1,0:T(8,128)(2,1)} custom-call(bf16[512,128]{1,0:T(8,128)(2,1)} %bitcast.44, bf16[96,512]{1,0:T(8,128)(2,1)} %bitcast.46, bf16[128,512]{1,0:T(8,128)(2,1)} %get-tuple-element.16.refs_2_, bf16[8,512]{1,0:T(8,128)(2,1)} %get-tuple-element.17.refs_3_, bf16[8,128]{1,0:T(8,128)(2,1)} %get-tuple-element.18.refs_4_, ...), custom_call_target="tpu_custom_call" | custom-call | flops 536870912 | bytes 4000000 | tf_op jit(solution)/shard_map/answer/pallas_call | solution.py:509
  40.3 0.0 copy-start.6
  40.4 8.7 %all-to-all-start.1 = ((bf16[64,8,896]{2,1,0:T(8,128)(2,1)}), bf16[64,8,896]{2,1,0:T(8,128)(2,1)S(1)}, u32[]{:S(2)}, u32[]{:S(2)}) async-start(bf16[64,8,896]{2,1,0:T(8,128)(2,1)} %bitcast.42), calls=%async_computation.1 | async-start | bytes 1835008 | tf_op jit(solution)/shard_map/all_to_all | solution.py:524
  49.1 0.0 copy-done.16
  49.1 0.1 add.55.refs_1_
  49.3 0.0 copy-done.17
  49.3 0.1 add.56.refs_2_
  49.4 0.0 copy-done.9
  49.4 0.1 broadcast_in_dim.39
  49.5 0.1 broadcast_in_dim_reshape.3.skip_ref
  49.6 0.0 copy-done.2
  49.6 0.0 copy-done.10
  49.6 0.0 copy-done.13
  49.6 0.0 copy-done.14
  49.6 0.0 copy-start.11
  49.6 1.0 copy-done.11
  50.6 0.0 copy-start.12
  50.6 0.9 copy-done.12
  51.6 2.3 %prompt.1 = (f32[512,512]{1,0:T(8,128)S(1)}, f32[8,512]{1,0:T(8,128)S(1)}) custom-call(bf16[512,512]{1,0:T(8,128)(2,1)S(1)} %copy-done.11, bf16[512,512]{1,0:T(8,128)(2,1)S(1)} %bitcast.40, bf16[2,64,512]{2,1,0:T(8,128)(2,1)S(1)} %bitcast.30, f32[512,8]{1,0:T(8,128)S(1)} %copy-done.12, f32[8,512]{1,0:T(8,128)S(1)} %copy-done.13, f32[8,512]{1,0:T(8,128)S(1)} %copy-done.14, ...), custom_call_target="tpu_custom_call" | custom-call | flops 536870912 | bytes 2500000 | tf_op jit(solution)/shard_map/prompt/pallas_call | solution.py:528
  53.9 39.5 %all-to-all-done.1 = bf16[64,8,896]{2,1,0:T(8,128)(2,1)S(1)} async-done(((bf16[64,8,896]{2,1,0:T(8,128)(2,1)}), bf16[64,8,896]{2,1,0:T(8,128)(2,1)S(1)}, u32[]{:S(2)}, u32[]{:S(2)}) %all-to-all-start.1) | async-done | bytes 917536 | tf_op jit(solution)/shard_map/all_to_all | solution.py:524
  93.4 0.0 copy-done
  93.4 0.0 copy-done.1
  93.4 0.0 copy-done.3
  93.4 0.0 copy-done.4
  93.4 0.0 copy-done.5
  93.4 0.0 copy-done.7
  93.4 0.0 copy-done.8
  93.4 1.3 %decode.1 = (f32[192,512]{1,0:T(8,128)S(1)}, f32[8,8,128]{2,1,0:T(8,128)S(1)}) custom-call(bf16[512,896]{1,0:T(8,128)(2,1)S(1)} %bitcast.28, s32[256,1]{1,0:T(8,128)S(1)} %add.55.refs_1_, s32[128,1]{1,0:T(8,128)S(1)} %add.56.refs_2_, bf16[4,2,48,512]{3,2,1,0:T(8,128)(2,1)S(1)} %copy-done, bf16[4,2,48,64]{3,2,1,0:T(8,128)(2,1)S(1)} %copy-done.1, ...), custom_call_target="tpu_custom_call" | custom-call | flops 201326592 | bytes 2500000 | tf_op jit(solution)/shard_map/decode/pallas_call | solution.py:543
  94.7 14.1 %all_to_all.15.refs_0_ = f32[8,8,128]{2,1,0:T(8,128)S(1)} all-to-all(f32[8,8,128]{2,1,0:T(8,128)S(1)} %get-tuple-element.25), channel_id=1, replica_groups=mesh['gen'=64,'mp'=8] {'mp'}, dimensions={0} | all-to-all | bytes 65536 | tf_op jit(solution)/shard_map/all_to_all | solution.py:565
  108.8 0.0 copy-done.6
  108.8 1.0 finish.1
  (4 shorter events, 0.0 us)
Async XLA Ops:
  2.5 33.3 %all-to-all-start = ((bf16[64,8,128]{2,1,0:T(8,128)(2,1)}), bf16[64,8,128]{2,1,0:T(8,128)(2,1)S(1)}, u32[]{:S(2)}, u32[]{:S(2)}) async-start(bf16[64,8,128]{2,1,0:T(8,128)(2,1)} %bitcast.45), calls=%async_computation | async-start | bytes 262144 | tf_op jit(solution)/shard_map/all_to_all | solution.py:471
  22.5 26.6 %copy-start.16 = (s32[32]{0:T(128)S(1)}, s32[32]{0:T(128)}, u32[]{:S(2)}) copy-start(s32[32]{0:T(128)} %param.25) | copy-start | bytes 388
  22.5 26.8 %copy-start.17 = (s32[16]{0:T(128)S(1)}, s32[16]{0:T(128)}, u32[]{:S(2)}) copy-start(s32[16]{0:T(128)} %param.26) | copy-start | bytes 196
  22.5 26.9 %copy-start.9 = (f32[8]{0:T(128)S(1)}, f32[8]{0:T(128)}, u32[]{:S(2)}) copy-start(f32[8]{0:T(128)} %param.34) | copy-start | bytes 100
  22.5 27.0 %copy-start.2 = (bf16[1,2,512,64]{2,3,1,0:T(8,128)(2,1)S(1)}, bf16[1,2,512,64]{2,3,1,0:T(8,128)(2,1)}, u32[]{:S(2)}) copy-start(bf16[1,2,512,64]{2,3,1,0:T(8,128)(2,1)} %param.20) | copy-start | bytes 393220
  22.5 27.0 %copy-start.10 = (bf16[1,512,512]{2,1,0:T(8,128)(2,1)S(1)}, bf16[1,512,512]{2,1,0:T(8,128)(2,1)}, u32[]{:S(2)}) copy-start(bf16[1,512,512]{2,1,0:T(8,128)(2,1)} %param.19) | copy-start | bytes 1572868
  29.9 19.6 %copy-start.13 = (f32[8,512]{1,0:T(8,128)S(1)}, f32[8,512]{1,0:T(8,128)}, u32[]{:S(2)}) copy-start(f32[8,512]{1,0:T(8,128)} %get-tuple-element.22.cumt_ref) | copy-start | bytes 49156
  29.9 19.6 %copy-start.14 = (f32[8,512]{1,0:T(8,128)S(1)}, f32[8,512]{1,0:T(8,128)}, u32[]{:S(2)}) copy-start(f32[8,512]{1,0:T(8,128)} %get-tuple-element.23.dtt_ref) | copy-start | bytes 49156
  35.8 0.7 copy-start.15
  36.5 56.9 %copy-start = (bf16[4,2,48,512]{3,2,1,0:T(8,128)(2,1)S(1)}, bf16[4,2,48,512]{3,2,1,0:T(8,128)(2,1)}, u32[]{:S(2)}) copy-start(bf16[4,2,48,512]{3,2,1,0:T(8,128)(2,1)} %refs_3_.1) | copy-start | bytes 1179652
  36.5 56.9 %copy-start.1 = (bf16[4,2,48,64]{3,2,1,0:T(8,128)(2,1)S(1)}, bf16[4,2,48,64]{3,2,1,0:T(8,128)(2,1)}, u32[]{:S(2)}) copy-start(bf16[4,2,48,64]{3,2,1,0:T(8,128)(2,1)} %refs_4_.3) | copy-start | bytes 147460
  36.5 56.9 %copy-start.3 = (bf16[4,512]{1,0:T(4,128)(2,1)S(1)}, bf16[4,512]{1,0:T(4,128)(2,1)}, u32[]{:S(2)}) copy-start(bf16[4,512]{1,0:T(4,128)(2,1)} %refs_9_.1) | copy-start | bytes 12292
  36.5 56.9 %copy-start.4 = (bf16[4,48,8]{1,2,0:T(8,128)(2,1)S(1)}, bf16[4,48,8]{1,2,0:T(8,128)(2,1)}, u32[]{:S(2)}) copy-start(bf16[4,48,8]{1,2,0:T(8,128)(2,1)} %param.29) | copy-start | bytes 9220
  36.5 56.9 %copy-start.5 = (f32[512]{0:T(512)S(1)}, f32[512]{0:T(512)}, u32[]{:S(2)}) copy-start(f32[512]{0:T(512)} %param.33) | copy-start | bytes 6148
  36.5 56.9 %copy-start.7 = (f32[8]{0:T(128)S(1)}, f32[8]{0:T(128)}, u32[]{:S(2)}) copy-start(f32[8]{0:T(128)} %param.30) | copy-start | bytes 100
  36.5 56.9 %copy-start.8 = (f32[8]{0:T(128)S(1)}, f32[8]{0:T(128)}, u32[]{:S(2)}) copy-start(f32[8]{0:T(128)} %param.31) | copy-start | bytes 100
  40.3 68.5 %copy-start.6 = (f32[512]{0:T(512)S(1)}, f32[512]{0:T(512)}, u32[]{:S(2)}) copy-start(f32[512]{0:T(512)} %param.35) | copy-start | bytes 6148
  40.4 53.0 %all-to-all-start.1 = ((bf16[64,8,896]{2,1,0:T(8,128)(2,1)}), bf16[64,8,896]{2,1,0:T(8,128)(2,1)S(1)}, u32[]{:S(2)}, u32[]{:S(2)}) async-start(bf16[64,8,896]{2,1,0:T(8,128)(2,1)} %bitcast.42), calls=%async_computation.1 | async-start | bytes 1835008 | tf_op jit(solution)/shard_map/all_to_all | solution.py:524
  49.6 1.0 copy-start.11
  50.6 0.9 copy-start.12

commit v8 on v7

--- a/solution.py
+++ b/solution.py
@@ -224,18 +224,7 @@
 
 
 def answer_kernel(*refs):
-    sources, turned_hbm, out_ref, targets = refs[:5], refs[5], refs[6], refs[7:12]
-    state_ref, sems, ys = refs[12:]
-    chunk = state_ref.shape[0] // CHUNKS
-    chunks = [slice(i * chunk, (i + 1) * chunk) for i in range(CHUNKS)]
-    copies = fetch(
-        sources + tuple(turned_hbm.at[part] for part in chunks),
-        targets + tuple(state_ref.at[part] for part in chunks),
-        sems,
-    )
-    for copy in copies[:5]:
-        copy.wait()
-    ask_ref, conv_ref, prefix_ref, tail_ref, late_ref = targets
+    ask_ref, conv_ref, prefix_ref, tail_ref, late_ref, state_ref, out_ref, ys = refs
     slots = ask_ref.shape[0]
     count = ys.shape[0]
     live_dev = count // SUB
@@ -260,8 +249,6 @@
     tall = GROUP_ROWS * SUB
     for group in range(live_dev // GROUP_ROWS):
         first = group * deep
-        if first % chunk == 0:
-            copies[5 + first // chunk].wait()
         rows = slice(group * tall, (group + 1) * tall)
         ys[rows, :] = mm(wide[rows, :], state_ref[first : first + deep, :]).astype(BF16)
     place = place[:, 0:1].astype(jnp.int32)
@@ -509,14 +496,10 @@
     answer = pl.pallas_call(
         answer_kernel,
         out_shape=shape((slots, width + width // 2 + width // 4), BF16),
-        in_specs=[pl.BlockSpec(memory_space=pl.ANY)] + [hbm()] * len(operands),
+        in_specs=[vmem()] * (len(operands) + 1),
         out_specs=vmem(),
-        scratch_shapes=staged(*operands, turned)
-        + [
-            dma((len(operands) + CHUNKS,)),
-            pltpu.VMEM((live_dev * SUB, width), BF16),
-        ],
-        compiler_params=params(WHOLE),
+        scratch_shapes=[pltpu.VMEM((live_dev * SUB, width), BF16)],
+        compiler_params=params(),
         cost_estimate=cost(2 * slots * 512 * 1024, 4000000),
         name="answer",
     )(*operands, turned)

time: 110 us -> 112 us (1.018)
  local copies, waits for them, and re-layouts: 3.08 us -> 6.26 us
  Pallas kernels: 17.7 us -> 16.3 us
    unnamed x36 -> x44, local copies, waits for them, and re-layouts: 2.72 us -> 5.89 us
    pallas_call x1, Pallas kernels: 3.82 us -> 2.21 us  [per_device(): pl.pallas_call(answer_kernel, out_shape=shape((slots, width + width // 2...]
where the time goes in v8:
time: 112 us
  waiting for transfers between devices  45.2 us (40%)
  starting transfers between devices  28.1 us (25%)
  Pallas kernels  16.3 us (15%)
  blocking collectives  14.1 us (13%)
  local copies, waits for them, and re-layouts  6.26 us (6%)
  between operations  1.53 us (1%)
    all_to_all x1, waiting for transfers between devices, per_device(): lax.all_to_all(answer.reshape(gens, SUB, lanes), 'gen', split_axis=0, con...  39.3 us
    all_to_all x1, starting transfers between devices, per_device(): lax.all_to_all(ask.reshape(gens, SUB, lanes), 'gen', split_axis=0, concat...  19.3 us
    all_to_all x1, blocking collectives, per_device(): sums = lax.all_to_all(sums, 'mp', split_axis=0, concat_axis=0, tiled=True)  14.1 us
    all_to_all x1, starting transfers between devices, per_device(): lax.all_to_all(answer.reshape(gens, SUB, lanes), 'gen', split_axis=0, con...  8.83 us
    pallas_call x1, Pallas kernels, per_device(): pl.pallas_call(state_kernel, out_shape=(shape((span, width), BF16), shape...  7.36 us
    unnamed x44, local copies, waits for them, and re-layouts  5.89 us
    all_to_all x1, waiting for transfers between devices, per_device(): lax.all_to_all(ask.reshape(gens, SUB, lanes), 'gen', split_axis=0, concat...  5.89 us
    pallas_call x1, Pallas kernels, per_device(): pl.pallas_call(prompt_kernel, out_shape=(shape((span, width), F32), shape...  2.48 us
  transfers between devices with their start and end apart: 2, of which 2 were waited for; matrix products, arithmetic and copies ran while one was open for 0% of the time, Pallas kernels for 9%

profile of v8, /device:TPU:1, one launch (start us, length us, event | category | flops | bytes accessed | tf_op | source)
XLA Modules:
  0.0 111.6 jit_solution(11498801959027638473)
XLA Ops:
  0.6 0.0 copy-start.5
  0.6 1.9 %ask.1 = bf16[512,128]{1,0:T(8,128)(2,1)} custom-call(bf16[4,2,48,64]{3,2,1,0:T(8,128)(2,1)} %refs_4_.3, s32[1,32]{1,0:T(1,128)} %bitcast.47, s32[1,16]{1,0:T(1,128)} %bitcast.48), custom_call_target="tpu_custom_call" | custom-call | flops 50331648 | bytes 300000 | tf_op jit(solution)/shard_map/ask/pallas_call | solution.py:447
  2.6 19.3 %all-to-all-start = ((bf16[64,8,128]{2,1,0:T(8,128)(2,1)}), bf16[64,8,128]{2,1,0:T(8,128)(2,1)S(1)}, u32[]{:S(2)}, u32[]{:S(2)}) async-start(bf16[64,8,128]{2,1,0:T(8,128)(2,1)} %bitcast.45), calls=%async_computation | async-start | bytes 262144 | tf_op jit(solution)/shard_map/all_to_all | solution.py:458
  22.5 0.0 copy-start.20
  22.5 0.0 copy-start.21
  22.6 0.0 copy-start.13
  22.6 0.0 copy-start.3
  22.6 0.0 copy-start.15
  22.6 7.4 %state.1 = (bf16[512,512]{1,0:T(8,128)(2,1)}, f32[512,8]{1,0:T(8,128)}, f32[8,512]{1,0:T(8,128)}, f32[8,512]{1,0:T(8,128)}, bf16[128,512]{1,0:T(8,128)(2,1)}, /*...) custom-call(s32[1]{0:T(128)S(6)} %copy.23.refs_0_, bf16[8,512]{1,0:T(8,128)(2,1)} %bitcast.46, ...), custom_call_target="tpu_custom_call" | custom-call | flops 335544320 | bytes 8000000 | tf_op jit(solution)/shard_map/state/pallas_call | solution.py:473
  30.0 5.9 %all-to-all-done = bf16[64,8,128]{2,1,0:T(8,128)(2,1)S(1)} async-done(((bf16[64,8,128]{2,1,0:T(8,128)(2,1)}), bf16[64,8,128]{2,1,0:T(8,128)(2,1)S(1)}, u32[]{:S(2)}, u32[]{:S(2)}) %all-to-all-start) | async-done | bytes 131104 | tf_op jit(solution)/shard_map/all_to_all | solution.py:458
  35.9 0.0 copy-done.5
  35.9 0.0 copy-start
  35.9 1.6 %copy-done = bf16[2048,512]{1,0:T(8,128)(2,1)S(1)} copy-done((bf16[2048,512]{1,0:T(8,128)(2,1)S(1)}, bf16[2048,512]{1,0:T(8,128)(2,1)}, u32[]{:S(2)}) %copy-start) | copy-done | bytes 2097176
  37.5 0.0 copy-start.4
  37.5 0.9 copy-done.4
  38.4 0.0 copy-start.8
  38.4 0.7 copy-done.8
  39.1 0.0 copy-start.14
  39.1 0.6 copy-done.14
  39.7 0.0 copy-start.18
  39.7 0.0 copy-start.19
  39.7 0.0 copy-start.1
  39.7 0.0 copy-start.2
  39.7 0.0 copy-start.6
  39.7 0.0 copy-start.7
  39.7 0.0 copy-start.9
  39.7 0.0 copy-start.11
  39.7 0.0 copy-start.12
  39.8 2.2 %answer.1 = bf16[512,896]{1,0:T(8,128)(2,1)} custom-call(bf16[512,128]{1,0:T(8,128)(2,1)S(1)} %bitcast.29, bf16[96,512]{1,0:T(8,128)(2,1)S(1)} %bitcast.32, bf16[128,512]{1,0:T(8,128)(2,1)S(1)} %copy-done.4, bf16[8,512]{1,0:T(8,128)(2,1)S(1)} %copy-done.8, bf16[8,128]{1,0:T(8,128)(2,1)S(1)} %copy-done.14, bf16[2048,512]{1,0:T(8,128)(2,1)S(1)} %copy-done), custom_call_target="tpu_custom_call" | custom-call | flops 536870912 | bytes 4000000 | tf_op jit(solution)/shard_map/answer/pallas_call | solution.py:496
  42.0 0.0 copy-start.10
  42.0 8.8 %all-to-all-start.1 = ((bf16[64,8,896]{2,1,0:T(8,128)(2,1)}), bf16[64,8,896]{2,1,0:T(8,128)(2,1)S(1)}, u32[]{:S(2)}, u32[]{:S(2)}) async-start(bf16[64,8,896]{2,1,0:T(8,128)(2,1)} %bitcast.15), calls=%async_computation.1 | async-start | bytes 1835008 | tf_op jit(solution)/shard_map/all_to_all | solution.py:507
  50.8 0.0 copy-done.20
  50.9 0.1 add.55.refs_1_
  51.0 0.0 copy-done.21
  51.0 0.1 add.56.refs_2_
  51.1 0.0 copy-done.13
  51.1 0.1 broadcast_in_dim.39
  51.2 0.1 broadcast_in_dim_reshape.3.skip_ref
  51.3 0.0 copy-done.3
  51.3 0.0 copy-done.15
  51.3 0.0 copy-done.18
  51.3 0.0 copy-done.19
  51.3 0.0 copy-start.16
  51.3 1.0 copy-done.16
  52.3 0.0 copy-start.17
  52.3 0.9 copy-done.17
  53.3 2.5 %prompt.1 = (f32[512,512]{1,0:T(8,128)S(1)}, f32[8,512]{1,0:T(8,128)S(1)}) custom-call(bf16[512,512]{1,0:T(8,128)(2,1)S(1)} %copy-done.16, bf16[512,512]{1,0:T(8,128)(2,1)S(1)} %bitcast.42, bf16[2,64,512]{2,1,0:T(8,128)(2,1)S(1)} %bitcast.31, f32[512,8]{1,0:T(8,128)S(1)} %copy-done.17, f32[8,512]{1,0:T(8,128)S(1)} %copy-done.18, f32[8,512]{1,0:T(8,128)S(1)} %copy-done.19, ...), custom_call_target="tpu_custom_call" | custom-call | flops 536870912 | bytes 2500000 | tf_op jit(solution)/shard_map/prompt/pallas_call | solution.py:511
  55.8 39.3 %all-to-all-done.1 = bf16[64,8,896]{2,1,0:T(8,128)(2,1)S(1)} async-done(((bf16[64,8,896]{2,1,0:T(8,128)(2,1)}), bf16[64,8,896]{2,1,0:T(8,128)(2,1)S(1)}, u32[]{:S(2)}, u32[]{:S(2)}) %all-to-all-start.1) | async-done | bytes 917536 | tf_op jit(solution)/shard_map/all_to_all | solution.py:507
  95.1 0.0 copy-done.1
  95.1 0.0 copy-done.2
  95.1 0.0 copy-done.6
  95.1 0.0 copy-done.7
  95.1 0.0 copy-done.9
  95.1 0.0 copy-done.11
  95.1 0.0 copy-done.12
  95.1 1.3 %decode.1 = (f32[192,512]{1,0:T(8,128)S(1)}, f32[8,8,128]{2,1,0:T(8,128)S(1)}) custom-call(bf16[512,896]{1,0:T(8,128)(2,1)S(1)} %bitcast.28, s32[256,1]{1,0:T(8,128)S(1)} %add.55.refs_1_, s32[128,1]{1,0:T(8,128)S(1)} %add.56.refs_2_, bf16[4,2,48,512]{3,2,1,0:T(8,128)(2,1)S(1)} %copy-done.1, bf16[4,2,48,64]{3,2,1,0:T(8,128)(2,1)S(1)} %copy-done.2, ...), custom_call_target="tpu_custom_call" | custom-call | flops 201326592 | bytes 2500000 | tf_op jit(solution)/shard_map/decode/pallas_call | solution.py:526
  96.4 14.1 %all_to_all.15.refs_0_ = f32[8,8,128]{2,1,0:T(8,128)S(1)} all-to-all(f32[8,8,128]{2,1,0:T(8,128)S(1)} %get-tuple-element.25), channel_id=1, replica_groups=mesh['gen'=64,'mp'=8] {'mp'}, dimensions={0} | all-to-all | bytes 65536 | tf_op jit(solution)/shard_map/all_to_all | solution.py:548
  110.5 0.0 copy-done.10
  110.5 1.0 finish.1
  (4 shorter events, 0.0 us)
Async XLA Ops:
  0.6 35.2 %copy-start.5 = (bf16[32,3,512]{2,0,1:T(8,128)(2,1)S(1)}, bf16[32,3,512]{2,0,1:T(8,128)(2,1)}, u32[]{:S(2)}) copy-start(bf16[32,3,512]{2,0,1:T(8,128)(2,1)} %param.24) | copy-start | bytes 294916
  2.6 33.3 %all-to-all-start = ((bf16[64,8,128]{2,1,0:T(8,128)(2,1)}), bf16[64,8,128]{2,1,0:T(8,128)(2,1)S(1)}, u32[]{:S(2)}, u32[]{:S(2)}) async-start(bf16[64,8,128]{2,1,0:T(8,128)(2,1)} %bitcast.45), calls=%async_computation | async-start | bytes 262144 | tf_op jit(solution)/shard_map/all_to_all | solution.py:458
  22.5 28.3 %copy-start.20 = (s32[32]{0:T(128)S(1)}, s32[32]{0:T(128)}, u32[]{:S(2)}) copy-start(s32[32]{0:T(128)} %param.25) | copy-start | bytes 388
  22.5 28.4 %copy-start.21 = (s32[16]{0:T(128)S(1)}, s32[16]{0:T(128)}, u32[]{:S(2)}) copy-start(s32[16]{0:T(128)} %param.26) | copy-start | bytes 196
  22.6 28.6 %copy-start.13 = (f32[8]{0:T(128)S(1)}, f32[8]{0:T(128)}, u32[]{:S(2)}) copy-start(f32[8]{0:T(128)} %param.34) | copy-start | bytes 100
  22.6 28.7 %copy-start.3 = (bf16[1,2,512,64]{2,3,1,0:T(8,128)(2,1)S(1)}, bf16[1,2,512,64]{2,3,1,0:T(8,128)(2,1)}, u32[]{:S(2)}) copy-start(bf16[1,2,512,64]{2,3,1,0:T(8,128)(2,1)} %param.20) | copy-start | bytes 393220
  22.6 28.7 %copy-start.15 = (bf16[1,512,512]{2,1,0:T(8,128)(2,1)S(1)}, bf16[1,512,512]{2,1,0:T(8,128)(2,1)}, u32[]{:S(2)}) copy-start(bf16[1,512,512]{2,1,0:T(8,128)(2,1)} %param.19) | copy-start | bytes 1572868
  35.9 1.6 %copy-start = (bf16[2048,512]{1,0:T(8,128)(2,1)S(1)}, bf16[2048,512]{1,0:T(8,128)(2,1)}, u32[]{:S(2)}) copy-start(bf16[2048,512]{1,0:T(8,128)(2,1)} %get-tuple-element.19.refs_5_) | copy-start | bytes 6291460
  37.5 0.9 copy-start.4
  38.4 0.7 copy-start.8
  39.1 0.6 copy-start.14
  39.7 11.6 %copy-start.18 = (f32[8,512]{1,0:T(8,128)S(1)}, f32[8,512]{1,0:T(8,128)}, u32[]{:S(2)}) copy-start(f32[8,512]{1,0:T(8,128)} %get-tuple-element.22.cumt_ref) | copy-start | bytes 49156
  39.7 11.6 %copy-start.19 = (f32[8,512]{1,0:T(8,128)S(1)}, f32[8,512]{1,0:T(8,128)}, u32[]{:S(2)}) copy-start(f32[8,512]{1,0:T(8,128)} %get-tuple-element.23.dtt_ref) | copy-start | bytes 49156
  39.7 55.4 %copy-start.1 = (bf16[4,2,48,512]{3,2,1,0:T(8,128)(2,1)S(1)}, bf16[4,2,48,512]{3,2,1,0:T(8,128)(2,1)}, u32[]{:S(2)}) copy-start(bf16[4,2,48,512]{3,2,1,0:T(8,128)(2,1)} %refs_3_.1) | copy-start | bytes 1179652
  39.7 55.4 %copy-start.2 = (bf16[4,2,48,64]{3,2,1,0:T(8,128)(2,1)S(1)}, bf16[4,2,48,64]{3,2,1,0:T(8,128)(2,1)}, u32[]{:S(2)}) copy-start(bf16[4,2,48,64]{3,2,1,0:T(8,128)(2,1)} %refs_4_.3) | copy-start | bytes 147460
  39.7 55.4 %copy-start.6 = (bf16[4,512]{1,0:T(4,128)(2,1)S(1)}, bf16[4,512]{1,0:T(4,128)(2,1)}, u32[]{:S(2)}) copy-start(bf16[4,512]{1,0:T(4,128)(2,1)} %refs_9_.1) | copy-start | bytes 12292
  39.7 55.4 %copy-start.7 = (bf16[4,48,8]{1,2,0:T(8,128)(2,1)S(1)}, bf16[4,48,8]{1,2,0:T(8,128)(2,1)}, u32[]{:S(2)}) copy-start(bf16[4,48,8]{1,2,0:T(8,128)(2,1)} %param.29) | copy-start | bytes 9220
  39.7 55.4 %copy-start.9 = (f32[512]{0:T(512)S(1)}, f32[512]{0:T(512)}, u32[]{:S(2)}) copy-start(f32[512]{0:T(512)} %param.33) | copy-start | bytes 6148
  39.7 55.4 %copy-start.11 = (f32[8]{0:T(128)S(1)}, f32[8]{0:T(128)}, u32[]{:S(2)}) copy-start(f32[8]{0:T(128)} %param.30) | copy-start | bytes 100
  39.7 55.4 %copy-start.12 = (f32[8]{0:T(128)S(1)}, f32[8]{0:T(128)}, u32[]{:S(2)}) copy-start(f32[8]{0:T(128)} %param.31) | copy-start | bytes 100
  42.0 68.6 %copy-start.10 = (f32[512]{0:T(512)S(1)}, f32[512]{0:T(512)}, u32[]{:S(2)}) copy-start(f32[512]{0:T(512)} %param.35) | copy-start | bytes 6148
  42.0 53.1 %all-to-all-start.1 = ((bf16[64,8,896]{2,1,0:T(8,128)(2,1)}), bf16[64,8,896]{2,1,0:T(8,128)(2,1)S(1)}, u32[]{:S(2)}, u32[]{:S(2)}) async-start(bf16[64,8,896]{2,1,0:T(8,128)(2,1)} %bitcast.15), calls=%async_computation.1 | async-start | bytes 1835008 | tf_op jit(solution)/shard_map/all_to_all | solution.py:507
  51.3 1.0 copy-start.16
  52.3 0.9 copy-start.17

commit v9 on v8

--- a/solution.py
+++ b/solution.py
@@ -102,9 +102,11 @@
 
 
 def state_kernel(*refs):
-    sources, live_hbm, outs, targets = refs[:8], refs[8], refs[9:17], refs[17:25]
-    live_ref, sems, xf = refs[25:]
-    xc_ref, cum_ref, cumt_ref, dtt_ref, st_ref, tail_ref, late_ref, turned_ref = outs
+    sources, live_hbm, outs, targets = refs[:8], refs[8], refs[9:14], refs[14:22]
+    live_ref, sems, xf = refs[22:]
+    xc_ref, cum_ref, cumt_ref, dtt_ref, pack_ref = outs
+    base = live_ref.shape[0] * STATE
+    st_ref = pack_ref.at[base : base + 2 * STATE]
     chunk = live_ref.shape[0] // CHUNKS
     chunks = [slice(i * chunk, (i + 1) * chunk) for i in range(CHUNKS)]
     copies = fetch(
@@ -158,7 +160,7 @@
     st_ref[STATE : 2 * STATE, :] = total.astype(BF16)
     row, col = iota((SUB, span), 0), iota((SUB, span), 1)
     tail = onehot((col == length - (taps - 1)) & (row == SUB - 1))
-    tail_ref[...] = mm(tail, x_ref[...]).astype(BF16)
+    tail = mm(tail, x_ref[...])
     row, col = iota((2 * SUB, span), 0), iota((2 * SUB, span), 1)
     both = mm(onehot(col == length - 2 + jnp.where(row < SUB, 0, 1)), x_ref[...])
     part = width // 4
@@ -168,12 +170,14 @@
         lanes = slice(i * part, (i + 1) * part)
         piece = jnp.where(row < 4, both[0:SUB, lanes], both[SUB:, lanes])
         late = jnp.where(jnp.bitwise_and(row, 3) == i, piece, late)
-    late_ref[...] = late.astype(BF16)
+    late = jnp.concatenate([late] * 4, 1)
+    base = base + 2 * STATE
+    pack_ref[base : base + 2 * SUB, :] = jnp.concatenate([tail, late], 0).astype(BF16)
     unit = onehot(iota((STATE, STATE), 0) == iota((STATE, STATE), 1))
     for k in range(live_ref.shape[0]):
         if k % chunk == 0:
             copies[8 + k // chunk].wait()
-        turned_ref[k * STATE : (k + 1) * STATE, :] = mm_nt(unit, live_ref[k]).astype(BF16)
+        pack_ref[k * STATE : (k + 1) * STATE, :] = mm_nt(unit, live_ref[k]).astype(BF16)
 
 
 def prompt_kernel(
@@ -224,11 +228,16 @@
 
 
 def answer_kernel(*refs):
-    ask_ref, conv_ref, prefix_ref, tail_ref, late_ref, state_ref, out_ref, ys = refs
+    ask_ref, conv_ref, state_ref, out_ref, ys = refs
+    base = ys.shape[0] // SUB * STATE
+    width = ys.shape[1]
+    prefix = state_ref[base : base + 2 * STATE, :]
+    base = base + 2 * STATE
+    ends = state_ref[base : base + 2 * SUB, :].astype(F32)
+    tail, late = ends[0:SUB, :], ends[SUB:, 0 : width // 4]
     slots = ask_ref.shape[0]
     count = ys.shape[0]
     live_dev = count // SUB
-    width = prefix_ref.shape[1]
     half = width // 2
     ask = ask_ref[...]
     down, lane = iota((slots, 1), 0), iota((1, slots), 1)
@@ -259,13 +268,13 @@
     conv_row = jnp.where((place > 0) & (in_slot >= 4), conv_row, -1)
     there = onehot(iota((1, kept), 1) == conv_row)
     live = (live + mm(there, conv_ref[...])).reshape(slots // SUB, SUB, width)
-    live = live + tail_ref[...].astype(F32)[None]
+    live = live + tail[None]
     out_ref[:, 0:width] = live.reshape(slots, width).astype(BF16)
-    new = mm(ask, prefix_ref[...])
+    new = mm(ask, prefix)
     new = jnp.where(in_slot < SUB // 2, new[:, 0:half], new[:, half:width])
     out_ref[:, width : width + half] = new.astype(BF16)
-    part = late_ref.shape[1]
-    late = jnp.broadcast_to(late_ref[...].astype(F32)[None], (slots // SUB, SUB, part))
+    part = late.shape[1]
+    late = jnp.broadcast_to(late[None], (slots // SUB, SUB, part))
     out_ref[:, width + half :] = late.reshape(slots, part).astype(BF16)
 
 
@@ -470,20 +479,17 @@
         bct,
         pre_x[0],
     )
-    xconv, cum, cumt, dtt, prefix, tail, late, turned = pl.pallas_call(
+    xconv, cum, cumt, dtt, pack = pl.pallas_call(
         state_kernel,
         out_shape=(
             shape((span, width), BF16),
             shape((span, heads), F32),
             shape((heads, span), F32),
             shape((heads, span), F32),
-            shape((2 * STATE, width), BF16),
-            shape((SUB, width), BF16),
-            shape((SUB, width // 4), BF16),
-            shape((live_dev * STATE, width), BF16),
+            shape((live_dev * STATE + 2 * STATE + 2 * SUB, width), BF16),
         ),
         in_specs=[hbm()] * (len(operands) + 1),
-        out_specs=(vmem(),) * 8,
+        out_specs=(vmem(),) * 5,
         scratch_shapes=[pltpu.SMEM((1,), jnp.int32)]
         + staged(*operands[1:], live)
         + [dma((len(operands) + CHUNKS,)), pltpu.VMEM((span + SUB, width), F32)],
@@ -492,7 +498,7 @@
         name="state",
     )(*operands, live)
 
-    operands = (asked, conv_rows, prefix, tail, late)
+    operands = (asked, conv_rows)
     answer = pl.pallas_call(
         answer_kernel,
         out_shape=shape((slots, width + width // 2 + width // 4), BF16),
@@ -502,7 +508,7 @@
         compiler_params=params(),
         cost_estimate=cost(2 * slots * 512 * 1024, 4000000),
         name="answer",
-    )(*operands, turned)
+    )(*operands, pack)
     lanes = answer.shape[1]
     got = lax.all_to_all(
         answer.reshape(gens, SUB, lanes), "gen", split_axis=0, concat_axis=0, tiled=True

time: 112 us -> 110 us (0.982)
  local copies, waits for them, and re-layouts: 6.26 us -> 4.07 us
    unnamed x44 -> x38, local copies, waits for them, and re-layouts: 5.89 us -> 3.71 us
where the time goes in v9:
time: 110 us; the launch traced here: 109 us
  waiting for transfers between devices  45.3 us (41%)
  starting transfers between devices  28.2 us (26%)
  Pallas kernels  16.2 us (15%)
  blocking collectives  14.1 us (13%)
  local copies, waits for them, and re-layouts  4.07 us (4%)
  between operations  1.53 us (1%)
    all_to_all x1, waiting for transfers between devices, per_device(): lax.all_to_all(answer.reshape(gens, SUB, lanes), 'gen', split_axis=0, con...  39.5 us
    all_to_all x1, starting transfers between devices, per_device(): lax.all_to_all(ask.reshape(gens, SUB, lanes), 'gen', split_axis=0, concat...  19.3 us
    all_to_all x1, blocking collectives, per_device(): sums = lax.all_to_all(sums, 'mp', split_axis=0, concat_axis=0, tiled=True)  14.1 us
    all_to_all x1, starting transfers between devices, per_device(): lax.all_to_all(answer.reshape(gens, SUB, lanes), 'gen', split_axis=0, con...  8.88 us
    pallas_call x1, Pallas kernels, per_device(): pl.pallas_call(state_kernel, out_shape=(shape((span, width), BF16), shape...  7.41 us
    all_to_all x1, waiting for transfers between devices, per_device(): lax.all_to_all(ask.reshape(gens, SUB, lanes), 'gen', split_axis=0, concat...  5.84 us
    unnamed x38, local copies, waits for them, and re-layouts  3.71 us
    pallas_call x1, Pallas kernels, per_device(): pl.pallas_call(prompt_kernel, out_shape=(shape((span, width), F32), shape...  2.3 us
  transfers between devices with their start and end apart: 2, of which 2 were waited for; matrix products, arithmetic and copies ran while one was open for 0% of the time, Pallas kernels for 9%

profile of v9, /device:TPU:1, one launch (start us, length us, event | category | flops | bytes accessed | tf_op | source)
XLA Modules:
  0.0 109.4 jit_solution(10038807177739903200)
XLA Ops:
  0.6 0.0 copy-start.4
  0.6 1.9 %ask.1 = bf16[512,128]{1,0:T(8,128)(2,1)} custom-call(bf16[4,2,48,64]{3,2,1,0:T(8,128)(2,1)} %refs_4_.3, s32[1,32]{1,0:T(1,128)} %bitcast.47, s32[1,16]{1,0:T(1,128)} %bitcast.48), custom_call_target="tpu_custom_call" | custom-call | flops 50331648 | bytes 300000 | tf_op jit(solution)/shard_map/ask/pallas_call | solution.py:456
  2.6 19.3 %all-to-all-start = ((bf16[64,8,128]{2,1,0:T(8,128)(2,1)}), bf16[64,8,128]{2,1,0:T(8,128)(2,1)S(1)}, u32[]{:S(2)}, u32[]{:S(2)}) async-start(bf16[64,8,128]{2,1,0:T(8,128)(2,1)} %bitcast.45), calls=%async_computation | async-start | bytes 262144 | tf_op jit(solution)/shard_map/all_to_all | solution.py:467
  22.5 0.0 copy-start.17
  22.5 0.0 copy-start.18
  22.6 0.0 copy-start.11
  22.6 0.0 copy-start.3
  22.6 0.0 copy-start.12
  22.6 7.4 %state.1 = (bf16[512,512]{1,0:T(8,128)(2,1)}, f32[512,8]{1,0:T(8,128)}, f32[8,512]{1,0:T(8,128)}, f32[8,512]{1,0:T(8,128)}, bf16[2192,512]{1,0:T(8,128)(2,1)}) custom-call(s32[1]{0:T(128)S(6)} %copy.23.refs_0_, bf16[8,512]{1,0:T(8,128)(2,1)} %bitcast.46, f32[1,8]{1,0:T(1,128)} %bitcast.37, f32[1,8]{1,0:T(1,128)} %bitcast.39, bf16[4,512]{1,0:T(4,128)(2,1)} %refs_9_.1, ...), custom_call_target="tpu_custom_call" | custom-call | flops 335544320 | bytes 8000000 | tf_op jit(solution)/shard_map/state/pallas_call | solution.py:482
  30.0 5.8 %all-to-all-done = bf16[64,8,128]{2,1,0:T(8,128)(2,1)S(1)} async-done(((bf16[64,8,128]{2,1,0:T(8,128)(2,1)}), bf16[64,8,128]{2,1,0:T(8,128)(2,1)S(1)}, u32[]{:S(2)}, u32[]{:S(2)}) %all-to-all-start) | async-done | bytes 131104 | tf_op jit(solution)/shard_map/all_to_all | solution.py:467
  35.9 0.0 copy-done.4
  35.9 0.0 copy-start
  35.9 1.6 %copy-done = bf16[2192,512]{1,0:T(8,128)(2,1)S(1)} copy-done((bf16[2192,512]{1,0:T(8,128)(2,1)S(1)}, bf16[2192,512]{1,0:T(8,128)(2,1)}, u32[]{:S(2)}) %copy-start) | copy-done | bytes 2244632
  37.5 0.0 copy-start.15
  37.5 0.0 copy-start.16
  37.5 0.0 copy-start.1
  37.5 0.0 copy-start.2
  37.5 0.0 copy-start.5
  37.5 0.0 copy-start.6
  37.5 0.0 copy-start.7
  37.5 0.0 copy-start.9
  37.6 0.0 copy-start.10
  37.6 2.2 %answer.1 = bf16[512,896]{1,0:T(8,128)(2,1)} custom-call(bf16[512,128]{1,0:T(8,128)(2,1)S(1)} %bitcast.29, bf16[96,512]{1,0:T(8,128)(2,1)S(1)} %bitcast.32, bf16[2192,512]{1,0:T(8,128)(2,1)S(1)} %copy-done), custom_call_target="tpu_custom_call" | custom-call | flops 536870912 | bytes 4000000 | tf_op jit(solution)/shard_map/answer/pallas_call | solution.py:502
  39.8 0.0 copy-start.8
  39.8 8.9 %all-to-all-start.1 = ((bf16[64,8,896]{2,1,0:T(8,128)(2,1)}), bf16[64,8,896]{2,1,0:T(8,128)(2,1)S(1)}, u32[]{:S(2)}, u32[]{:S(2)}) async-start(bf16[64,8,896]{2,1,0:T(8,128)(2,1)} %bitcast.15), calls=%async_computation.1 | async-start | bytes 1835008 | tf_op jit(solution)/shard_map/all_to_all | solution.py:513
  48.6 0.0 copy-done.17
  48.7 0.1 add.55.refs_1_
  48.8 0.0 copy-done.18
  48.9 0.1 add.56.refs_2_
  48.9 0.0 copy-done.11
  49.0 0.1 broadcast_in_dim.39
  49.0 0.1 broadcast_in_dim_reshape.3.skip_ref
  49.1 0.0 copy-done.3
  49.1 0.0 copy-done.12
  49.1 0.0 copy-done.15
  49.1 0.0 copy-done.16
  49.1 0.0 copy-start.13
  49.1 1.0 copy-done.13
  50.2 0.0 copy-start.14
  50.2 0.9 copy-done.14
  51.1 2.3 %prompt.1 = (f32[512,512]{1,0:T(8,128)S(1)}, f32[8,512]{1,0:T(8,128)S(1)}) custom-call(bf16[512,512]{1,0:T(8,128)(2,1)S(1)} %copy-done.13, bf16[512,512]{1,0:T(8,128)(2,1)S(1)} %bitcast.42, bf16[2,64,512]{2,1,0:T(8,128)(2,1)S(1)} %bitcast.31, f32[512,8]{1,0:T(8,128)S(1)} %copy-done.14, f32[8,512]{1,0:T(8,128)S(1)} %copy-done.15, f32[8,512]{1,0:T(8,128)S(1)} %copy-done.16, ...), custom_call_target="tpu_custom_call" | custom-call | flops 536870912 | bytes 2500000 | tf_op jit(solution)/shard_map/prompt/pallas_call | solution.py:517
  53.4 39.5 %all-to-all-done.1 = bf16[64,8,896]{2,1,0:T(8,128)(2,1)S(1)} async-done(((bf16[64,8,896]{2,1,0:T(8,128)(2,1)}), bf16[64,8,896]{2,1,0:T(8,128)(2,1)S(1)}, u32[]{:S(2)}, u32[]{:S(2)}) %all-to-all-start.1) | async-done | bytes 917536 | tf_op jit(solution)/shard_map/all_to_all | solution.py:513
  92.9 0.0 copy-done.1
  92.9 0.0 copy-done.2
  92.9 0.0 copy-done.5
  92.9 0.0 copy-done.6
  92.9 0.0 copy-done.7
  92.9 0.0 copy-done.9
  92.9 0.0 copy-done.10
  92.9 1.3 %decode.1 = (f32[192,512]{1,0:T(8,128)S(1)}, f32[8,8,128]{2,1,0:T(8,128)S(1)}) custom-call(bf16[512,896]{1,0:T(8,128)(2,1)S(1)} %bitcast.28, s32[256,1]{1,0:T(8,128)S(1)} %add.55.refs_1_, s32[128,1]{1,0:T(8,128)S(1)} %add.56.refs_2_, bf16[4,2,48,512]{3,2,1,0:T(8,128)(2,1)S(1)} %copy-done.1, bf16[4,2,48,64]{3,2,1,0:T(8,128)(2,1)S(1)} %copy-done.2, ...), custom_call_target="tpu_custom_call" | custom-call | flops 201326592 | bytes 2500000 | tf_op jit(solution)/shard_map/decode/pallas_call | solution.py:532
  94.2 14.1 %all_to_all.15.refs_0_ = f32[8,8,128]{2,1,0:T(8,128)S(1)} all-to-all(f32[8,8,128]{2,1,0:T(8,128)S(1)} %get-tuple-element.19), channel_id=1, replica_groups=mesh['gen'=64,'mp'=8] {'mp'}, dimensions={0} | all-to-all | bytes 65536 | tf_op jit(solution)/shard_map/all_to_all | solution.py:554
  108.4 0.0 copy-done.8
  108.4 1.0 finish.1
  (4 shorter events, 0.0 us)
Async XLA Ops:
  0.6 35.2 %copy-start.4 = (bf16[32,3,512]{2,0,1:T(8,128)(2,1)S(1)}, bf16[32,3,512]{2,0,1:T(8,128)(2,1)}, u32[]{:S(2)}) copy-start(bf16[32,3,512]{2,0,1:T(8,128)(2,1)} %param.24) | copy-start | bytes 294916
  2.6 33.3 %all-to-all-start = ((bf16[64,8,128]{2,1,0:T(8,128)(2,1)}), bf16[64,8,128]{2,1,0:T(8,128)(2,1)S(1)}, u32[]{:S(2)}, u32[]{:S(2)}) async-start(bf16[64,8,128]{2,1,0:T(8,128)(2,1)} %bitcast.45), calls=%async_computation | async-start | bytes 262144 | tf_op jit(solution)/shard_map/all_to_all | solution.py:467
  22.5 26.1 %copy-start.17 = (s32[32]{0:T(128)S(1)}, s32[32]{0:T(128)}, u32[]{:S(2)}) copy-start(s32[32]{0:T(128)} %param.25) | copy-start | bytes 388
  22.5 26.3 %copy-start.18 = (s32[16]{0:T(128)S(1)}, s32[16]{0:T(128)}, u32[]{:S(2)}) copy-start(s32[16]{0:T(128)} %param.26) | copy-start | bytes 196
  22.6 26.4 %copy-start.11 = (f32[8]{0:T(128)S(1)}, f32[8]{0:T(128)}, u32[]{:S(2)}) copy-start(f32[8]{0:T(128)} %param.34) | copy-start | bytes 100
  22.6 26.5 %copy-start.3 = (bf16[1,2,512,64]{2,3,1,0:T(8,128)(2,1)S(1)}, bf16[1,2,512,64]{2,3,1,0:T(8,128)(2,1)}, u32[]{:S(2)}) copy-start(bf16[1,2,512,64]{2,3,1,0:T(8,128)(2,1)} %param.20) | copy-start | bytes 393220
  22.6 26.5 %copy-start.12 = (bf16[1,512,512]{2,1,0:T(8,128)(2,1)S(1)}, bf16[1,512,512]{2,1,0:T(8,128)(2,1)}, u32[]{:S(2)}) copy-start(bf16[1,512,512]{2,1,0:T(8,128)(2,1)} %param.19) | copy-start | bytes 1572868
  35.9 1.6 %copy-start = (bf16[2192,512]{1,0:T(8,128)(2,1)S(1)}, bf16[2192,512]{1,0:T(8,128)(2,1)}, u32[]{:S(2)}) copy-start(bf16[2192,512]{1,0:T(8,128)(2,1)} %get-tuple-element.13.refs_2_) | copy-start | bytes 6733828
  37.5 11.6 %copy-start.15 = (f32[8,512]{1,0:T(8,128)S(1)}, f32[8,512]{1,0:T(8,128)}, u32[]{:S(2)}) copy-start(f32[8,512]{1,0:T(8,128)} %get-tuple-element.16.cumt_ref) | copy-start | bytes 49156
  37.5 11.6 %copy-start.16 = (f32[8,512]{1,0:T(8,128)S(1)}, f32[8,512]{1,0:T(8,128)}, u32[]{:S(2)}) copy-start(f32[8,512]{1,0:T(8,128)} %get-tuple-element.17.dtt_ref) | copy-start | bytes 49156
  37.5 55.4 %copy-start.1 = (bf16[4,2,48,512]{3,2,1,0:T(8,128)(2,1)S(1)}, bf16[4,2,48,512]{3,2,1,0:T(8,128)(2,1)}, u32[]{:S(2)}) copy-start(bf16[4,2,48,512]{3,2,1,0:T(8,128)(2,1)} %refs_3_.1) | copy-start | bytes 1179652
  37.5 55.4 %copy-start.2 = (bf16[4,2,48,64]{3,2,1,0:T(8,128)(2,1)S(1)}, bf16[4,2,48,64]{3,2,1,0:T(8,128)(2,1)}, u32[]{:S(2)}) copy-start(bf16[4,2,48,64]{3,2,1,0:T(8,128)(2,1)} %refs_4_.3) | copy-start | bytes 147460
  37.5 55.4 %copy-start.5 = (bf16[4,512]{1,0:T(4,128)(2,1)S(1)}, bf16[4,512]{1,0:T(4,128)(2,1)}, u32[]{:S(2)}) copy-start(bf16[4,512]{1,0:T(4,128)(2,1)} %refs_9_.1) | copy-start | bytes 12292
  37.5 55.4 %copy-start.6 = (bf16[4,48,8]{1,2,0:T(8,128)(2,1)S(1)}, bf16[4,48,8]{1,2,0:T(8,128)(2,1)}, u32[]{:S(2)}) copy-start(bf16[4,48,8]{1,2,0:T(8,128)(2,1)} %param.29) | copy-start | bytes 9220
  37.5 55.4 %copy-start.7 = (f32[512]{0:T(512)S(1)}, f32[512]{0:T(512)}, u32[]{:S(2)}) copy-start(f32[512]{0:T(512)} %param.33) | copy-start | bytes 6148
  37.5 55.4 %copy-start.9 = (f32[8]{0:T(128)S(1)}, f32[8]{0:T(128)}, u32[]{:S(2)}) copy-start(f32[8]{0:T(128)} %param.30) | copy-start | bytes 100
  37.6 55.4 %copy-start.10 = (f32[8]{0:T(128)S(1)}, f32[8]{0:T(128)}, u32[]{:S(2)}) copy-start(f32[8]{0:T(128)} %param.31) | copy-start | bytes 100
  39.8 68.6 %copy-start.8 = (f32[512]{0:T(512)S(1)}, f32[512]{0:T(512)}, u32[]{:S(2)}) copy-start(f32[512]{0:T(512)} %param.35) | copy-start | bytes 6148
  39.8 53.1 %all-to-all-start.1 = ((bf16[64,8,896]{2,1,0:T(8,128)(2,1)}), bf16[64,8,896]{2,1,0:T(8,128)(2,1)S(1)}, u32[]{:S(2)}, u32[]{:S(2)}) async-start(bf16[64,8,896]{2,1,0:T(8,128)(2,1)} %bitcast.15), calls=%async_computation.1 | async-start | bytes 1835008 | tf_op jit(solution)/shard_map/all_to_all | solution.py:513
  49.1 1.0 copy-start.13
  50.2 0.9 copy-start.14
